TPU v7x, 128 devices: a whole 4x4x4 slice. The times are simulated.
128 devices in a mesh: dp: 4 (over y_hi, core), expert: 32 (over x, z, y_lo).
Axes of the slice: x: 4, y: 4 (y_hi: 2, y_lo: 2; y = y_hi * 2 + y_lo), z: 4, core: 2. Of those that a mesh axis runs over, the one named last changes fastest.
Arguments:
- tokens: bfloat16 [16384, 2048], P(('dp', 'expert')), may hold values from -6 to 6
- grad_out: bfloat16 [16384, 2048], P(('dp', 'expert')), may hold values from -3 to 3
- gates: float32 [16384, 2], P(('dp', 'expert')), may hold values from 0.2 to 1
- expert_ids: int32 [16384, 2], P(('dp', 'expert')), may hold values from 0 to 31, all different within a row; in each aligned block of 128 rows (0 to 127, 128 to 255, ...) at most 16 rows name the same one
- w_gate: bfloat16 [32, 2048, 4096], P('expert', None, 'dp'), may hold values from -0.125 to 0.125
- w_up: bfloat16 [32, 2048, 4096], P('expert', None, 'dp'), may hold values from -0.125 to 0.125
- w_down: bfloat16 [32, 4096, 2048], P('expert', 'dp'), may hold values from -0.09375 to 0.09375
Outputs:
- grad_tokens: bfloat16 [16384, 2048], P(('dp', 'expert'))
- grad_gate: bfloat16 [32, 2048, 4096], P('expert', None, 'dp')
- grad_up: bfloat16 [32, 2048, 4096], P('expert', None, 'dp')
- grad_down: bfloat16 [32, 4096, 2048], P('expert', 'dp')
Inputs may be any that keep to these rules, and one draw needn't show every extreme that they name: `expert_ids`: each row names two different experts; among the rows of one device no expert is named by more than 16 rows.
All inputs are finite; a program needn't handle non-finite values.
Results may differ from a plain program's by a relative error of at most 0.015.
Values may be sent and summed in bfloat16 or wider, within the bound.
No kernel may reach another device: no remote copies, remote signals or barrier semaphores. Data moves between devices by JAX's collectives and lax.ppermute only.
A program may use at most 192 MiB of HBM per device.

v0:
```python
import jax
import jax.numpy as jnp
from jax import lax
from jax.sharding import PartitionSpec as P

BLOCK = 512


def block_terms(in_block, dy_block, gate_weight, up_weight, down_weight):
    contract_last = (((1,), (1,)), ((), ()))
    contract_rows = (((0,), (0,)), ((), ()))
    gate_pre = jnp.dot(in_block, gate_weight, preferred_element_type=jnp.float32)
    up_pre = jnp.dot(in_block, up_weight, preferred_element_type=jnp.float32)
    gate_sigmoid = jax.nn.sigmoid(gate_pre)
    silu_gate = gate_pre * gate_sigmoid
    hidden = (silu_gate * up_pre).astype(jnp.bfloat16)
    d_hidden = lax.dot_general(
        dy_block, down_weight, contract_last, preferred_element_type=jnp.float32
    )
    d_gate = (d_hidden * up_pre * gate_sigmoid * (1.0 + gate_pre * (1.0 - gate_sigmoid))).astype(
        jnp.bfloat16
    )
    d_up = (d_hidden * silu_gate).astype(jnp.bfloat16)
    d_input = lax.dot_general(
        d_gate, gate_weight, contract_last, preferred_element_type=jnp.float32
    )
    d_input = d_input + lax.dot_general(
        d_up, up_weight, contract_last, preferred_element_type=jnp.float32
    )
    grad_gate = lax.dot_general(in_block, d_gate, contract_rows, preferred_element_type=jnp.float32)
    grad_up = lax.dot_general(in_block, d_up, contract_rows, preferred_element_type=jnp.float32)
    grad_down = lax.dot_general(hidden, dy_block, contract_rows, preferred_element_type=jnp.float32)
    return (d_input.astype(jnp.bfloat16), (grad_gate, grad_up, grad_down))


def expert_pass(sent_rows, sent_grads, live_slots, slot_limit, weights, totals):
    slot_count, model_width = sent_rows.shape
    sources = slot_count // slot_limit
    counts = jnp.sum(live_slots.reshape(sources, slot_limit).astype(jnp.float32), axis=1).astype(
        jnp.int32
    )
    starts = jnp.cumsum(counts) - counts
    filled = jnp.sum(counts)
    position = jnp.arange(slot_count, dtype=jnp.int32)
    source_of = jnp.sum((starts[None, :] <= position[:, None]).astype(jnp.int32), axis=1) - 1
    source_of = jnp.clip(source_of, 0, sources - 1)
    within = position < filled
    source_row = jnp.where(within, source_of * slot_limit + position - starts[source_of], 0)
    packed_x = jnp.where(within[:, None], sent_rows[source_row], jnp.zeros((), jnp.bfloat16))
    packed_dy = jnp.where(within[:, None], sent_grads[source_row], jnp.zeros((), jnp.bfloat16))
    blocks = (filled + BLOCK - 1) // BLOCK

    def advance(block_index, carried):
        packed_dx, sums_now = carried
        first_row = block_index * BLOCK
        in_block = lax.dynamic_slice_in_dim(packed_x, first_row, BLOCK, 0)
        dy_block = lax.dynamic_slice_in_dim(packed_dy, first_row, BLOCK, 0)
        d_input, grads = block_terms(in_block, dy_block, weights[0], weights[1], weights[2])
        packed_dx = lax.dynamic_update_slice_in_dim(packed_dx, d_input, first_row, 0)
        sums_now = (sums_now[0] + grads[0], sums_now[1] + grads[1], sums_now[2] + grads[2])
        return (packed_dx, sums_now)

    start_dx = jnp.zeros((slot_count, model_width), jnp.bfloat16)
    packed_dx, totals = lax.fori_loop(0, blocks, advance, (start_dx, totals))
    local_rank = position % slot_limit
    slot_source = position // slot_limit
    valid_slot = local_rank < counts[slot_source]
    back_row = jnp.where(valid_slot, starts[slot_source] + local_rank, 0)
    slot_dx = jnp.where(valid_slot[:, None], packed_dx[back_row], jnp.zeros((), jnp.bfloat16))
    return (slot_dx, totals)


def shards(tokens, grad_out, gates, expert_ids, w_gate, w_up, w_down):
    tok_rows, model_width = tokens.shape
    experts = lax.axis_size("expert")
    groups = lax.axis_size("dp")
    slot_limit = 4 * tok_rows // experts
    routes = expert_ids.reshape(-1)
    route_count = routes.shape[0]
    onehot = (routes[:, None] == jnp.arange(experts, dtype=jnp.int32)[None, :]).astype(jnp.int32)
    slot_rank = jnp.sum((jnp.cumsum(onehot, axis=0) - onehot) * onehot, axis=1)
    slot_of = routes * slot_limit + slot_rank
    slot_ids = jnp.arange(experts * slot_limit, dtype=jnp.int32)
    matches = slot_of[None, :] == slot_ids[:, None]
    occupied = jnp.any(matches, axis=1)
    route_of = jnp.sum(
        jnp.where(matches, jnp.arange(route_count, dtype=jnp.int32)[None, :], 0), axis=1
    )
    token_of = route_of // 2
    send_x = jnp.where(occupied[:, None], tokens[token_of], jnp.zeros((), jnp.bfloat16))
    scaled = gates.reshape(-1)[route_of][:, None] * grad_out[token_of].astype(jnp.float32)
    send_dy = jnp.where(occupied[:, None], scaled, 0.0).astype(jnp.bfloat16)
    send_live = occupied.astype(jnp.bfloat16)
    weights = (w_gate[0], w_up[0], w_down[0])
    hid_quarter = w_gate.shape[2]
    zero_sums = (
        jnp.zeros((model_width, hid_quarter), jnp.float32),
        jnp.zeros((model_width, hid_quarter), jnp.float32),
        jnp.zeros((hid_quarter, model_width), jnp.float32),
    )
    many_x = jnp.broadcast_to(send_x[None], (groups,) + send_x.shape).reshape(-1, model_width)
    many_dy = jnp.broadcast_to(send_dy[None], (groups,) + send_dy.shape).reshape(-1, model_width)
    many_live = jnp.broadcast_to(send_live[None], (groups,) + send_live.shape).reshape(-1)
    got_x, got_dy, got_live = (
        lax.all_to_all(many_x, ("dp", "expert"), split_axis=0, concat_axis=0, tiled=True),
        lax.all_to_all(many_dy, ("dp", "expert"), split_axis=0, concat_axis=0, tiled=True),
        lax.all_to_all(many_live, ("dp", "expert"), split_axis=0, concat_axis=0, tiled=True),
    )
    slot_dx, totals = expert_pass(got_x, got_dy, got_live, slot_limit, weights, zero_sums)
    returned = lax.all_to_all(slot_dx, ("dp", "expert"), split_axis=0, concat_axis=0, tiled=True)
    route_rows = jnp.sum(
        returned.reshape(groups, experts * slot_limit, model_width).astype(jnp.float32), axis=0
    ).astype(jnp.bfloat16)
    per_route = route_rows[slot_of].astype(jnp.float32).reshape(tok_rows, 2, model_width)
    grad_tokens = jnp.sum(per_route, axis=1).astype(jnp.bfloat16)
    return (
        grad_tokens,
        totals[0].astype(jnp.bfloat16)[None],
        totals[1].astype(jnp.bfloat16)[None],
        totals[2].astype(jnp.bfloat16)[None],
    )


def solution(mesh):
    placed = (
        P(("dp", "expert"), None),
        P(("dp", "expert"), None),
        P(("dp", "expert"), None),
        P(("dp", "expert"), None),
        P("expert", None, "dp"),
        P("expert", None, "dp"),
        P("expert", "dp", None),
    )
    return jax.shard_map(
        shards,
        mesh=mesh,
        in_specs=placed,
        out_specs=(
            P(("dp", "expert"), None),
            P("expert", None, "dp"),
            P("expert", None, "dp"),
            P("expert", "dp", None),
        ),
        check_vma=False,
    )
```

profile of v0, /device:TPU:0, one launch (start us, length us, event | category | flops | bytes accessed | tf_op | source)
XLA Modules:
  0.0 660.3 jit_solution(2506988427402694628)
XLA Ops:
  4.0 11.1 %all-to-all-start = ((bf16[128,16,1]{1,2,0:T(2,128)(2,1)}), bf16[128,16,1]{1,2,0:T(2,128)(2,1)S(1)}, u32[]{:S(2)}, u32[]{:S(2)}) async-start(bf16[128,16,1]{1,2,0:T(2,128)(2,1)} %copy.36), calls=%async_computation | async-start | bytes 131072 | tf_op jit(solution)/shard_map/all_to_all | solution.py:107
  29.5 10.3 %all-to-all-start.1 = ((bf16[128,16,2048]{2,1,0:T(8,128)(2,1)}), bf16[128,16,2048]{2,1,0:T(8,128)(2,1)}, u32[]{:S(2)}, u32[]{:S(2)}) async-start(bf16[128,16,2048]{2,1,0:T(8,128)(2,1)} %bitcast.86), calls=%async_computation.1 | async-start | bytes 16777216 | tf_op jit(solution)/shard_map/all_to_all | solution.py:106
  44.9 103.2 %all-to-all-done.1 = bf16[128,16,2048]{2,1,0:T(8,128)(2,1)} async-done(((bf16[128,16,2048]{2,1,0:T(8,128)(2,1)}), bf16[128,16,2048]{2,1,0:T(8,128)(2,1)}, u32[]{:S(2)}, u32[]{:S(2)}) %all-to-all-start.1) | async-done | bytes 8388640 | tf_op jit(solution)/shard_map/all_to_all | solution.py:106
  152.4 14.0 %all-to-all-start.2 = ((bf16[128,16,2048]{2,1,0:T(8,128)(2,1)}), bf16[128,16,2048]{2,1,0:T(8,128)(2,1)}, u32[]{:S(2)}, u32[]{:S(2)}) async-start(bf16[128,16,2048]{2,1,0:T(8,128)(2,1)} %bitcast.85), calls=%async_computation.2 | async-start | bytes 16777216 | tf_op jit(solution)/shard_map/all_to_all | solution.py:105
  169.6 12.6 %gather_fusion.3 = s32[2048]{0:T(1024)S(1)} fusion(s32[128]{0:T(128)S(1)} %get-tuple-element.99, s32[2048]{0:T(1024)S(1)} %broadcast_clamp_fusion.2), kind=kCustom, calls=%fused_computation.3 | custom fusion | bytes 24576 | tf_op jit(solution)/shard_map/gather | solution.py:48
  182.2 12.6 %gather_fusion.7 = s32[2048]{0:T(1024)S(1)} fusion(s32[128]{0:T(128)S(1)} %get-tuple-element.99, s32[2048]{0:T(1024)S(1)} %broadcast_clamp_fusion.3), kind=kCustom, calls=%fused_computation.7 | custom fusion | bytes 24576 | tf_op jit(solution)/shard_map/gather | solution.py:68
  194.8 12.6 %gather_fusion = s32[2048]{0:T(1024)S(1)} fusion(s32[128]{0:T(128)S(1)} %get-tuple-element.97, s32[2048]{0:T(1024)S(1)} %broadcast_clamp_fusion.3), kind=kCustom, calls=%fused_computation | custom fusion | bytes 24576 | tf_op jit(solution)/shard_map/gather | solution.py:67
  210.2 20.8 %gather_fusion.4 = bf16[2048,2048]{1,0:T(8,128)(2,1)} fusion(bf16[2048,2048]{1,0:T(8,128)(2,1)} %bitcast.6, s32[2048]{0:T(1024)S(1)} %broadcast_clamp_fusion.1), kind=kCustom, calls=%fused_computation.4 | custom fusion | bytes 16785408 | tf_op jit(solution)/shard_map/gather | solution.py:50
  231.0 42.5 %all-to-all-done.2 = bf16[128,16,2048]{2,1,0:T(8,128)(2,1)} async-done(((bf16[128,16,2048]{2,1,0:T(8,128)(2,1)}), bf16[128,16,2048]{2,1,0:T(8,128)(2,1)}, u32[]{:S(2)}, u32[]{:S(2)}) %all-to-all-start.2) | async-done | bytes 8388640 | tf_op jit(solution)/shard_map/all_to_all | solution.py:105
  273.5 20.8 %gather_fusion.6 = bf16[2048,2048]{1,0:T(8,128)(2,1)} fusion(bf16[2048,2048]{1,0:T(8,128)(2,1)} %bitcast.14, s32[2048]{0:T(1024)S(1)} %broadcast_clamp_fusion.1), kind=kCustom, calls=%fused_computation.6 | custom fusion | bytes 16785408 | tf_op jit(solution)/shard_map/gather | solution.py:49
  294.3 11.8 %broadcast_select_fusion = (bf16[2048,2048]{1,0:T(8,128)(2,1)}, bf16[2048,2048]{1,0:T(8,128)(2,1)}) fusion(bf16[2048,2048]{1,0:T(8,128)(2,1)} %gather_fusion.6, pred[2048]{0:T(1024)(128)(4,1)S(1)} %iota_compare_fusion.4, bf16[2048,2048]{1,0:T(8,128)(2,1)} %gather_fusion.4), kind=kLoop, calls=%fused_computation.37 | loop fusion | flops 8388608 | bytes 33556480 | tf_op jit(solution)/shard_map/jit(_where)/select_n | solution.py:49
  323.2 172.0 %while.16 = (s32[]{:T(128)}, bf16[2048,2048]{1,0:T(8,128)(2,1)}, f32[2048,1024]{1,0:T(8,128)}, f32[2048,1024]{1,0:T(8,128)}, f32[1024,2048]{1,0:T(8,128)}, /*ind...) while((s32[]{:T(128)}, bf16[2048,2048]{1,0:T(8,128)(2,1)}, ...), condition=%wide.region_10.11_spmd, body=%wide.region_9.10_spmd.sunk | while | flops 17198219264 | bytes 314573312 | solution.py:64
  341.3 6.1 fusion.74
  356.6 9.7 %convolution_add_fusion.8 = f32[1024,2048]{1,0:T(8,128)} fusion(f32[1024,2048]{1,0:T(8,128)} %get-tuple-element.194, bf16[2048,2048]{1,0:T(8,128)(2,1)} %get-tuple-element.211, s32[]{:T(128)S(6)} %select_n.235, f32[512,1024]{1,0:T(8,128)S(1)} %fusion.72, f32[512,1024]{1,0:T(8,128)S(1)} %fusion.71), kind=kOutput, calls=%fused_computation.11.clone.1 | convolution fusion | flops 2152726528 | bytes 23068676 | tf_op jit(solution)/shard_map/while/body/dot_general | solution.py:32
  399.4 9.7 %convolution_add_fusion.8 = f32[1024,2048]{1,0:T(8,128)} fusion(f32[1024,2048]{1,0:T(8,128)} %get-tuple-element.194, bf16[2048,2048]{1,0:T(8,128)(2,1)} %get-tuple-element.211, s32[]{:T(128)S(6)} %select_n.235, f32[512,1024]{1,0:T(8,128)S(1)} %fusion.72, f32[512,1024]{1,0:T(8,128)S(1)} %fusion.71), kind=kOutput, calls=%fused_computation.11.clone.1 | convolution fusion | flops 2152726528 | bytes 23068676 | tf_op jit(solution)/shard_map/while/body/dot_general | solution.py:32
  427.1 6.1 fusion.74
  442.3 9.7 %convolution_add_fusion.8 = f32[1024,2048]{1,0:T(8,128)} fusion(f32[1024,2048]{1,0:T(8,128)} %get-tuple-element.194, bf16[2048,2048]{1,0:T(8,128)(2,1)} %get-tuple-element.211, s32[]{:T(128)S(6)} %select_n.235, f32[512,1024]{1,0:T(8,128)S(1)} %fusion.72, f32[512,1024]{1,0:T(8,128)S(1)} %fusion.71), kind=kOutput, calls=%fused_computation.11.clone.1 | convolution fusion | flops 2152726528 | bytes 23068676 | tf_op jit(solution)/shard_map/while/body/dot_general | solution.py:32
  470.0 6.1 fusion.74
  485.3 9.7 %convolution_add_fusion.8 = f32[1024,2048]{1,0:T(8,128)} fusion(f32[1024,2048]{1,0:T(8,128)} %get-tuple-element.194, bf16[2048,2048]{1,0:T(8,128)(2,1)} %get-tuple-element.211, s32[]{:T(128)S(6)} %select_n.235, f32[512,1024]{1,0:T(8,128)S(1)} %fusion.72, f32[512,1024]{1,0:T(8,128)S(1)} %fusion.71), kind=kOutput, calls=%fused_computation.11.clone.1 | convolution fusion | flops 2152726528 | bytes 23068676 | tf_op jit(solution)/shard_map/while/body/dot_general | solution.py:32
  495.2 20.8 %gather_fusion.8 = bf16[2048,2048]{1,0:T(8,128)(2,1)} fusion(bf16[2048,2048]{1,0:T(8,128)(2,1)} %get-tuple-element.65, s32[2048]{0:T(1024)S(1)} %copy-done.7), kind=kCustom, calls=%fused_computation.8 | custom fusion | bytes 16785408 | tf_op jit(solution)/shard_map/gather | solution.py:69
  516.0 7.3 %broadcast_select_fusion.2 = bf16[128,16,2048]{2,1,0:T(8,128)(2,1)} fusion(bf16[128,16,2048]{2,1,0:T(8,128)(2,1)} %bitcast.84, pred[128,16]{1,0:T(8,128)(4,1)S(1)} %copy-done.6), kind=kLoop, calls=%fused_computation.39 | loop fusion | flops 4194304 | bytes 16779264 | tf_op jit(solution)/shard_map/jit(_where)/select_n | solution.py:69
  523.2 15.4 %all-to-all-start.3 = ((bf16[128,16,2048]{2,1,0:T(8,128)(2,1)}), bf16[128,16,2048]{2,1,0:T(8,128)(2,1)}, u32[]{:S(2)}, u32[]{:S(2)}) async-start(bf16[128,16,2048]{2,1,0:T(8,128)(2,1)} %broadcast_select_fusion.2), calls=%async_computation.3 | async-start | bytes 16777216 | tf_op jit(solution)/shard_map/all_to_all | solution.py:110
  545.0 10.5 %convert_bitcast_fusion.1 = (bf16[1,2048,1024]{2,1,0:T(8,128)(2,1)}, bf16[1,2048,1024]{2,1,0:T(8,128)(2,1)}) fusion(f32[2048,1024]{1,0:T(8,128)} %get-tuple-element.67, f32[2048,1024]{1,0:T(8,128)} %get-tuple-element.66), kind=kLoop, calls=%fused_computation.41 | loop fusion | flops 4194304 | bytes 25165824 | tf_op jit(solution)/shard_map/broadcast_in_dim | solution.py:119
  555.5 91.5 %all-to-all-done.3 = bf16[128,16,2048]{2,1,0:T(8,128)(2,1)} async-done(((bf16[128,16,2048]{2,1,0:T(8,128)(2,1)}), bf16[128,16,2048]{2,1,0:T(8,128)(2,1)}, u32[]{:S(2)}, u32[]{:S(2)}) %all-to-all-start.3) | async-done | bytes 8388640 | tf_op jit(solution)/shard_map/all_to_all | solution.py:110
  (193 shorter events, 182.5 us)
Async XLA Ops:
  0.6 15.6 %copy-start = (bf16[128,2048]{1,0:T(8,128)(2,1)S(1)}, bf16[128,2048]{1,0:T(8,128)(2,1)}, u32[]{:S(2)}) copy-start(bf16[128,2048]{1,0:T(8,128)(2,1)} %param.10) | copy-start | bytes 1572868
  2.7 12.6 %copy-start.8 = (s32[256]{0:T(256)}, s32[256]{0:T(256)S(1)}, u32[]{:S(2)}) copy-start(s32[256]{0:T(256)S(1)} %fusion.26) | copy-start | bytes 3076
  4.0 21.2 %all-to-all-start = ((bf16[128,16,1]{1,2,0:T(2,128)(2,1)}), bf16[128,16,1]{1,2,0:T(2,128)(2,1)S(1)}, u32[]{:S(2)}, u32[]{:S(2)}) async-start(bf16[128,16,1]{1,2,0:T(2,128)(2,1)} %copy.36), calls=%async_computation | async-start | bytes 131072 | tf_op jit(solution)/shard_map/all_to_all | solution.py:107
  29.5 10.3 %copy-start.4 = (bf16[128,2048]{1,0:T(8,128)(2,1)S(1)}, bf16[128,2048]{1,0:T(8,128)(2,1)}, u32[]{:S(2)}) copy-start(bf16[128,2048]{1,0:T(8,128)(2,1)} %param.9) | copy-start | bytes 1572868
  29.5 118.6 %all-to-all-start.1 = ((bf16[128,16,2048]{2,1,0:T(8,128)(2,1)}), bf16[128,16,2048]{2,1,0:T(8,128)(2,1)}, u32[]{:S(2)}, u32[]{:S(2)}) async-start(bf16[128,16,2048]{2,1,0:T(8,128)(2,1)} %bitcast.86), calls=%async_computation.1 | async-start | bytes 16777216 | tf_op jit(solution)/shard_map/all_to_all | solution.py:106
  152.4 121.1 %all-to-all-start.2 = ((bf16[128,16,2048]{2,1,0:T(8,128)(2,1)}), bf16[128,16,2048]{2,1,0:T(8,128)(2,1)}, u32[]{:S(2)}, u32[]{:S(2)}) async-start(bf16[128,16,2048]{2,1,0:T(8,128)(2,1)} %bitcast.85), calls=%async_computation.2 | async-start | bytes 16777216 | tf_op jit(solution)/shard_map/all_to_all | solution.py:105
  323.2 172.0 %copy-start.7 = (s32[2048]{0:T(1024)S(1)}, s32[2048]{0:T(1024)}, u32[]{:S(2)}) copy-start(s32[2048]{0:T(1024)} %broadcast_clamp_fusion) | copy-start | bytes 24580
  323.3 6.4 copy-start.12
  336.9 10.5 %slice-start = ((s8[8388608]{0:T(1024)(128)(4,1)}), s8[4194304]{0:T(1024)(128)(4,1)S(1)}, s32[]{:S(2)}) async-start(s8[8388608]{0:T(1024)(128)(4,1)} %bitcast.80), calls=%async_computation.4 | async-start | bytes 8388608 | tf_op jit(solution)/shard_map/while
  341.3 8.9 %slice-start.2 = ((s8[8388608]{0:T(1024)(128)(4,1)}), s8[4194304]{0:T(1024)(128)(4,1)S(1)}, s32[]{:S(2)}) async-start(s8[8388608]{0:T(1024)(128)(4,1)} %bitcast.82), calls=%async_computation.6 | async-start | bytes 8388608 | tf_op jit(solution)/shard_map/while
  366.3 6.4 copy-start.12
  379.8 10.5 %slice-start = ((s8[8388608]{0:T(1024)(128)(4,1)}), s8[4194304]{0:T(1024)(128)(4,1)S(1)}, s32[]{:S(2)}) async-start(s8[8388608]{0:T(1024)(128)(4,1)} %bitcast.80), calls=%async_computation.4 | async-start | bytes 8388608 | tf_op jit(solution)/shard_map/while
  384.2 8.8 %slice-start.2 = ((s8[8388608]{0:T(1024)(128)(4,1)}), s8[4194304]{0:T(1024)(128)(4,1)S(1)}, s32[]{:S(2)}) async-start(s8[8388608]{0:T(1024)(128)(4,1)} %bitcast.82), calls=%async_computation.6 | async-start | bytes 8388608 | tf_op jit(solution)/shard_map/while
  409.1 6.4 copy-start.12
  422.6 10.5 %slice-start = ((s8[8388608]{0:T(1024)(128)(4,1)}), s8[4194304]{0:T(1024)(128)(4,1)S(1)}, s32[]{:S(2)}) async-start(s8[8388608]{0:T(1024)(128)(4,1)} %bitcast.80), calls=%async_computation.4 | async-start | bytes 8388608 | tf_op jit(solution)/shard_map/while
  427.1 8.9 %slice-start.2 = ((s8[8388608]{0:T(1024)(128)(4,1)}), s8[4194304]{0:T(1024)(128)(4,1)S(1)}, s32[]{:S(2)}) async-start(s8[8388608]{0:T(1024)(128)(4,1)} %bitcast.82), calls=%async_computation.6 | async-start | bytes 8388608 | tf_op jit(solution)/shard_map/while
  452.0 6.4 copy-start.12
  465.6 10.5 %slice-start = ((s8[8388608]{0:T(1024)(128)(4,1)}), s8[4194304]{0:T(1024)(128)(4,1)S(1)}, s32[]{:S(2)}) async-start(s8[8388608]{0:T(1024)(128)(4,1)} %bitcast.80), calls=%async_computation.4 | async-start | bytes 8388608 | tf_op jit(solution)/shard_map/while
  470.0 8.9 %slice-start.2 = ((s8[8388608]{0:T(1024)(128)(4,1)}), s8[4194304]{0:T(1024)(128)(4,1)S(1)}, s32[]{:S(2)}) async-start(s8[8388608]{0:T(1024)(128)(4,1)} %bitcast.82), calls=%async_computation.6 | async-start | bytes 8388608 | tf_op jit(solution)/shard_map/while
  495.1 20.8 %copy-start.6 = (pred[128,16]{1,0:T(8,128)(4,1)S(1)}, pred[128,16]{1,0:T(8,128)(4,1)}, u32[]{:S(2)}) copy-start(pred[128,16]{1,0:T(8,128)(4,1)} %fusion.20) | copy-start | bytes 6148
  523.2 15.4 %copy-start.10 = (s32[128,2]{0,1:T(2,128)S(1)}, s32[128,2]{0,1:T(2,128)}, u32[]{:S(2)}) copy-start(s32[128,2]{0,1:T(2,128)} %param.12) | copy-start | bytes 3076
  523.2 15.7 %copy-start.9 = (s32[256]{0:T(256)S(1)}, s32[256]{0:T(256)}, u32[]{:S(2)}) copy-start(s32[256]{0:T(256)} %copy-done.8) | copy-start | bytes 3076
  523.2 123.8 %all-to-all-start.3 = ((bf16[128,16,2048]{2,1,0:T(8,128)(2,1)}), bf16[128,16,2048]{2,1,0:T(8,128)(2,1)}, u32[]{:S(2)}, u32[]{:S(2)}) async-start(bf16[128,16,2048]{2,1,0:T(8,128)(2,1)} %broadcast_select_fusion.2), calls=%async_computation.3 | async-start | bytes 16777216 | tf_op jit(solution)/shard_map/all_to_all | solution.py:110
  652.2 7.7 %copy-start.1 = (bf16[128,2048]{1,0:T(8,128)(2,1)S(1)}, bf16[128,2048]{1,0:T(8,128)(2,1)}, u32[]{:S(2)}) copy-start(bf16[128,2048]{1,0:T(8,128)(2,1)} %param.10) | copy-start | bytes 1572868
  (28 other events, 110.9 us)
where the time goes:
time: 670 us; the launch traced here: 660 us
  waiting for transfers between devices  237 us (35%)
  local copies, waits for them, and re-layouts  163 us (24%)
  matrix products  152 us (23%)
  other arithmetic  54.4 us (8%)
  starting transfers between devices  50.9 us (8%)
    all_to_all x1, waiting for transfers between devices, shards(): lax.all_to_all(many_dy, ('dp', 'expert'), split_axis=0, concat_axis=0, ti...  103 us
    all_to_all x1, waiting for transfers between devices, shards(): lax.all_to_all(slot_dx, ('dp', 'expert'), split_axis=0, concat_axis=0, ti...  91.5 us
    all_to_all x1, waiting for transfers between devices, shards(): lax.all_to_all(many_x, ('dp', 'expert'), split_axis=0, concat_axis=0, til...  42.5 us
    dot_general x4, matrix products, block_terms(): lax.dot_general(hidden, dy_block, contract_rows, preferred_element_type=j...  38.7 us
    dot_general x4, matrix products, block_terms(): lax.dot_general(d_up, up_weight, contract_last, preferred_element_type=jn...  24.4 us
    dot_general x4, matrix products, block_terms(): jnp.dot(in_block, gate_weight, preferred_element_type=jnp.float32)  21.2 us
    gather x1, local copies, waits for them, and re-layouts, expert_pass(): packed_dx[back_row]  20.8 us
    gather x1, local copies, waits for them, and re-layouts, expert_pass(): sent_grads[source_row]  20.8 us
  transfers between devices with their start and end apart: 4, of which 3 were waited for; matrix products, arithmetic and copies ran while one was open for 14% of the time, Pallas kernels for 0%

commit v1 on v0

v1 whole, which is shorter than its diff:
```python
import jax
import jax.numpy as jnp
from jax import lax
from jax.experimental import pallas as pl
from jax.experimental.pallas import tpu as pltpu
from jax.sharding import Mesh, PartitionSpec as P

DEVICE = ("yhi", "core", "x", "z", "ylo")
EXPERT = ("x", "z", "ylo")
PEERS = ("yhi", "x", "z", "ylo")

BF16 = jnp.bfloat16
F32 = jnp.float32
RANKS = 8
ROWS = 2 * RANKS
MIB = 1024 * 1024

CONTRACT_LAST = (((1,), (1,)), ((), ()))
CONTRACT_ROWS = (((0,), (0,)), ((), ()))


def params(mib):
    return pltpu.CompilerParams(vmem_limit_bytes=mib * MIB)


def route_slots(ids_ref, experts, chunk):
    tok = ids_ref.shape[0]
    lane = lax.broadcasted_iota(jnp.int32, (tok, experts), 1)
    picks = [(ids_ref[:, k : k + 1] == lane).astype(F32) for k in range(2)]
    below = lax.broadcasted_iota(jnp.int32, (tok, tok), 1) < lax.broadcasted_iota(
        jnp.int32, (tok, tok), 0
    )
    ahead = jnp.dot(
        below.astype(BF16), (picks[0] + picks[1]).astype(BF16), preferred_element_type=F32
    )
    slots = []
    for k in range(2):
        rank = jnp.sum(ahead * picks[k], axis=1, keepdims=True).astype(jnp.int32) - chunk * RANKS
        inside = (rank >= 0) & (rank < RANKS)
        slots.append(jnp.where(inside, ids_ref[:, k : k + 1] * ROWS + rank, -1))
    return slots


def pack_kernel(chunk, experts, ids_ref, gates_ref, tok_ref, grad_ref, out_ref):
    tok = ids_ref.shape[0]
    slots = route_slots(ids_ref, experts, chunk)
    lane = lax.broadcasted_iota(jnp.int32, (tok, experts * ROWS), 1)
    x_pick = ((lane == slots[0]) | (lane == slots[1])).astype(BF16)
    packed = lax.dot_general(x_pick, tok_ref[...], CONTRACT_ROWS, preferred_element_type=F32)
    for k in range(2):
        dy = (gates_ref[:, k : k + 1] * grad_ref[...].astype(F32)).astype(BF16)
        there = jnp.where(slots[k] >= 0, slots[k] + RANKS, -1)
        dy_pick = (lane == there).astype(BF16)
        packed = packed + lax.dot_general(
            dy_pick, dy, CONTRACT_ROWS, preferred_element_type=F32
        )
    packed = packed.astype(BF16).reshape(experts, ROWS, packed.shape[1])
    out_ref[:experts] = packed
    out_ref[experts:] = packed


def pack(chunk, experts, ids, gates, tokens, grad_out):
    tok, width = tokens.shape
    cols = 512
    return pl.pallas_call(
        lambda *refs: pack_kernel(chunk, experts, *refs),
        grid=(width // cols,),
        in_specs=[
            pl.BlockSpec((tok, 2), lambda i: (0, 0)),
            pl.BlockSpec((tok, 2), lambda i: (0, 0)),
            pl.BlockSpec((tok, cols), lambda i: (0, i)),
            pl.BlockSpec((tok, cols), lambda i: (0, i)),
        ],
        out_specs=pl.BlockSpec((2 * experts, ROWS, cols), lambda i: (0, 0, i)),
        out_shape=jax.ShapeDtypeStruct((2 * experts, ROWS, width), BF16),
        compiler_params=params(48),
        cost_estimate=pl.CostEstimate(
            flops=2 * 3 * tok * experts * ROWS * width,
            bytes_accessed=12 * MIB,
            transcendentals=0,
        ),
        name="pack",
    )(ids, gates, tokens, grad_out)


def rows_kernel(
    hid_steps,
    got_ref,
    wg_ref,
    wu_ref,
    wd_ref,
    wg_rows_ref,
    wu_rows_ref,
    x_ref,
    dy_ref,
    h_ref,
    dg_ref,
    du_ref,
    dx_ref,
    dx_wide,
):
    step = pl.program_id(0)
    peers, _, width = got_ref.shape
    rows = peers * RANKS
    hid_cols = wg_ref.shape[1]
    dx_cols = wg_rows_ref.shape[0]

    @pl.when(step == 0)
    def _():
        for col in range(0, width, 512):
            both = got_ref[:, :, col : col + 512].astype(F32)
            x_ref[:, col : col + 512] = both[:, :RANKS].reshape(rows, 512).astype(BF16)
            dy_ref[:, col : col + 512] = both[:, RANKS:].reshape(rows, 512).astype(BF16)

    @pl.when(step < hid_steps)
    def _():
        x = x_ref[...]
        g = jnp.dot(x, wg_ref[...], preferred_element_type=F32)
        u = jnp.dot(x, wu_ref[...], preferred_element_type=F32)
        dh = lax.dot_general(dy_ref[...], wd_ref[...], CONTRACT_LAST, preferred_element_type=F32)
        sig = jax.nn.sigmoid(g)
        silu = g * sig
        cols = pl.ds(pl.multiple_of(step * hid_cols, hid_cols), hid_cols)
        h_ref[:, cols] = (silu * u).astype(BF16)
        dg_ref[:, cols] = (dh * u * sig * (1.0 + g * (1.0 - sig))).astype(BF16)
        du_ref[:, cols] = (dh * silu).astype(BF16)

    for part in range(width // dx_cols):

        @pl.when(step == hid_steps + part)
        def _():
            dx = lax.dot_general(
                dg_ref[...], wg_rows_ref[...], CONTRACT_LAST, preferred_element_type=F32
            )
            dx = dx + lax.dot_general(
                du_ref[...], wu_rows_ref[...], CONTRACT_LAST, preferred_element_type=F32
            )
            half, col = divmod(part * dx_cols, width // 2)
            dx_wide[:, half * RANKS : (half + 1) * RANKS, col : col + dx_cols] = dx.reshape(
                peers, RANKS, dx_cols
            )

    @pl.when(step == pl.num_programs(0) - 1)
    def _():
        dx_ref[...] = dx_wide[...].astype(BF16)


def rows_pass(got, wg, wu, wd):
    peers, _, width = got.shape
    hid = wg.shape[1]
    rows = peers * RANKS
    hid_cols, dx_cols = 256, 512
    hid_steps, dx_steps = hid // hid_cols, width // dx_cols
    first = lambda i: jnp.minimum(i, hid_steps - 1)
    second = lambda i: jnp.maximum(i - hid_steps, 0)
    whole2 = lambda r, c: pl.BlockSpec((r, c), lambda i: (0, 0))
    return pl.pallas_call(
        lambda *refs: rows_kernel(hid_steps, *refs),
        grid=(hid_steps + dx_steps,),
        in_specs=[
            pl.BlockSpec((peers, ROWS, width), lambda i: (0, 0, 0)),
            pl.BlockSpec((width, hid_cols), lambda i: (0, first(i))),
            pl.BlockSpec((width, hid_cols), lambda i: (0, first(i))),
            pl.BlockSpec((hid_cols, width), lambda i: (first(i), 0)),
            pl.BlockSpec((dx_cols, hid), lambda i: (second(i), 0)),
            pl.BlockSpec((dx_cols, hid), lambda i: (second(i), 0)),
        ],
        out_specs=[
            whole2(rows, width),
            whole2(rows, width),
            whole2(rows, hid),
            whole2(rows, hid),
            whole2(rows, hid),
            pl.BlockSpec((peers, ROWS, width // 2), lambda i: (0, 0, 0)),
        ],
        out_shape=[
            jax.ShapeDtypeStruct((rows, width), BF16),
            jax.ShapeDtypeStruct((rows, width), BF16),
            jax.ShapeDtypeStruct((rows, hid), BF16),
            jax.ShapeDtypeStruct((rows, hid), BF16),
            jax.ShapeDtypeStruct((rows, hid), BF16),
            jax.ShapeDtypeStruct((peers, ROWS, width // 2), BF16),
        ],
        scratch_shapes=[pltpu.VMEM((peers, ROWS, width // 2), F32)],
        compiler_params=params(56),
        cost_estimate=pl.CostEstimate(
            flops=2 * 5 * rows * width * hid, bytes_accessed=32 * MIB, transcendentals=rows * hid
        ),
        name="rows",
    )(got, wg, wu, wd, wg, wu)


def grads_kernel(groups, *refs):
    x, dy, h, dg, du = (refs[i * groups : (i + 1) * groups] for i in range(5))
    gate_ref, up_ref, down_ref = refs[5 * groups :]

    def total(left, right):
        acc = None
        for a, b in zip(left, right):
            term = lax.dot_general(a[...], b[...], CONTRACT_ROWS, preferred_element_type=F32)
            acc = term if acc is None else acc + term
        return acc

    gate_ref[...] = total(x, dg).astype(BF16)
    up_ref[...] = total(x, du).astype(BF16)
    down_ref[...] = total(dy, h).T.astype(BF16)


def weight_grads(groups):
    rows, width = groups[0][0].shape
    hid = groups[0][2].shape[1]
    cols = 256
    count = len(groups)
    narrow = pl.BlockSpec((rows, cols), lambda i: (0, i))
    whole = pl.BlockSpec((rows, hid), lambda i: (0, 0))
    return pl.pallas_call(
        lambda *refs: grads_kernel(count, *refs),
        grid=(width // cols,),
        in_specs=[narrow] * (2 * count) + [whole] * (3 * count),
        out_specs=[
            pl.BlockSpec((cols, hid), lambda i: (i, 0)),
            pl.BlockSpec((cols, hid), lambda i: (i, 0)),
            pl.BlockSpec((hid, cols), lambda i: (0, i)),
        ],
        out_shape=[
            jax.ShapeDtypeStruct((width, hid), BF16),
            jax.ShapeDtypeStruct((width, hid), BF16),
            jax.ShapeDtypeStruct((hid, width), BF16),
        ],
        compiler_params=params(56),
        cost_estimate=pl.CostEstimate(
            flops=2 * 3 * count * rows * width * hid, bytes_accessed=40 * MIB, transcendentals=0
        ),
        name="weight_grads",
    )(*[group[i] for i in range(5) for group in groups])


def collect_kernel(experts, ids_ref, back0_ref, back1_ref, out_ref):
    half = pl.program_id(0)
    tok = ids_ref.shape[0]
    lane = lax.broadcasted_iota(jnp.int32, (tok, experts * ROWS), 1)
    total = None
    for chunk, back in enumerate((back0_ref, back1_ref)):
        slots = route_slots(ids_ref, experts, chunk)
        pick = jnp.zeros((tok, experts * ROWS), jnp.bool_)
        for slot in slots:
            pick = pick | (lane == jnp.where(slot >= 0, slot + half * RANKS, -1))
        dx = (back[:experts].astype(F32) + back[experts:].astype(F32)).astype(BF16)
        dx = dx.reshape(experts * ROWS, dx.shape[2])
        term = jnp.dot(pick.astype(BF16), dx, preferred_element_type=F32)
        total = term if total is None else total + term
    out_ref[...] = total.astype(BF16)


def collect(experts, ids, back):
    tok = ids.shape[0]
    peers, _, half = back[0].shape
    cols = half
    whole = pl.BlockSpec((peers, ROWS, cols), lambda i: (0, 0, 0))
    return pl.pallas_call(
        lambda *refs: collect_kernel(experts, *refs),
        grid=(2,),
        in_specs=[pl.BlockSpec((tok, 2), lambda i: (0, 0)), whole, whole],
        out_specs=pl.BlockSpec((tok, cols), lambda i: (0, i)),
        out_shape=jax.ShapeDtypeStruct((tok, 2 * half), BF16),
        compiler_params=params(48),
        cost_estimate=pl.CostEstimate(
            flops=2 * 4 * tok * experts * ROWS * half, bytes_accessed=5 * MIB, transcendentals=0
        ),
        name="collect",
    )(ids, back[0], back[1])


def exchange(rows):
    return lax.all_to_all(rows, PEERS, split_axis=0, concat_axis=0, tiled=True)


def other_core(rows):
    return lax.ppermute(rows, "core", [(0, 1), (1, 0)])


def shards(tokens, grad_out, gates, expert_ids, w_gate, w_up, w_down):
    experts = lax.axis_size(EXPERT)
    wg, wu, wd = w_gate[0], w_up[0], w_down[0]
    got = []
    for chunk in range(2):
        got.append(exchange(pack(chunk, experts, expert_ids, gates, tokens, grad_out)))
    groups, back = [], []
    for chunk in range(2):
        mine = rows_pass(got[chunk], wg, wu, wd)
        theirs = rows_pass(other_core(got[chunk]), wg, wu, wd)
        groups += [mine[:5], theirs[:5]]
        partial = mine[5].astype(F32) + other_core(theirs[5]).astype(F32)
        back.append(exchange(partial.astype(BF16)))
    grads = weight_grads(groups)
    grad_tokens = collect(experts, expert_ids, back)
    return (grad_tokens,) + tuple(grad[None] for grad in grads)


def solution(mesh):
    fine = Mesh(mesh.devices.reshape(2, 2, 4, 4, 2), DEVICE)
    per_token = P(DEVICE, None)
    columns = P(EXPERT, None, ("yhi", "core"))
    rows = P(EXPERT, ("yhi", "core"), None)
    return jax.shard_map(
        shards,
        mesh=fine,
        in_specs=(per_token,) * 4 + (columns, columns, rows),
        out_specs=(per_token, columns, columns, rows),
        check_vma=False,
    )
```

time: 670 us -> 297 us (0.44); the launches traced: 660 us -> 295 us
  local copies, waits for them, and re-layouts: 163 us -> 9.68 us
  matrix products: 152 us -> 0 us
  Pallas kernels: 0 us -> 136 us
  waiting for transfers between devices: 237 us -> 101 us
  other arithmetic: 54.4 us -> 8.74 us
  starting transfers between devices: 50.9 us -> 38.9 us
    dot_general x32 -> x0, matrix products: 152 us -> none  [the longest x4 38.7 us: block_terms(): lax.dot_general(hidden, dy_block, contract_rows, preferred_element_type=j...]
    pallas_call x0 -> x8, Pallas kernels: none -> 136 us  [the longest x4 87.7 us: rows_pass(): pl.pallas_call(lambda *refs: rows_kernel(hid_steps, *refs), grid=(hid_ste...]
    all_to_all x4, waiting for transfers between devices: 237 us -> 101 us  [exchange(): return lax.all_to_all(rows, PEERS, split_axis=0, concat_axis=0, tiled=True)]
    gather x12 -> x0, local copies, waits for them, and re-layouts: 114 us -> none  [the longest x1 20.8 us: expert_pass(): packed_dx[back_row]]
    select_n x9 -> x0, other arithmetic: 21.6 us -> none  [the longest x1 11.8 us: expert_pass(): jnp.where(within[:, None], sent_rows[source_row], jnp.zeros((), jnp.bfloa...]
    while x80 -> x0, local copies, waits for them, and re-layouts: 19.1 us -> none
    broadcast_in_dim x7 -> x0, local copies, waits for them, and re-layouts: 18 us -> none  [the longest x1 4.29 us: expert_pass(): start_dx = jnp.zeros((slot_count, model_width), jnp.bfloat16)]
    broadcast_in_dim x2 -> x0, other arithmetic: 16.6 us -> none  [the longest x1 10.5 us: shards(): totals[1].astype(jnp.bfloat16)[None]]
  transfers between devices with their start and end apart: 4 -> 8, of which waited for: 3 -> 3; matrix products, arithmetic and copies ran while one was open for 14% -> 3% of each run, Pallas kernels for 0% -> 43%
where the time goes in v1:
time: 297 us; the launch traced here: 295 us
  Pallas kernels  136 us (46%)
  waiting for transfers between devices  101 us (34%)
  starting transfers between devices  38.9 us (13%)
  local copies, waits for them, and re-layouts  9.68 us (3%)
  other arithmetic  8.74 us (3%)
    all_to_all x4, waiting for transfers between devices, exchange(): return lax.all_to_all(rows, PEERS, split_axis=0, concat_axis=0, tiled=True)  101 us
    pallas_call x4, Pallas kernels, rows_pass(): pl.pallas_call(lambda *refs: rows_kernel(hid_steps, *refs), grid=(hid_ste...  87.7 us
    all_to_all x4, starting transfers between devices, exchange(): return lax.all_to_all(rows, PEERS, split_axis=0, concat_axis=0, tiled=True)  38.3 us
    pallas_call x1, Pallas kernels, weight_grads(): pl.pallas_call(lambda *refs: grads_kernel(count, *refs), grid=(width // c...  34.9 us
    unnamed x16, local copies, waits for them, and re-layouts  9.68 us
    pallas_call x2, Pallas kernels, pack(): pl.pallas_call(lambda *refs: pack_kernel(chunk, experts, *refs), grid=(wi...  9.23 us
    convert_element_type x2, other arithmetic, shards(): back.append(exchange(partial.astype(BF16)))  8.74 us
  transfers between devices with their start and end apart: 8, of which 3 were waited for; matrix products, arithmetic and copies ran while one was open for 3% of the time, Pallas kernels for 43%

profile of v1, /device:TPU:0, one launch (start us, length us, event | category | flops | bytes accessed | tf_op | source)
XLA Modules:
  0.0 295.4 jit_solution(4360985171589893523)
XLA Ops:
  0.6 0.8 copy.15.refs_0_
  1.4 0.8 copy.12.refs_1_
  2.2 1.0 copy-done.2
  3.2 1.0 copy-done.4
  4.3 4.6 %pack.2 = bf16[64,16,2048]{2,1,0:T(8,128)(2,1)S(1)} custom-call(s32[128,2]{1,0:T(8,128)S(1)} %copy.15.refs_0_, f32[128,2]{1,0:T(8,128)S(1)} %copy.12.refs_1_, bf16[128,2048]{1,0:T(8,128)(2,1)S(1)} %copy-done.2, bf16[128,2048]{1,0:T(8,128)(2,1)S(1)} %copy-done.4), custom_call_target="tpu_custom_call" | custom-call | flops 805306368 | bytes 12582912 | tf_op jit(solution)/shard_map/pack/pallas_call | solution.py:65
  8.9 2.0 copy-done.1
  10.9 11.9 %all-to-all-start = ((bf16[64,16,2048]{2,1,0:T(8,128)(2,1)}), bf16[64,16,2048]{2,1,0:T(8,128)(2,1)}, u32[]{:S(2)}, u32[]{:S(2)}) async-start(bf16[64,16,2048]{2,1,0:T(8,128)(2,1)} %copy-done.1), calls=%async_computation | async-start | bytes 8388608 | tf_op jit(solution)/shard_map/all_to_all | solution.py:275
  22.9 4.6 %pack.3 = bf16[64,16,2048]{2,1,0:T(8,128)(2,1)S(1)} custom-call(s32[128,2]{1,0:T(8,128)S(1)} %copy.15.refs_0_, f32[128,2]{1,0:T(8,128)S(1)} %copy.12.refs_1_, bf16[128,2048]{1,0:T(8,128)(2,1)S(1)} %copy-done.3, bf16[128,2048]{1,0:T(8,128)(2,1)S(1)} %copy-done.5), custom_call_target="tpu_custom_call" | custom-call | flops 805306368 | bytes 12582912 | tf_op jit(solution)/shard_map/pack/pallas_call | solution.py:65
  27.5 2.0 copy-done
  29.5 46.6 %all-to-all-done.refs_0_ = bf16[64,16,2048]{2,1,0:T(8,128)(2,1)} async-done(((bf16[64,16,2048]{2,1,0:T(8,128)(2,1)}), bf16[64,16,2048]{2,1,0:T(8,128)(2,1)}, u32[]{:S(2)}, u32[]{:S(2)}) %all-to-all-start) | async-done | bytes 4194336 | tf_op jit(solution)/shard_map/all_to_all | solution.py:275
  76.1 9.3 %all-to-all-start.2 = ((bf16[64,16,2048]{2,1,0:T(8,128)(2,1)}), bf16[64,16,2048]{2,1,0:T(8,128)(2,1)}, u32[]{:S(2)}, u32[]{:S(2)}) async-start(bf16[64,16,2048]{2,1,0:T(8,128)(2,1)} %copy-done), calls=%async_computation.2 | async-start | bytes 8388608 | tf_op jit(solution)/shard_map/all_to_all | solution.py:275
  85.5 51.2 %all-to-all-done.2.refs_0_ = bf16[64,16,2048]{2,1,0:T(8,128)(2,1)} async-done(((bf16[64,16,2048]{2,1,0:T(8,128)(2,1)}), bf16[64,16,2048]{2,1,0:T(8,128)(2,1)}, u32[]{:S(2)}, u32[]{:S(2)}) %all-to-all-start.2) | async-done | bytes 4194336 | tf_op jit(solution)/shard_map/all_to_all | solution.py:275
  136.7 21.9 %rows.5 = (bf16[512,2048]{1,0:T(8,128)(2,1)}, bf16[512,2048]{1,0:T(8,128)(2,1)}, bf16[512,1024]{1,0:T(8,128)(2,1)}, bf16[512,1024]{1,0:T(8,128)(2,1)}, bf16[512,...) custom-call(bf16[64,16,2048]{2,1,0:T(8,128)(2,1)} %collective-permute-done.refs_0_, bf16[2048,1024]{1,0:T(8,128)(2,1)} %bitcast.6, ...), custom_call_target="tpu_custom_call" | custom-call | flops 10737418240 | bytes 33554432 | tf_op jit(solution)/shard_map/rows/pallas_call | solution.py:157
  159.1 2.0 copy-done.6
  161.2 21.9 %rows.7 = (bf16[512,2048]{1,0:T(8,128)(2,1)}, bf16[512,2048]{1,0:T(8,128)(2,1)}, bf16[512,1024]{1,0:T(8,128)(2,1)}, bf16[512,1024]{1,0:T(8,128)(2,1)}, bf16[512,...) custom-call(bf16[64,16,2048]{2,1,0:T(8,128)(2,1)} %copy-done.6, bf16[2048,1024]{1,0:T(8,128)(2,1)} %bitcast.8, ...), custom_call_target="tpu_custom_call" | custom-call | flops 10737418240 | bytes 33554432 | tf_op jit(solution)/shard_map/rows/pallas_call | solution.py:157
  183.1 21.9 %rows.4 = (bf16[512,2048]{1,0:T(8,128)(2,1)}, bf16[512,2048]{1,0:T(8,128)(2,1)}, bf16[512,1024]{1,0:T(8,128)(2,1)}, bf16[512,1024]{1,0:T(8,128)(2,1)}, bf16[512,...) custom-call(bf16[64,16,2048]{2,1,0:T(8,128)(2,1)} %all-to-all-done.refs_0_, bf16[2048,1024]{1,0:T(8,128)(2,1)} %bitcast.10, ...), custom_call_target="tpu_custom_call" | custom-call | flops 10737418240 | bytes 33554432 | tf_op jit(solution)/shard_map/rows/pallas_call | solution.py:157
  205.0 4.1 %add_convert_fusion.1 = bf16[64,16,1024]{2,1,0:T(8,128)(2,1)} fusion(bf16[64,16,1024]{2,1,0:T(8,128)(2,1)S(1)} %collective-permute-done.1, bf16[64,16,1024]{2,1,0:T(8,128)(2,1)} %get-tuple-element.31), kind=kLoop, calls=%fused_computation.1 | loop fusion | flops 4194304 | bytes 6291456 | tf_op jit(solution)/shard_map/convert_element_type | solution.py:294
  209.1 9.7 %all-to-all-start.1 = ((bf16[64,16,1024]{2,1,0:T(8,128)(2,1)}), bf16[64,16,1024]{2,1,0:T(8,128)(2,1)S(1)}, u32[]{:S(2)}, u32[]{:S(2)}) async-start(bf16[64,16,1024]{2,1,0:T(8,128)(2,1)} %add_convert_fusion.1), calls=%async_computation.1 | async-start | bytes 4194304 | tf_op jit(solution)/shard_map/all_to_all | solution.py:275
  218.8 21.9 %rows.6 = (bf16[512,2048]{1,0:T(8,128)(2,1)}, bf16[512,2048]{1,0:T(8,128)(2,1)}, bf16[512,1024]{1,0:T(8,128)(2,1)}, bf16[512,1024]{1,0:T(8,128)(2,1)}, bf16[512,...) custom-call(bf16[64,16,2048]{2,1,0:T(8,128)(2,1)} %all-to-all-done.2.refs_0_, bf16[2048,1024]{1,0:T(8,128)(2,1)} %bitcast.12, ...), custom_call_target="tpu_custom_call" | custom-call | flops 10737418240 | bytes 33554432 | tf_op jit(solution)/shard_map/rows/pallas_call | solution.py:157
  240.7 4.7 %add_convert_fusion = bf16[64,16,1024]{2,1,0:T(8,128)(2,1)} fusion(bf16[64,16,1024]{2,1,0:T(8,128)(2,1)} %collective-permute-done.3, bf16[64,16,1024]{2,1,0:T(8,128)(2,1)} %get-tuple-element.33), kind=kLoop, calls=%fused_computation | loop fusion | flops 4194304 | bytes 6291456 | tf_op jit(solution)/shard_map/convert_element_type | solution.py:294
  245.4 3.1 %all-to-all-done.1.refs_1_ = bf16[64,16,1024]{2,1,0:T(8,128)(2,1)S(1)} async-done(((bf16[64,16,1024]{2,1,0:T(8,128)(2,1)}), bf16[64,16,1024]{2,1,0:T(8,128)(2,1)S(1)}, u32[]{:S(2)}, u32[]{:S(2)}) %all-to-all-start.1) | async-done | bytes 2097184 | tf_op jit(solution)/shard_map/all_to_all | solution.py:275
  248.5 7.4 %all-to-all-start.3 = ((bf16[64,16,1024]{2,1,0:T(8,128)(2,1)}), bf16[64,16,1024]{2,1,0:T(8,128)(2,1)}, u32[]{:S(2)}, u32[]{:S(2)}) async-start(bf16[64,16,1024]{2,1,0:T(8,128)(2,1)} %add_convert_fusion), calls=%async_computation.3 | async-start | bytes 4194304 | tf_op jit(solution)/shard_map/all_to_all | solution.py:275
  255.9 34.9 %weight_grads.1 = (bf16[2048,1024]{1,0:T(8,128)(2,1)}, bf16[2048,1024]{1,0:T(8,128)(2,1)}, bf16[1024,2048]{1,0:T(8,128)(2,1)}) custom-call(bf16[512,2048]{1,0:T(8,128)(2,1)} %get-tuple-element.35.refs_0_, bf16[512,2048]{1,0:T(8,128)(2,1)} %get-tuple-element.36.refs_1_, bf16[512,2048]{1,0:T(8,128)(2,1)} %get-tuple-element.37.refs_2_, ...), custom_call_target="tpu_custom_call" | custom-call | flops 25769803776 | bytes 41943040 | tf_op jit(solution)/shard_map/weight_grads/pallas_call | solution.py:216
  290.8 4.6 %collect.1 = bf16[128,2048]{1,0:T(8,128)(2,1)} custom-call(s32[128,2]{1,0:T(8,128)S(1)} %copy.15.refs_0_, bf16[64,16,1024]{2,1,0:T(8,128)(2,1)S(1)} %all-to-all-done.1.refs_1_, bf16[64,16,1024]{2,1,0:T(8,128)(2,1)} %all-to-all-done.3.refs_2_), custom_call_target="tpu_custom_call" | custom-call | flops 536870912 | bytes 5242880 | tf_op jit(solution)/shard_map/collect/pallas_call | solution.py:260
  (18 shorter events, 0.6 us)
Async XLA Ops:
  2.2 1.0 copy-start.2
  3.2 1.0 copy-start.4
  8.9 2.0 copy-start.1
  10.9 11.9 %copy-start.3 = (bf16[128,2048]{1,0:T(8,128)(2,1)S(1)}, bf16[128,2048]{1,0:T(8,128)(2,1)}, u32[]{:S(2)}) copy-start(bf16[128,2048]{1,0:T(8,128)(2,1)} %refs_2_.3) | copy-start | bytes 1572868
  10.9 11.9 %copy-start.5 = (bf16[128,2048]{1,0:T(8,128)(2,1)S(1)}, bf16[128,2048]{1,0:T(8,128)(2,1)}, u32[]{:S(2)}) copy-start(bf16[128,2048]{1,0:T(8,128)(2,1)} %refs_3_.3) | copy-start | bytes 1572868
  10.9 65.2 %all-to-all-start = ((bf16[64,16,2048]{2,1,0:T(8,128)(2,1)}), bf16[64,16,2048]{2,1,0:T(8,128)(2,1)}, u32[]{:S(2)}, u32[]{:S(2)}) async-start(bf16[64,16,2048]{2,1,0:T(8,128)(2,1)} %copy-done.1), calls=%async_computation | async-start | bytes 8388608 | tf_op jit(solution)/shard_map/all_to_all | solution.py:275
  27.5 2.0 copy-start
  76.1 60.6 %all-to-all-start.2 = ((bf16[64,16,2048]{2,1,0:T(8,128)(2,1)}), bf16[64,16,2048]{2,1,0:T(8,128)(2,1)}, u32[]{:S(2)}, u32[]{:S(2)}) async-start(bf16[64,16,2048]{2,1,0:T(8,128)(2,1)} %copy-done), calls=%async_computation.2 | async-start | bytes 8388608 | tf_op jit(solution)/shard_map/all_to_all | solution.py:275
  85.4 51.3 %collective-permute-start = (bf16[64,16,2048]{2,1,0:T(8,128)(2,1)}, bf16[64,16,2048]{2,1,0:T(8,128)(2,1)}, u32[]{:S(2)}, u32[]{:S(2)}) collective-permute-start(bf16[64,16,2048]{2,1,0:T(8,128)(2,1)} %all-to-all-done.refs_0_), channel_id=1, source_target_pairs={{0,32},{32,0},{1,33},{33,1},{2,34},{34,2},{3,35},{35,3},{4,36},{36... | collective-permute-start | bytes 12582920 | tf_op jit(solution)/shard_map/ppermute | solution.py:279
  136.7 22.4 %collective-permute-start.2 = (bf16[64,16,2048]{2,1,0:T(8,128)(2,1)}, bf16[64,16,2048]{2,1,0:T(8,128)(2,1)S(1)}, u32[]{:S(2)}, u32[]{:S(2)}) collective-permute-start(bf16[64,16,2048]{2,1,0:T(8,128)(2,1)} %all-to-all-done.2.refs_0_), channel_id=1, source_target_pairs={{0,32},{32,0},{1,33},{33,1},{2,34},{34,2},{3,35},{35,3},{4,36},{36... | collective-permute-start | bytes 12582920 | tf_op jit(solution)/shard_map/ppermute | solution.py:279
  158.6 46.4 %collective-permute-start.1 = (bf16[64,16,1024]{2,1,0:T(8,128)(2,1)}, bf16[64,16,1024]{2,1,0:T(8,128)(2,1)S(1)}, u32[]{:S(2)}, u32[]{:S(2)}) collective-permute-start(bf16[64,16,1024]{2,1,0:T(8,128)(2,1)} %get-tuple-element.32), channel_id=1, source_target_pairs={{0,32},{32,0},{1,33},{33,1},{2,34},{34,2},{3,35},{35,3},{4,36},{36... | collective-permute-start | bytes 6291464 | tf_op jit(solution)/shard_map/ppermute | solution.py:279
  159.1 2.0 copy-start.6
  183.1 57.7 %collective-permute-start.3 = (bf16[64,16,1024]{2,1,0:T(8,128)(2,1)}, bf16[64,16,1024]{2,1,0:T(8,128)(2,1)}, u32[]{:S(2)}, u32[]{:S(2)}) collective-permute-start(bf16[64,16,1024]{2,1,0:T(8,128)(2,1)} %get-tuple-element.34), channel_id=1, source_target_pairs={{0,32},{32,0},{1,33},{33,1},{2,34},{34,2},{3,35},{35,3},{4,36},{36... | collective-permute-start | bytes 6291464 | tf_op jit(solution)/shard_map/ppermute | solution.py:279
  209.1 39.4 %all-to-all-start.1 = ((bf16[64,16,1024]{2,1,0:T(8,128)(2,1)}), bf16[64,16,1024]{2,1,0:T(8,128)(2,1)S(1)}, u32[]{:S(2)}, u32[]{:S(2)}) async-start(bf16[64,16,1024]{2,1,0:T(8,128)(2,1)} %add_convert_fusion.1), calls=%async_computation.1 | async-start | bytes 4194304 | tf_op jit(solution)/shard_map/all_to_all | solution.py:275
  248.5 42.3 %all-to-all-start.3 = ((bf16[64,16,1024]{2,1,0:T(8,128)(2,1)}), bf16[64,16,1024]{2,1,0:T(8,128)(2,1)}, u32[]{:S(2)}, u32[]{:S(2)}) async-start(bf16[64,16,1024]{2,1,0:T(8,128)(2,1)} %add_convert_fusion), calls=%async_computation.3 | async-start | bytes 4194304 | tf_op jit(solution)/shard_map/all_to_all | solution.py:275

commit v2 on v0

v2 whole, which is shorter than its diff:
```python
import jax
import jax.numpy as jnp
from jax import lax
from jax.experimental import pallas as pl
from jax.experimental.pallas import tpu as pltpu
from jax.sharding import Mesh, PartitionSpec as P

DEVICE = ("yhi", "core", "x", "z", "ylo")
EXPERT = ("x", "z", "ylo")
PEERS = ("yhi", "x", "z", "ylo")

BF16 = jnp.bfloat16
F32 = jnp.float32
RANKS = 8
ROWS = 2 * RANKS
MIB = 1024 * 1024

CONTRACT_LAST = (((1,), (1,)), ((), ()))
CONTRACT_ROWS = (((0,), (0,)), ((), ()))


def params(mib):
    return pltpu.CompilerParams(vmem_limit_bytes=mib * MIB)


def route_slots(ids_ref, experts, chunk):
    tok = ids_ref.shape[1]
    expert = lax.broadcasted_iota(jnp.int32, (experts, tok), 0)
    picks = [(ids_ref[k : k + 1, :] == expert).astype(F32) for k in range(2)]
    before = lax.broadcasted_iota(jnp.int32, (tok, tok), 0) < lax.broadcasted_iota(
        jnp.int32, (tok, tok), 1
    )
    ahead = jnp.dot(
        (picks[0] + picks[1]).astype(BF16), before.astype(BF16), preferred_element_type=F32
    )
    slots = []
    for k in range(2):
        rank = jnp.sum(ahead * picks[k], axis=0, keepdims=True).astype(jnp.int32) - chunk * RANKS
        inside = (rank >= 0) & (rank < RANKS)
        slots.append(jnp.where(inside, ids_ref[k : k + 1, :] * ROWS + rank, -1))
    return slots


def as_column(row):
    size = row.shape[1]
    same = lax.broadcasted_iota(jnp.int32, (size, size), 0) == lax.broadcasted_iota(
        jnp.int32, (size, size), 1
    )
    return jnp.sum(jnp.where(same, row, jnp.zeros_like(row)), axis=1, keepdims=True)


def pack_kernel(chunk, experts, ids_ref, gates_ref, tok_ref, grad_ref, out_ref, picks):
    tok = ids_ref.shape[1]

    @pl.when(pl.program_id(0) == 0)
    def _():
        slots = route_slots(ids_ref, experts, chunk)
        at = lax.broadcasted_iota(jnp.int32, (experts * ROWS, tok), 0)
        picks[0] = ((at == slots[0]) | (at == slots[1])).astype(BF16)
        for k in range(2):
            there = jnp.where(slots[k] >= 0, slots[k] + RANKS, -1)
            picks[1 + k] = (at == there).astype(BF16)

    packed = jnp.dot(picks[0], tok_ref[...], preferred_element_type=F32)
    for k in range(2):
        gate = as_column(gates_ref[k : k + 1, :])
        dy = (gate * grad_ref[...].astype(F32)).astype(BF16)
        packed = packed + jnp.dot(picks[1 + k], dy, preferred_element_type=F32)
    packed = packed.astype(BF16).reshape(experts, ROWS, packed.shape[1])
    out_ref[:experts] = packed
    out_ref[experts:] = packed


def pack(chunk, experts, ids, gates, tokens, grad_out):
    tok, width = tokens.shape
    cols = 512
    return pl.pallas_call(
        lambda *refs: pack_kernel(chunk, experts, *refs),
        grid=(width // cols,),
        in_specs=[
            pl.BlockSpec((2, tok), lambda i: (0, 0)),
            pl.BlockSpec((2, tok), lambda i: (0, 0)),
            pl.BlockSpec((tok, cols), lambda i: (0, i)),
            pl.BlockSpec((tok, cols), lambda i: (0, i)),
        ],
        out_specs=pl.BlockSpec((2 * experts, ROWS, cols), lambda i: (0, 0, i)),
        out_shape=jax.ShapeDtypeStruct((2 * experts, ROWS, width), BF16),
        scratch_shapes=[pltpu.VMEM((3, experts * ROWS, tok), BF16)],
        compiler_params=params(60),
        cost_estimate=cost(2 * 3 * tok * experts * ROWS * width, 12, 0),
        name="pack",
    )(ids, gates, tokens, grad_out)


def block(size, index):
    return pl.ds(index * size if isinstance(index, int) else pl.multiple_of(index * size, size), size)


def cost(flops, mib, transcendentals=0):
    return pl.CostEstimate(
        flops=flops // 8, bytes_accessed=mib * MIB // 8, transcendentals=transcendentals // 8
    )


def hidden_kernel(
    got0, got1, wg, wu, wd, x, dy, h, dg, du, dx,
    got_v, wg_v, wu_v, wd_v, x_v, dy_v, h_v, dg_v, du_v, dx_v,
    got_sem, w_sem, row_sem, hid_sem, dx_sem,
):
    peers, _, width = got0.shape
    hid = wg.shape[1]
    rows = peers * RANKS
    split, unit, out = 512, 256, 256
    splits, units = width // split, hid // unit

    def got_copy(group, i):
        return pltpu.make_async_copy(
            (got0, got1)[group].at[:, :, block(split, i)],
            got_v.at[group, :, :, block(split, i)],
            got_sem.at[group, i],
        )

    def w_copy(which, j):
        src, dst = ((wg, wg_v), (wu, wu_v), (wd, wd_v))[which]
        at = (block(unit, j), slice(None)) if which == 2 else (slice(None), block(unit, j))
        return pltpu.make_async_copy(src.at[at], dst.at[at], w_sem.at[which, j])

    def out_copy(src, dst, sem, group, cols, i):
        at = (block(rows, group), block(cols, i))
        return pltpu.make_async_copy(src.at[at], dst.at[at], sem)

    for i in range(splits):
        got_copy(0, i).start()
    for which in range(3):
        w_copy(which, 0).start()
    for i in range(splits):
        got_copy(1, i).start()
    for j in range(1, units):
        for which in range(3):
            w_copy(which, j).start()

    def row_copies(group, i):
        return [
            out_copy(src, dst, row_sem.at[n, group, i], group, split, i)
            for n, (src, dst) in enumerate(((x_v, x), (dy_v, dy)))
        ]

    def hid_copies(group, j):
        return [
            out_copy(src, dst, hid_sem.at[n, group, j], group, unit, j)
            for n, (src, dst) in enumerate(((h_v, h), (dg_v, dg), (du_v, du)))
        ]

    for group in range(2):
        here = block(rows, group)

        @pl.loop(0, splits)
        def _(i):
            got_copy(group, i).wait()
            cols = block(split, i)
            both = got_v[group, :, :, cols].astype(F32)
            x_v[here, cols] = both[:, :RANKS].reshape(rows, split).astype(BF16)
            dy_v[here, cols] = both[:, RANKS:].reshape(rows, split).astype(BF16)
            for copy in row_copies(group, i):
                copy.start()

        @pl.loop(0, units)
        def _(j):
            if group == 0:
                for which in range(3):
                    w_copy(which, j).wait()
            cols = block(unit, j)
            g = jnp.dot(x_v[here, :], wg_v[:, cols], preferred_element_type=F32)
            u = jnp.dot(x_v[here, :], wu_v[:, cols], preferred_element_type=F32)
            sig = jax.nn.sigmoid(g)
            silu = g * sig
            h_v[here, cols] = (silu * u).astype(BF16)
            slope = u * sig * (1.0 + g * (1.0 - sig))
            dh = lax.dot_general(
                dy_v[here, :], wd_v[cols, :], CONTRACT_LAST, preferred_element_type=F32
            )
            dg_v[here, cols] = (dh * slope).astype(BF16)
            du_v[here, cols] = (dh * silu).astype(BF16)
            for copy in hid_copies(group, j):
                copy.start()

        if group == 0:
            input_grad_tiles(dg_v, du_v, wg_v, wu_v, rows, out, dx_v)
            pltpu.make_async_copy(dx_v, dx, dx_sem).start()
    pltpu.make_async_copy(dx_v, dx, dx_sem).wait()
    for group in range(2):
        for copy in [c for i in range(splits) for c in row_copies(group, i)]:
            copy.wait()
        for copy in [c for j in range(units) for c in hid_copies(group, j)]:
            copy.wait()


def input_grad_tiles(dg, du, wg, wu, rows, cols, dx):
    peers = rows // RANKS
    half = wg.shape[0] // 2

    @pl.loop(0, half // cols)
    def _(i):
        parts = []
        for side in range(2):
            at = pl.ds(pl.multiple_of(side * half + i * cols, cols), cols)
            part = lax.dot_general(
                dg[:rows, :], wg[at, :], CONTRACT_LAST, preferred_element_type=F32
            ) + lax.dot_general(du[:rows, :], wu[at, :], CONTRACT_LAST, preferred_element_type=F32)
            parts.append(part.reshape(peers, RANKS, cols))
        dx[:, :, block(cols, i)] = jnp.concatenate(parts, axis=1).astype(BF16)


def hidden_pass(got0, got1, wg, wu, wd):
    peers, _, width = got0.shape
    hid = wg.shape[1]
    rows = 2 * peers * RANKS
    splits, units = width // 512, hid // 256
    wide, narrow = (jax.ShapeDtypeStruct((rows, n), BF16) for n in (width, hid))
    return pl.pallas_call(
        hidden_kernel,
        in_specs=[pl.BlockSpec(memory_space=pl.ANY)] * 5,
        out_specs=[pl.BlockSpec(memory_space=pl.ANY)] * 6,
        out_shape=[
            wide,
            wide,
            narrow,
            narrow,
            narrow,
            jax.ShapeDtypeStruct((peers, ROWS, width // 2), BF16),
        ],
        scratch_shapes=[
            pltpu.VMEM((2, peers, ROWS, width), BF16),
            pltpu.VMEM((width, hid), BF16),
            pltpu.VMEM((width, hid), BF16),
            pltpu.VMEM((hid, width), BF16),
            pltpu.VMEM((rows, width), BF16),
            pltpu.VMEM((rows, width), BF16),
            pltpu.VMEM((rows, hid), BF16),
            pltpu.VMEM((rows, hid), BF16),
            pltpu.VMEM((rows, hid), BF16),
            pltpu.VMEM((peers, ROWS, width // 2), BF16),
            pltpu.SemaphoreType.DMA((2, splits)),
            pltpu.SemaphoreType.DMA((3, units)),
            pltpu.SemaphoreType.DMA((2, 2, splits)),
            pltpu.SemaphoreType.DMA((3, 2, units)),
            pltpu.SemaphoreType.DMA,
        ],
        compiler_params=params(60),
        cost_estimate=cost(2 * 4 * rows * width * hid, 36, rows * hid),
        name="hidden",
    )(got0, got1, wg, wu, wd)


def input_grad_kernel(dg_ref, du_ref, wg0_ref, wg1_ref, wu0_ref, wu1_ref, more_ref, dx_ref):
    peers, _, cols = dx_ref.shape
    parts = []
    for wg_ref, wu_ref in ((wg0_ref, wu0_ref), (wg1_ref, wu1_ref)):
        part = lax.dot_general(
            dg_ref[...], wg_ref[...], CONTRACT_LAST, preferred_element_type=F32
        ) + lax.dot_general(du_ref[...], wu_ref[...], CONTRACT_LAST, preferred_element_type=F32)
        parts.append(part.reshape(peers, RANKS, cols))
    dx_ref[...] = (jnp.concatenate(parts, axis=1) + more_ref[...].astype(F32)).astype(BF16)


def input_grad(dg, du, wg, wu, more):
    hid = dg.shape[1]
    width = wg.shape[0]
    peers = more.shape[0]
    rows = peers * RANKS
    cols = 256
    steps = width // 2 // cols
    whole = pl.BlockSpec((rows, hid), lambda i: (1, 0))
    low = pl.BlockSpec((cols, hid), lambda i: (i, 0))
    high = pl.BlockSpec((cols, hid), lambda i: (i + steps, 0))
    out = pl.BlockSpec((peers, ROWS, cols), lambda i: (0, 0, i))
    return pl.pallas_call(
        input_grad_kernel,
        grid=(steps,),
        in_specs=[whole, whole, low, high, low, high, out],
        out_specs=out,
        out_shape=jax.ShapeDtypeStruct(more.shape, BF16),
        compiler_params=params(60),
        cost_estimate=cost(2 * 2 * rows * width * hid, 14, 0),
        name="input_grad",
    )(dg, du, wg, wg, wu, wu, more)


def down_grad_kernel(dy_ref, h_ref, *refs):
    total = lax.dot_general(dy_ref[...], h_ref[...], CONTRACT_ROWS, preferred_element_type=F32)
    if len(refs) > 1:
        total = (refs[0][...] + total).T
    refs[-1][...] = total.astype(refs[-1].dtype)


def down_grad(dy, h, before=None):
    rows, width = dy.shape
    hid = h.shape[1]
    cols = 512
    tall = pl.BlockSpec((cols, hid), lambda i: (i, 0))
    more = () if before is None else (before,)
    return pl.pallas_call(
        down_grad_kernel,
        grid=(width // cols,),
        in_specs=[
            pl.BlockSpec((rows, cols), lambda i: (0, i)),
            pl.BlockSpec((rows, hid), lambda i: (0, 0)),
        ]
        + [tall] * len(more),
        out_specs=pl.BlockSpec((hid, cols), lambda i: (0, i)) if more else tall,
        out_shape=jax.ShapeDtypeStruct(
            (hid, width) if more else (width, hid), BF16 if more else F32
        ),
        compiler_params=params(60),
        cost_estimate=cost(2 * rows * width * hid, 20, 0),
        name="down_grad",
    )(dy, h, *more)


def gate_up_kernel(x0_ref, x1_ref, dg0_ref, dg1_ref, du0_ref, du1_ref, gate_ref, up_ref):
    def write(left, right, out_ref):
        total = lax.dot_general(
            x0_ref[...], left[...], CONTRACT_ROWS, preferred_element_type=F32
        ) + lax.dot_general(x1_ref[...], right[...], CONTRACT_ROWS, preferred_element_type=F32)
        out_ref[...] = total.astype(BF16)

    pl.when(pl.program_id(0) == 0)(lambda: write(dg0_ref, dg1_ref, gate_ref))
    pl.when(pl.program_id(0) == 1)(lambda: write(du0_ref, du1_ref, up_ref))


def gate_up_grads(x, dg, du):
    rows, width = x[0].shape
    hid = dg[0].shape[1]
    cols = 512
    steps = width // cols
    x_spec = pl.BlockSpec((rows, cols), lambda o, i: (0, i))
    whole = pl.BlockSpec((rows, hid), lambda o, i: (0, 0))
    flat = jax.ShapeDtypeStruct((width, hid), BF16)
    return pl.pallas_call(
        gate_up_kernel,
        grid=(2, steps),
        in_specs=[x_spec] * 2 + [whole] * 4,
        out_specs=[
            pl.BlockSpec((cols, hid), lambda o, i: (jnp.where(o == 0, i, steps - 1), 0)),
            pl.BlockSpec((cols, hid), lambda o, i: (jnp.where(o == 0, 0, i), 0)),
        ],
        out_shape=[flat, flat],
        compiler_params=params(60),
        cost_estimate=cost(2 * 4 * rows * width * hid, 32, 0),
        name="gate_up_grads",
    )(*x, *dg, *du)


def collect_kernel(chunk, experts, ids_ref, back_ref, *refs):
    half = pl.program_id(0)
    tok = ids_ref.shape[1]
    lane = lax.broadcasted_iota(jnp.int32, (tok, experts * ROWS), 1)
    pick = jnp.zeros((tok, experts * ROWS), jnp.bool_)
    for slot in route_slots(ids_ref, experts, chunk):
        there = jnp.where(slot >= 0, slot + half * RANKS, -1)
        pick = pick | (lane == as_column(there))
    dx = (back_ref[:experts].astype(F32) + back_ref[experts:].astype(F32)).astype(BF16)
    dx = dx.reshape(experts * ROWS, dx.shape[2])
    total = jnp.dot(pick.astype(BF16), dx, preferred_element_type=F32)
    if len(refs) > 1:
        total = refs[0][...] + total
    refs[-1][...] = total.astype(refs[-1].dtype)


def collect(chunk, experts, ids, back, before=None):
    tok = ids.shape[1]
    peers, _, half = back.shape
    out = pl.BlockSpec((tok, half), lambda i: (0, i))
    more = () if before is None else (before,)
    return pl.pallas_call(
        lambda *refs: collect_kernel(chunk, experts, *refs),
        grid=(2,),
        in_specs=[
            pl.BlockSpec((2, tok), lambda i: (0, 0)),
            pl.BlockSpec((peers, ROWS, half), lambda i: (0, 0, 0)),
        ]
        + [out] * len(more),
        out_specs=out,
        out_shape=jax.ShapeDtypeStruct((tok, 2 * half), BF16 if more else F32),
        compiler_params=params(60),
        cost_estimate=cost(2 * 2 * tok * experts * ROWS * half, 4, 0),
        name="collect",
    )(ids, back, *more)


def exchange(rows):
    return lax.all_to_all(rows, PEERS, split_axis=0, concat_axis=0, tiled=True)


def other_core(rows):
    return lax.ppermute(rows, "core", [(0, 1), (1, 0)])


def shards(tokens, grad_out, gates, expert_ids, w_gate, w_up, w_down):
    experts = lax.axis_size(EXPERT)
    wg, wu, wd = w_gate[0], w_up[0], w_down[0]
    ids, scales = expert_ids.T, gates.T
    sends = [pack(chunk, experts, ids, scales, tokens, grad_out) for chunk in range(2)]
    got0, send1 = lax.optimization_barrier((exchange(sends[0]), sends[1]))
    got = [got0, exchange(send1)]
    x, dg, du, back, down, dx = [], [], [], [], None, None
    for chunk in range(2):
        rows = got[chunk]
        if chunk:
            rows, down, dx = lax.optimization_barrier((rows, down, dx))
        now = hidden_pass(other_core(rows), rows, wg, wu, wd)
        sent, dy, h = other_core(now[5]), now[1], now[2]
        if chunk:
            part = collect(0, experts, ids, back[0])
            dy, part = lax.optimization_barrier((dy, part))
        down = down_grad(dy, h, down)
        sent, down = lax.optimization_barrier((sent, down))
        dx = input_grad(now[3], now[4], wg, wu, sent)
        back.append(exchange(dx))
        for held, value in zip((x, dg, du), (now[0], now[3], now[4])):
            held.append(value)
    x[1], _ = lax.optimization_barrier((x[1], dx))
    grad_gate, grad_up = gate_up_grads(x, dg, du)
    grad_tokens = collect(1, experts, ids, back[1], part)
    return (grad_tokens, grad_gate[None], grad_up[None], down[None])


def solution(mesh):
    fine = Mesh(mesh.devices.reshape(2, 2, 4, 4, 2), DEVICE)
    per_token = P(DEVICE, None)
    columns = P(EXPERT, None, ("yhi", "core"))
    rows = P(EXPERT, ("yhi", "core"), None)
    return jax.shard_map(
        shards,
        mesh=fine,
        in_specs=(per_token,) * 4 + (columns, columns, rows),
        out_specs=(per_token, columns, columns, rows),
        check_vma=False,
    )
```

time: 670 us -> 241 us (0.36); the launches traced: 660 us -> 240 us
  waiting for transfers between devices: 237 us -> 61.1 us
  local copies, waits for them, and re-layouts: 163 us -> 3.98 us
  matrix products: 152 us -> 0 us
  Pallas kernels: 0 us -> 137 us
  other arithmetic: 54.4 us -> 0 us
  starting transfers between devices: 50.9 us -> 37.5 us
    all_to_all x4, waiting for transfers between devices: 237 us -> 61.1 us  [exchange(): return lax.all_to_all(rows, PEERS, split_axis=0, concat_axis=0, tiled=True)]
    dot_general x32 -> x0, matrix products: 152 us -> none  [the longest x4 38.7 us: block_terms(): lax.dot_general(hidden, dy_block, contract_rows, preferred_element_type=j...]
    pallas_call x0 -> x11, Pallas kernels: none -> 137 us  [the longest x2 55 us: hidden_pass(): pl.pallas_call(hidden_kernel, in_specs=[pl.BlockSpec(memory_space=pl.ANY)...]
    gather x12 -> x0, local copies, waits for them, and re-layouts: 114 us -> none  [the longest x1 20.8 us: expert_pass(): packed_dx[back_row]]
    select_n x9 -> x0, other arithmetic: 21.6 us -> none  [the longest x1 11.8 us: expert_pass(): jnp.where(within[:, None], sent_rows[source_row], jnp.zeros((), jnp.bfloa...]
    while x80 -> x0, local copies, waits for them, and re-layouts: 19.1 us -> none
    broadcast_in_dim x7 -> x0, local copies, waits for them, and re-layouts: 18 us -> none  [the longest x1 4.29 us: expert_pass(): start_dx = jnp.zeros((slot_count, model_width), jnp.bfloat16)]
    broadcast_in_dim x2 -> x0, other arithmetic: 16.6 us -> none  [the longest x1 10.5 us: shards(): totals[1].astype(jnp.bfloat16)[None]]
  transfers between devices with their start and end apart: 4 -> 8, of which waited for: 3 -> 4; matrix products, arithmetic and copies ran while one was open for 14% -> 0% of each run, Pallas kernels for 0% -> 49%
where the time goes in v2:
time: 241 us; the launch traced here: 240 us
  Pallas kernels  137 us (57%)
  waiting for transfers between devices  61.1 us (25%)
  starting transfers between devices  37.5 us (16%)
  local copies, waits for them, and re-layouts  3.98 us (2%)
    all_to_all x4, waiting for transfers between devices, exchange(): return lax.all_to_all(rows, PEERS, split_axis=0, concat_axis=0, tiled=True)  61.1 us
    pallas_call x2, Pallas kernels, hidden_pass(): pl.pallas_call(hidden_kernel, in_specs=[pl.BlockSpec(memory_space=pl.ANY)...  55 us
    all_to_all x4, starting transfers between devices, exchange(): return lax.all_to_all(rows, PEERS, split_axis=0, concat_axis=0, tiled=True)  36.8 us
    pallas_call x1, Pallas kernels, gate_up_grads(): pl.pallas_call(gate_up_kernel, grid=(2, steps), in_specs=[x_spec] * 2 + [...  24.8 us
    pallas_call x2, Pallas kernels, down_grad(): pl.pallas_call(down_grad_kernel, grid=(width // cols,), in_specs=[pl.Bloc...  19.3 us
    pallas_call x2, Pallas kernels, input_grad(): pl.pallas_call(input_grad_kernel, grid=(steps,), in_specs=[whole, whole,...  18.9 us
    pallas_call x2, Pallas kernels, pack(): pl.pallas_call(lambda *refs: pack_kernel(chunk, experts, *refs), grid=(wi...  11.2 us
    pallas_call x2, Pallas kernels, collect(): pl.pallas_call(lambda *refs: collect_kernel(chunk, experts, *refs), grid=...  7.44 us
  transfers between devices with their start and end apart: 8, of which 4 were waited for; matrix products, arithmetic and copies ran while one was open for 0% of the time, Pallas kernels for 49%

profile of v2, /device:TPU:0, one launch (start us, length us, event | category | flops | bytes accessed | tf_op | source)
XLA Modules:
  0.0 239.9 jit_solution(8967959183866344277)
XLA Ops:
  0.6 5.6 %pack.2 = bf16[64,16,2048]{2,1,0:T(8,128)(2,1)} custom-call(s32[2,128]{1,0:T(2,128)} %bitcast.23, f32[2,128]{1,0:T(2,128)} %bitcast.27, bf16[128,2048]{1,0:T(8,128)(2,1)} %refs_2_.3, bf16[128,2048]{1,0:T(8,128)(2,1)} %refs_3_.3), custom_call_target="tpu_custom_call" | custom-call | flops 100663296 | bytes 1572864 | tf_op jit(solution)/shard_map/pack/pallas_call | solution.py:77
  6.2 11.8 %all-to-all-start = ((bf16[64,16,2048]{2,1,0:T(8,128)(2,1)}), bf16[64,16,2048]{2,1,0:T(8,128)(2,1)}, u32[]{:S(2)}, u32[]{:S(2)}) async-start(bf16[64,16,2048]{2,1,0:T(8,128)(2,1)} %pack.2), calls=%async_computation | async-start | bytes 8388608 | tf_op jit(solution)/shard_map/all_to_all | solution.py:392
  18.0 5.6 %pack.3 = bf16[64,16,2048]{2,1,0:T(8,128)(2,1)} custom-call(s32[2,128]{1,0:T(2,128)} %bitcast.24, f32[2,128]{1,0:T(2,128)} %bitcast.28, bf16[128,2048]{1,0:T(8,128)(2,1)} %refs_2_.3, bf16[128,2048]{1,0:T(8,128)(2,1)} %refs_3_.3), custom_call_target="tpu_custom_call" | custom-call | flops 100663296 | bytes 1572864 | tf_op jit(solution)/shard_map/pack/pallas_call | solution.py:77
  23.6 47.6 %all-to-all-done.got1 = bf16[64,16,2048]{2,1,0:T(8,128)(2,1)} async-done(((bf16[64,16,2048]{2,1,0:T(8,128)(2,1)}), bf16[64,16,2048]{2,1,0:T(8,128)(2,1)}, u32[]{:S(2)}, u32[]{:S(2)}) %all-to-all-start) | async-done | bytes 4194336 | tf_op jit(solution)/shard_map/all_to_all | solution.py:392
  71.3 9.3 %all-to-all-start.1 = ((bf16[64,16,2048]{2,1,0:T(8,128)(2,1)}), bf16[64,16,2048]{2,1,0:T(8,128)(2,1)}, u32[]{:S(2)}, u32[]{:S(2)}) async-start(bf16[64,16,2048]{2,1,0:T(8,128)(2,1)} %pack.3), calls=%async_computation.1 | async-start | bytes 8388608 | tf_op jit(solution)/shard_map/all_to_all | solution.py:392
  80.6 27.5 %hidden.2 = (bf16[1024,2048]{1,0:T(8,128)(2,1)}, bf16[1024,2048]{1,0:T(8,128)(2,1)}, bf16[1024,1024]{1,0:T(8,128)(2,1)}, bf16[1024,1024]{1,0:T(8,128)(2,1)}, bf1...) custom-call(bf16[64,16,2048]{2,1,0:T(8,128)(2,1)} %collective-permute-done.got0, ...), custom_call_target="tpu_custom_call" | custom-call | flops 2147483648 | bytes 4718592 | tf_op jit(solution)/shard_map/hidden/pallas_call | solution.py:220
  108.1 0.3 collective-permute-start.1
  108.4 9.2 %down_grad.2.refs_0_ = f32[2048,1024]{1,0:T(8,128)} custom-call(bf16[1024,2048]{1,0:T(8,128)(2,1)} %get-tuple-element.32.dy_ref, bf16[1024,1024]{1,0:T(8,128)(2,1)} %get-tuple-element.33.h_ref), custom_call_target="tpu_custom_call" | custom-call | flops 536870912 | bytes 2621440 | tf_op jit(solution)/shard_map/down_grad/pallas_call | solution.py:302
  117.6 1.3 copy-done.2
  118.9 9.4 %input_grad.2 = bf16[64,16,1024]{2,1,0:T(8,128)(2,1)} custom-call(bf16[1024,1024]{1,0:T(8,128)(2,1)} %get-tuple-element.35.dg_ref.dg0_ref, bf16[1024,1024]{1,0:T(8,128)(2,1)} %get-tuple-element.36.du_ref.du0_ref, bf16[2048,1024]{1,0:T(8,128)(2,1)} %bitcast.9, bf16[2048,1024]{1,0:T(8,128)(2,1)} %bitcast.10, bf16[2048,1024]{1,0:T(8,128)(2,1)} %bitcast.15, ...), custom_call_target="tpu_custom_call" | custom-call | flops 536870912 | bytes 1835008 | tf_op jit(solution)/shard_map/input_grad/pallas_call | solution.py:277
  128.3 6.3 %all-to-all-done.1.got1 = bf16[64,16,2048]{2,1,0:T(8,128)(2,1)} async-done(((bf16[64,16,2048]{2,1,0:T(8,128)(2,1)}), bf16[64,16,2048]{2,1,0:T(8,128)(2,1)}, u32[]{:S(2)}, u32[]{:S(2)}) %all-to-all-start.1) | async-done | bytes 4194336 | tf_op jit(solution)/shard_map/all_to_all | solution.py:392
  134.7 7.7 %all-to-all-start.2 = ((bf16[64,16,1024]{2,1,0:T(8,128)(2,1)}), bf16[64,16,1024]{2,1,0:T(8,128)(2,1)S(1)}, u32[]{:S(2)}, u32[]{:S(2)}) async-start(bf16[64,16,1024]{2,1,0:T(8,128)(2,1)} %input_grad.2), calls=%async_computation.2 | async-start | bytes 4194304 | tf_op jit(solution)/shard_map/all_to_all | solution.py:392
  142.4 27.5 %hidden.3 = (bf16[1024,2048]{1,0:T(8,128)(2,1)}, bf16[1024,2048]{1,0:T(8,128)(2,1)}, bf16[1024,1024]{1,0:T(8,128)(2,1)}, bf16[1024,1024]{1,0:T(8,128)(2,1)}, bf1...) custom-call(bf16[64,16,2048]{2,1,0:T(8,128)(2,1)} %collective-permute-done.2.got0, ...), custom_call_target="tpu_custom_call" | custom-call | flops 2147483648 | bytes 4718592 | tf_op jit(solution)/shard_map/hidden/pallas_call | solution.py:220
  169.9 0.3 collective-permute-start.3
  170.2 2.0 all-to-all-done.2.refs_1_
  172.2 1.3 copy-done
  173.5 3.7 %collect.2.refs_2_ = f32[128,2048]{1,0:T(8,128)} custom-call(s32[2,128]{1,0:T(2,128)} %bitcast.25, bf16[64,16,1024]{2,1,0:T(8,128)(2,1)} %copy-done), custom_call_target="tpu_custom_call" | custom-call | flops 33554432 | bytes 524288 | tf_op jit(solution)/shard_map/collect/pallas_call | solution.py:375
  177.2 10.1 %down_grad.3 = bf16[1024,2048]{1,0:T(8,128)(2,1)} custom-call(bf16[1024,2048]{1,0:T(8,128)(2,1)} %get-tuple-element.43.dy_ref, bf16[1024,1024]{1,0:T(8,128)(2,1)} %get-tuple-element.44.h_ref, f32[2048,1024]{1,0:T(8,128)} %down_grad.2.refs_0_), custom_call_target="tpu_custom_call" | custom-call | flops 536870912 | bytes 2621440 | tf_op jit(solution)/shard_map/down_grad/pallas_call | solution.py:302
  187.3 9.4 %input_grad.3 = bf16[64,16,1024]{2,1,0:T(8,128)(2,1)} custom-call(bf16[1024,1024]{1,0:T(8,128)(2,1)} %get-tuple-element.39.dg_ref.dg1_ref, bf16[1024,1024]{1,0:T(8,128)(2,1)} %get-tuple-element.40.du_ref.du1_ref, bf16[2048,1024]{1,0:T(8,128)(2,1)} %bitcast.12, bf16[2048,1024]{1,0:T(8,128)(2,1)} %bitcast.13, bf16[2048,1024]{1,0:T(8,128)(2,1)} %bitcast.18, ...), custom_call_target="tpu_custom_call" | custom-call | flops 536870912 | bytes 1835008 | tf_op jit(solution)/shard_map/input_grad/pallas_call | solution.py:277
  196.8 8.1 %all-to-all-start.3 = ((bf16[64,16,1024]{2,1,0:T(8,128)(2,1)}), bf16[64,16,1024]{2,1,0:T(8,128)(2,1)S(1)}, u32[]{:S(2)}, u32[]{:S(2)}) async-start(bf16[64,16,1024]{2,1,0:T(8,128)(2,1)} %input_grad.3), calls=%async_computation.3 | async-start | bytes 4194304 | tf_op jit(solution)/shard_map/all_to_all | solution.py:392
  204.9 24.8 %gate_up_grads.1 = (bf16[2048,1024]{1,0:T(8,128)(2,1)}, bf16[2048,1024]{1,0:T(8,128)(2,1)}) custom-call(bf16[1024,2048]{1,0:T(8,128)(2,1)} %get-tuple-element.48.x0_ref, bf16[1024,2048]{1,0:T(8,128)(2,1)} %get-tuple-element.50.x1_ref, bf16[1024,1024]{1,0:T(8,128)(2,1)} %get-tuple-element.35.dg_ref.dg0_ref, ...), custom_call_target="tpu_custom_call" | custom-call | flops 2147483648 | bytes 4194304 | tf_op jit(solution)/shard_map/gate_up_grads/pallas_call | solution.py:339
  229.7 5.1 %all-to-all-done.3.refs_1_ = bf16[64,16,1024]{2,1,0:T(8,128)(2,1)S(1)} async-done(((bf16[64,16,1024]{2,1,0:T(8,128)(2,1)}), bf16[64,16,1024]{2,1,0:T(8,128)(2,1)S(1)}, u32[]{:S(2)}, u32[]{:S(2)}) %all-to-all-start.3) | async-done | bytes 2097184 | tf_op jit(solution)/shard_map/all_to_all | solution.py:392
  234.8 1.3 copy-done.1
  236.1 3.8 %collect.3 = bf16[128,2048]{1,0:T(8,128)(2,1)} custom-call(s32[2,128]{1,0:T(2,128)} %bitcast.26, bf16[64,16,1024]{2,1,0:T(8,128)(2,1)} %copy-done.1, f32[128,2048]{1,0:T(8,128)} %collect.2.refs_2_), custom_call_target="tpu_custom_call" | custom-call | flops 33554432 | bytes 524288 | tf_op jit(solution)/shard_map/collect/pallas_call | solution.py:375
  (9 shorter events, 0.0 us)
Async XLA Ops:
  6.2 65.0 %all-to-all-start = ((bf16[64,16,2048]{2,1,0:T(8,128)(2,1)}), bf16[64,16,2048]{2,1,0:T(8,128)(2,1)}, u32[]{:S(2)}, u32[]{:S(2)}) async-start(bf16[64,16,2048]{2,1,0:T(8,128)(2,1)} %pack.2), calls=%async_computation | async-start | bytes 8388608 | tf_op jit(solution)/shard_map/all_to_all | solution.py:392
  71.3 9.3 %collective-permute-start = (bf16[64,16,2048]{2,1,0:T(8,128)(2,1)}, bf16[64,16,2048]{2,1,0:T(8,128)(2,1)}, u32[]{:S(2)}, u32[]{:S(2)}) collective-permute-start(bf16[64,16,2048]{2,1,0:T(8,128)(2,1)} %all-to-all-done.got1), channel_id=1, source_target_pairs={{0,32},{32,0},{1,33},{33,1},{2,34},{34,2},{3,35},{35,3},{4,36},{36... | collective-permute-start | bytes 12582920 | tf_op jit(solution)/shard_map/ppermute | solution.py:396
  71.3 63.4 %all-to-all-start.1 = ((bf16[64,16,2048]{2,1,0:T(8,128)(2,1)}), bf16[64,16,2048]{2,1,0:T(8,128)(2,1)}, u32[]{:S(2)}, u32[]{:S(2)}) async-start(bf16[64,16,2048]{2,1,0:T(8,128)(2,1)} %pack.3), calls=%async_computation.1 | async-start | bytes 8388608 | tf_op jit(solution)/shard_map/all_to_all | solution.py:392
  108.1 9.5 %collective-permute-start.1 = (bf16[64,16,1024]{2,1,0:T(8,128)(2,1)}, bf16[64,16,1024]{2,1,0:T(8,128)(2,1)S(1)}, u32[]{:S(2)}, u32[]{:S(2)}) collective-permute-start(bf16[64,16,1024]{2,1,0:T(8,128)(2,1)} %get-tuple-element.31), channel_id=1, source_target_pairs={{0,32},{32,0},{1,33},{33,1},{2,34},{34,2},{3,35},{35,3},{4,36},{36... | collective-permute-start | bytes 6291464 | tf_op jit(solution)/shard_map/ppermute | solution.py:396
  117.6 1.3 copy-start.2
  134.7 7.7 %collective-permute-start.2 = (bf16[64,16,2048]{2,1,0:T(8,128)(2,1)}, bf16[64,16,2048]{2,1,0:T(8,128)(2,1)}, u32[]{:S(2)}, u32[]{:S(2)}) collective-permute-start(bf16[64,16,2048]{2,1,0:T(8,128)(2,1)} %all-to-all-done.1.got1), channel_id=1, source_target_pairs={{0,32},{32,0},{1,33},{33,1},{2,34},{34,2},{3,35},{35,3},{4,36},{36... | collective-permute-start | bytes 12582920 | tf_op jit(solution)/shard_map/ppermute | solution.py:396
  134.7 37.5 %all-to-all-start.2 = ((bf16[64,16,1024]{2,1,0:T(8,128)(2,1)}), bf16[64,16,1024]{2,1,0:T(8,128)(2,1)S(1)}, u32[]{:S(2)}, u32[]{:S(2)}) async-start(bf16[64,16,1024]{2,1,0:T(8,128)(2,1)} %input_grad.2), calls=%async_computation.2 | async-start | bytes 4194304 | tf_op jit(solution)/shard_map/all_to_all | solution.py:392
  169.9 17.4 %collective-permute-start.3 = (bf16[64,16,1024]{2,1,0:T(8,128)(2,1)}, bf16[64,16,1024]{2,1,0:T(8,128)(2,1)}, u32[]{:S(2)}, u32[]{:S(2)}) collective-permute-start(bf16[64,16,1024]{2,1,0:T(8,128)(2,1)} %get-tuple-element.41), channel_id=1, source_target_pairs={{0,32},{32,0},{1,33},{33,1},{2,34},{34,2},{3,35},{35,3},{4,36},{36... | collective-permute-start | bytes 6291464 | tf_op jit(solution)/shard_map/ppermute | solution.py:396
  172.2 1.3 copy-start
  196.8 38.0 %all-to-all-start.3 = ((bf16[64,16,1024]{2,1,0:T(8,128)(2,1)}), bf16[64,16,1024]{2,1,0:T(8,128)(2,1)S(1)}, u32[]{:S(2)}, u32[]{:S(2)}) async-start(bf16[64,16,1024]{2,1,0:T(8,128)(2,1)} %input_grad.3), calls=%async_computation.3 | async-start | bytes 4194304 | tf_op jit(solution)/shard_map/all_to_all | solution.py:392
  234.8 1.3 copy-start.1

commit v3 on v2

v3 whole, which is shorter than its diff:
```python
import jax
import jax.numpy as jnp
from jax import lax
from jax.experimental import pallas as pl
from jax.experimental.pallas import tpu as pltpu
from jax.sharding import Mesh, PartitionSpec as P

DEVICE = ("yhi", "core", "x", "z", "ylo")
EXPERT = ("x", "z", "ylo")
PEERS = ("yhi", "x", "z", "ylo")

BF16 = jnp.bfloat16
F32 = jnp.float32
RANKS = 8
ROWS = 2 * RANKS
MIB = 1024 * 1024

CONTRACT_LAST = (((1,), (1,)), ((), ()))
CONTRACT_ROWS = (((0,), (0,)), ((), ()))


def params(mib):
    return pltpu.CompilerParams(vmem_limit_bytes=mib * MIB)


def route_slots(ids_ref, experts, chunk):
    tok = ids_ref.shape[1]
    expert = lax.broadcasted_iota(jnp.int32, (experts, tok), 0)
    picks = [(ids_ref[k : k + 1, :] == expert).astype(F32) for k in range(2)]
    before = lax.broadcasted_iota(jnp.int32, (tok, tok), 0) < lax.broadcasted_iota(
        jnp.int32, (tok, tok), 1
    )
    ahead = jnp.dot(
        (picks[0] + picks[1]).astype(BF16), before.astype(BF16), preferred_element_type=F32
    )
    slots = []
    for k in range(2):
        rank = jnp.sum(ahead * picks[k], axis=0, keepdims=True).astype(jnp.int32) - chunk * RANKS
        inside = (rank >= 0) & (rank < RANKS)
        slots.append(jnp.where(inside, ids_ref[k : k + 1, :] * ROWS + rank, -1))
    return slots


def as_column(row):
    size = row.shape[1]
    same = lax.broadcasted_iota(jnp.int32, (size, size), 0) == lax.broadcasted_iota(
        jnp.int32, (size, size), 1
    )
    return jnp.sum(jnp.where(same, row, jnp.zeros_like(row)), axis=1, keepdims=True)


def pack_kernel(chunk, experts, ids_ref, gates_ref, tok_ref, grad_ref, out_ref, picks):
    tok = ids_ref.shape[1]

    @pl.when(pl.program_id(0) == 0)
    def _():
        slots = route_slots(ids_ref, experts, chunk)
        at = lax.broadcasted_iota(jnp.int32, (experts * ROWS, tok), 0)
        picks[0] = ((at == slots[0]) | (at == slots[1])).astype(BF16)
        for k in range(2):
            there = jnp.where(slots[k] >= 0, slots[k] + RANKS, -1)
            picks[1 + k] = (at == there).astype(BF16)

    packed = jnp.dot(picks[0], tok_ref[...], preferred_element_type=F32)
    for k in range(2):
        gate = as_column(gates_ref[k : k + 1, :])
        dy = (gate * grad_ref[...].astype(F32)).astype(BF16)
        packed = packed + jnp.dot(picks[1 + k], dy, preferred_element_type=F32)
    packed = packed.astype(BF16).reshape(experts, ROWS, packed.shape[1])
    out_ref[:experts] = packed
    out_ref[experts:] = packed


def pack(chunk, experts, ids, gates, tokens, grad_out):
    tok, width = tokens.shape
    cols = 512
    return pl.pallas_call(
        lambda *refs: pack_kernel(chunk, experts, *refs),
        grid=(width // cols,),
        in_specs=[
            pl.BlockSpec((2, tok), lambda i: (0, 0)),
            pl.BlockSpec((2, tok), lambda i: (0, 0)),
            pl.BlockSpec((tok, cols), lambda i: (0, i)),
            pl.BlockSpec((tok, cols), lambda i: (0, i)),
        ],
        out_specs=pl.BlockSpec((2 * experts, ROWS, cols), lambda i: (0, 0, i)),
        out_shape=jax.ShapeDtypeStruct((2 * experts, ROWS, width), BF16),
        scratch_shapes=[pltpu.VMEM((3, experts * ROWS, tok), BF16)],
        compiler_params=params(60),
        cost_estimate=cost(2 * 3 * tok * experts * ROWS * width, 12, 0),
        name="pack",
    )(ids, gates, tokens, grad_out)


def block(size, index):
    return pl.ds(index * size if isinstance(index, int) else pl.multiple_of(index * size, size), size)


def cost(flops, mib, transcendentals=0):
    return pl.CostEstimate(
        flops=flops // 8, bytes_accessed=mib * MIB // 8, transcendentals=transcendentals // 8
    )


def hidden_kernel(
    unit, out, got0, got1, wg, wu, wd, x, dy, h, dg, du, dx0, dx1,
    got_v0, got_v1, wg_v, wu_v, wd_v, x_v0, x_v1, dy_v0, dy_v1, h_v, dg_v, du_v, dx_v,
    got_sem, w_sem, row_sem, hid_sem, dx_sem,
):
    got, got_v = (got0, got1), (got_v0, got_v1)
    x_v, dy_v = (x_v0, x_v1), (dy_v0, dy_v1)
    peers, _, width = got0.shape
    hid = wg.shape[1]
    rows = peers * RANKS
    split = 512
    splits, units = width // split, hid // unit

    def got_copy(group, i):
        at = (slice(None), slice(None), block(split, i))
        return pltpu.make_async_copy(
            got[group].at[at], got_v[group].at[at], got_sem.at[group, i]
        )

    def w_copy(which, j):
        src, dst = ((wg, wg_v), (wu, wu_v), (wd, wd_v))[which]
        at = (block(unit, j), slice(None)) if which == 2 else (slice(None), block(unit, j))
        return pltpu.make_async_copy(src.at[at], dst.at[at], w_sem.at[which, j])

    def row_copies(group):
        at = (block(rows, group), slice(None))
        return [
            pltpu.make_async_copy(src[group], dst.at[at], row_sem.at[n, group])
            for n, (src, dst) in enumerate(((x_v, x), (dy_v, dy)))
        ]

    hid_copies = [
        pltpu.make_async_copy(src, dst, hid_sem.at[n])
        for n, (src, dst) in enumerate(((h_v, h), (dg_v, dg), (du_v, du)))
    ]
    dx_copies = [
        pltpu.make_async_copy(dx_v.at[block(peers, n)], (dx0, dx1)[n], dx_sem.at[n])
        for n in range(2)
    ]

    for i in range(splits):
        got_copy(0, i).start()
    for which in range(3):
        w_copy(which, 0).start()
    for i in range(splits):
        got_copy(1, i).start()
    for j in range(1, units):
        for which in range(3):
            w_copy(which, j).start()

    def split_rows(group, i):
        cols = block(split, i)
        both = got_v[group][:, :, cols].astype(F32)
        x_v[group][:, cols] = both[:, :RANKS].reshape(rows, split).astype(BF16)
        dy_v[group][:, cols] = both[:, RANKS:].reshape(rows, split).astype(BF16)

    @pl.loop(0, splits)
    def _(i):
        got_copy(0, i).wait()
        split_rows(0, i)

    for group in range(2):
        here = block(rows, group)

        @pl.loop(0, units)
        def _(j):
            if group == 0:
                for which in range(3):
                    w_copy(which, j).wait()
                for part in range(splits // units):
                    got_copy(1, j * (splits // units) + part).wait()
                for part in range(splits // units):
                    split_rows(1, j * (splits // units) + part)
            cols = block(unit, j)
            g = jnp.dot(x_v[group][...], wg_v[:, cols], preferred_element_type=F32)
            u = jnp.dot(x_v[group][...], wu_v[:, cols], preferred_element_type=F32)
            sig = jax.nn.sigmoid(g)
            silu = g * sig
            h_v[here, cols] = (silu * u).astype(BF16)
            slope = u * sig * (1.0 + g * (1.0 - sig))
            dh = lax.dot_general(
                dy_v[group][...], wd_v[cols, :], CONTRACT_LAST, preferred_element_type=F32
            )
            dg_v[here, cols] = (dh * slope).astype(BF16)
            du_v[here, cols] = (dh * silu).astype(BF16)

        for copy in row_copies(group):
            copy.start()
    for copy in hid_copies:
        copy.start()

    half = width // 2

    @pl.loop(0, half // out)
    def _(i):
        parts = []
        for side in range(2):
            at = block(out, side * (half // out) + i)
            part = lax.dot_general(
                dg_v[...], wg_v[at, :], CONTRACT_LAST, preferred_element_type=F32
            ) + lax.dot_general(du_v[...], wu_v[at, :], CONTRACT_LAST, preferred_element_type=F32)
            parts.append(part.reshape(2 * peers, RANKS, out))
        dx_v[:, :, block(out, i)] = jnp.concatenate(parts, axis=1).astype(BF16)

    for copy in dx_copies:
        copy.start()
    for copy in [c for group in range(2) for c in row_copies(group)] + hid_copies + dx_copies:
        copy.wait()


def hidden_pass(got0, got1, wg, wu, wd, unit=512, out=512):
    peers, _, width = got0.shape
    hid = wg.shape[1]
    rows = 2 * peers * RANKS
    splits, units = width // 512, hid // unit
    wide, narrow = (jax.ShapeDtypeStruct((rows, n), BF16) for n in (width, hid))
    dx = jax.ShapeDtypeStruct((peers, ROWS, width // 2), BF16)
    return pl.pallas_call(
        lambda *refs: hidden_kernel(unit, out, *refs),
        in_specs=[pl.BlockSpec(memory_space=pl.ANY)] * 5,
        out_specs=[pl.BlockSpec(memory_space=pl.ANY)] * 7,
        out_shape=[wide, wide, narrow, narrow, narrow, dx, dx],
        scratch_shapes=[
            pltpu.VMEM((peers, ROWS, width), BF16),
            pltpu.VMEM((peers, ROWS, width), BF16),
            pltpu.VMEM((width, hid), BF16),
            pltpu.VMEM((width, hid), BF16),
            pltpu.VMEM((hid, width), BF16),
            pltpu.VMEM((rows // 2, width), BF16),
            pltpu.VMEM((rows // 2, width), BF16),
            pltpu.VMEM((rows // 2, width), BF16),
            pltpu.VMEM((rows // 2, width), BF16),
            pltpu.VMEM((rows, hid), BF16),
            pltpu.VMEM((rows, hid), BF16),
            pltpu.VMEM((rows, hid), BF16),
            pltpu.VMEM((2 * peers, ROWS, width // 2), BF16),
            pltpu.SemaphoreType.DMA((2, splits)),
            pltpu.SemaphoreType.DMA((3, units)),
            pltpu.SemaphoreType.DMA((2, 2)),
            pltpu.SemaphoreType.DMA((3,)),
            pltpu.SemaphoreType.DMA((2,)),
        ],
        compiler_params=params(60),
        cost_estimate=cost(2 * 5 * rows * width * hid, 36, rows * hid),
        name="hidden",
    )(got0, got1, wg, wu, wd)


def add_kernel(a_ref, b_ref, out_ref):
    out_ref[...] = (a_ref[...].astype(F32) + b_ref[...].astype(F32)).astype(BF16)


def add(a, b):
    peers, rows, width = a.shape
    part = pl.BlockSpec((peers // 4, rows, width), lambda i: (i, 0, 0))
    return pl.pallas_call(
        add_kernel,
        grid=(4,),
        in_specs=[part, part],
        out_specs=part,
        out_shape=jax.ShapeDtypeStruct(a.shape, BF16),
        compiler_params=params(32),
        cost_estimate=cost(0, 6, 0),
        name="add",
    )(a, b)


def early_grads_kernel(x_ref, dy_ref, dg_ref, h_ref, gate_ref, down_ref):
    for left, right, out in ((x_ref, dg_ref, gate_ref), (dy_ref, h_ref, down_ref)):
        out[...] = lax.dot_general(
            left[...], right[...], CONTRACT_ROWS, preferred_element_type=F32
        )


def early_grads(x, dy, dg, h):
    rows, width = dy.shape
    hid = h.shape[1]
    cols = 512
    narrow = pl.BlockSpec((rows, cols), lambda i: (0, i))
    whole = pl.BlockSpec((rows, hid), lambda i: (0, 0))
    tall = pl.BlockSpec((cols, hid), lambda i: (i, 0))
    return pl.pallas_call(
        early_grads_kernel,
        grid=(width // cols,),
        in_specs=[narrow, narrow, whole, whole],
        out_specs=[tall, tall],
        out_shape=[jax.ShapeDtypeStruct((width, hid), F32)] * 2,
        compiler_params=params(60),
        cost_estimate=cost(2 * 2 * rows * width * hid, 28, 0),
        name="early_grads",
    )(x, dy, dg, h)


def weight_grads_kernel(
    x0_ref, x1_ref, dy_ref, gate0_ref, down0_ref, dg1, du0, du1, h1, gate_ref, up_ref, down_ref,
    dg1_v, du0_v, du1_v, h1_v, sem,
):
    whole = ((dg1, dg1_v), (du0, du0_v), (du1, du1_v), (h1, h1_v))
    copies = [pltpu.make_async_copy(src, dst, sem.at[n]) for n, (src, dst) in enumerate(whole)]
    first = pl.program_id(0) == 0

    @pl.when(first)
    def _():
        for copy in copies:
            copy.start()

    def arrived(*numbers):
        @pl.when(first)
        def _():
            for n in numbers:
                copies[n].wait()

    def term(left, right):
        return lax.dot_general(
            left[...], right[...], CONTRACT_ROWS, preferred_element_type=F32
        )

    arrived(0)
    gate_ref[...] = (gate0_ref[...] + term(x1_ref, dg1_v)).astype(BF16)
    arrived(1, 2)
    up_ref[...] = (term(x0_ref, du0_v) + term(x1_ref, du1_v)).astype(BF16)
    arrived(3)
    down_ref[...] = (down0_ref[...] + term(dy_ref, h1_v)).T.astype(BF16)


def weight_grads(x, du, dg1, dy1, h1, early):
    rows, width = dy1.shape
    hid = h1.shape[1]
    cols = 512
    narrow = pl.BlockSpec((rows, cols), lambda i: (0, i))
    tall = pl.BlockSpec((cols, hid), lambda i: (i, 0))
    flat = jax.ShapeDtypeStruct((width, hid), BF16)
    return pl.pallas_call(
        weight_grads_kernel,
        grid=(width // cols,),
        in_specs=[narrow] * 3 + [tall] * 2 + [pl.BlockSpec(memory_space=pl.ANY)] * 4,
        out_specs=[tall, tall, pl.BlockSpec((hid, cols), lambda i: (0, i))],
        out_shape=[flat, flat, jax.ShapeDtypeStruct((hid, width), BF16)],
        scratch_shapes=[pltpu.VMEM((rows, hid), BF16)] * 4 + [pltpu.SemaphoreType.DMA((4,))],
        compiler_params=params(60),
        cost_estimate=cost(2 * 4 * rows * width * hid, 48, 0),
        name="weight_grads",
    )(*x, dy1, *early, dg1, *du, h1)


def collect_kernel(chunk, experts, ids_ref, back_ref, *refs):
    half = pl.program_id(0)
    tok = ids_ref.shape[1]
    lane = lax.broadcasted_iota(jnp.int32, (tok, experts * ROWS), 1)
    pick = jnp.zeros((tok, experts * ROWS), jnp.bool_)
    for slot in route_slots(ids_ref, experts, chunk):
        there = jnp.where(slot >= 0, slot + half * RANKS, -1)
        pick = pick | (lane == as_column(there))
    dx = (back_ref[:experts].astype(F32) + back_ref[experts:].astype(F32)).astype(BF16)
    dx = dx.reshape(experts * ROWS, dx.shape[2])
    total = jnp.dot(pick.astype(BF16), dx, preferred_element_type=F32)
    if len(refs) > 1:
        total = refs[0][...] + total
    refs[-1][...] = total.astype(refs[-1].dtype)


def collect(chunk, experts, ids, back, before=None):
    tok = ids.shape[1]
    peers, _, half = back.shape
    out = pl.BlockSpec((tok, half), lambda i: (0, i))
    more = () if before is None else (before,)
    return pl.pallas_call(
        lambda *refs: collect_kernel(chunk, experts, *refs),
        grid=(2,),
        in_specs=[
            pl.BlockSpec((2, tok), lambda i: (0, 0)),
            pl.BlockSpec((peers, ROWS, half), lambda i: (0, 0, 0)),
        ]
        + [out] * len(more),
        out_specs=out,
        out_shape=jax.ShapeDtypeStruct((tok, 2 * half), BF16 if more else F32),
        compiler_params=params(24),
        cost_estimate=cost(2 * 2 * tok * experts * ROWS * half, 4, 0),
        name="collect",
    )(ids, back, *more)


def exchange(rows):
    return lax.all_to_all(rows, PEERS, split_axis=0, concat_axis=0, tiled=True)


def other_core(rows):
    return lax.ppermute(rows, "core", [(0, 1), (1, 0)])


def shards(tokens, grad_out, gates, expert_ids, w_gate, w_up, w_down):
    experts = lax.axis_size(EXPERT)
    wg, wu, wd = w_gate[0], w_up[0], w_down[0]
    ids, scales = expert_ids.T, gates.T
    sends = [pack(chunk, experts, ids, scales, tokens, grad_out) for chunk in range(2)]
    got0, send1 = lax.optimization_barrier((exchange(sends[0]), sends[1]))
    got = [got0, exchange(send1)]
    x, du, back = [], [], []
    for chunk in range(2):
        rows = got[chunk]
        if chunk:
            rows, early, dx = lax.optimization_barrier((rows, early, dx))
        now = hidden_pass(other_core(rows), rows, wg, wu, wd)
        x.append(now[0])
        du.append(now[4])
        theirs = now[5]
        if chunk:
            first, theirs = lax.optimization_barrier((back[0], theirs))
            part = collect(0, experts, ids, first)
        sent = other_core(theirs)
        if chunk:
            sent, part = lax.optimization_barrier((sent, part))
        else:
            early = early_grads(now[0], now[1], now[3], now[2])
            sent, early = lax.optimization_barrier((sent, early))
        dx = add(now[6], sent)
        back.append(exchange(dx))
    x[1], _ = lax.optimization_barrier((x[1], dx))
    grad_gate, grad_up, down = weight_grads(x, du, now[3], now[1], now[2], early)
    grad_tokens = collect(1, experts, ids, back[1], part)
    return (grad_tokens, grad_gate[None], grad_up[None], down[None])


def solution(mesh):
    fine = Mesh(mesh.devices.reshape(2, 2, 4, 4, 2), DEVICE)
    per_token = P(DEVICE, None)
    columns = P(EXPERT, None, ("yhi", "core"))
    rows = P(EXPERT, ("yhi", "core"), None)
    return jax.shard_map(
        shards,
        mesh=fine,
        in_specs=(per_token,) * 4 + (columns, columns, rows),
        out_specs=(per_token, columns, columns, rows),
        check_vma=False,
    )
```

time: 241 us -> 223 us (0.925)
  Pallas kernels: 137 us -> 124 us
  waiting for transfers between devices: 61.1 us -> 56.9 us
  local copies, waits for them, and re-layouts: 3.98 us -> 0.02 us
  starting transfers between devices: 37.5 us -> 40.3 us
    pallas_call x7 -> x6, Pallas kernels: 118 us -> 109 us  [the longest x2 62 us: hidden_pass(): pl.pallas_call(lambda *refs: hidden_kernel(unit, out, *refs), in_specs=[p...]
    all_to_all x4, waiting for transfers between devices: 61.1 us -> 54.1 us  [exchange(): return lax.all_to_all(rows, PEERS, split_axis=0, concat_axis=0, tiled=True)]
    pallas_call x2, Pallas kernels: 7.44 us -> 3.4 us  [collect(): pl.pallas_call(lambda *refs: collect_kernel(chunk, experts, *refs), grid=...]
    unnamed x6, local copies, waits for them, and re-layouts: 3.98 us -> 0.02 us
    all_to_all x4, starting transfers between devices: 36.8 us -> 39.7 us  [exchange(): return lax.all_to_all(rows, PEERS, split_axis=0, concat_axis=0, tiled=True)]
    ppermute x4, waiting for transfers between devices: 0.01 us -> 2.81 us  [other_core(): return lax.ppermute(rows, 'core', [(0, 1), (1, 0)])]
  transfers between devices with their start and end apart: 8 -> 8, of which waited for: 4 -> 4; matrix products, arithmetic and copies ran while one was open for 0% -> 0% of each run, Pallas kernels for 49% -> 51%
where the time goes in v3:
time: 223 us; the launch traced here: 222 us
  Pallas kernels  124 us (56%)
  waiting for transfers between devices  56.9 us (26%)
  starting transfers between devices  40.3 us (18%)
    pallas_call x2, Pallas kernels, hidden_pass(): pl.pallas_call(lambda *refs: hidden_kernel(unit, out, *refs), in_specs=[p...  62 us
    all_to_all x4, waiting for transfers between devices, exchange(): return lax.all_to_all(rows, PEERS, split_axis=0, concat_axis=0, tiled=True)  54.1 us
    all_to_all x4, starting transfers between devices, exchange(): return lax.all_to_all(rows, PEERS, split_axis=0, concat_axis=0, tiled=True)  39.7 us
    pallas_call x1, Pallas kernels, weight_grads(): pl.pallas_call(weight_grads_kernel, grid=(width // cols,), in_specs=[narr...  27.3 us
    pallas_call x1, Pallas kernels, early_grads(): pl.pallas_call(early_grads_kernel, grid=(width // cols,), in_specs=[narro...  14 us
    pallas_call x2, Pallas kernels, pack(): pl.pallas_call(lambda *refs: pack_kernel(chunk, experts, *refs), grid=(wi...  11.2 us
    pallas_call x2, Pallas kernels, add(): pl.pallas_call(add_kernel, grid=(4,), in_specs=[part, part], out_specs=pa...  6.01 us
  transfers between devices with their start and end apart: 8, of which 4 were waited for; matrix products, arithmetic and copies ran while one was open for 0% of the time, Pallas kernels for 51%

profile of v3, /device:TPU:0, one launch (start us, length us, event | category | flops | bytes accessed | tf_op | source)
XLA Modules:
  0.0 221.9 jit_solution(743167382502311380)
XLA Ops:
  0.6 5.6 %pack.2 = bf16[64,16,2048]{2,1,0:T(8,128)(2,1)} custom-call(s32[2,128]{1,0:T(2,128)} %bitcast.8, f32[2,128]{1,0:T(2,128)} %bitcast.18, bf16[128,2048]{1,0:T(8,128)(2,1)} %refs_2_.3, bf16[128,2048]{1,0:T(8,128)(2,1)} %refs_3_.3), custom_call_target="tpu_custom_call" | custom-call | flops 100663296 | bytes 1572864 | tf_op jit(solution)/shard_map/pack/pallas_call | solution.py:77
  6.2 11.8 %all-to-all-start = ((bf16[64,16,2048]{2,1,0:T(8,128)(2,1)}), bf16[64,16,2048]{2,1,0:T(8,128)(2,1)}, u32[]{:S(2)}, u32[]{:S(2)}) async-start(bf16[64,16,2048]{2,1,0:T(8,128)(2,1)} %pack.2), calls=%async_computation | async-start | bytes 8388608 | tf_op jit(solution)/shard_map/all_to_all | solution.py:388
  18.0 5.6 %pack.3 = bf16[64,16,2048]{2,1,0:T(8,128)(2,1)} custom-call(s32[2,128]{1,0:T(2,128)} %bitcast.9, f32[2,128]{1,0:T(2,128)} %bitcast.19, bf16[128,2048]{1,0:T(8,128)(2,1)} %refs_2_.3, bf16[128,2048]{1,0:T(8,128)(2,1)} %refs_3_.3), custom_call_target="tpu_custom_call" | custom-call | flops 100663296 | bytes 1572864 | tf_op jit(solution)/shard_map/pack/pallas_call | solution.py:77
  23.6 47.6 %all-to-all-done.refs_1_ = bf16[64,16,2048]{2,1,0:T(8,128)(2,1)} async-done(((bf16[64,16,2048]{2,1,0:T(8,128)(2,1)}), bf16[64,16,2048]{2,1,0:T(8,128)(2,1)}, u32[]{:S(2)}, u32[]{:S(2)}) %all-to-all-start) | async-done | bytes 4194336 | tf_op jit(solution)/shard_map/all_to_all | solution.py:388
  71.3 9.5 %all-to-all-start.1 = ((bf16[64,16,2048]{2,1,0:T(8,128)(2,1)}), bf16[64,16,2048]{2,1,0:T(8,128)(2,1)}, u32[]{:S(2)}, u32[]{:S(2)}) async-start(bf16[64,16,2048]{2,1,0:T(8,128)(2,1)} %pack.3), calls=%async_computation.1 | async-start | bytes 8388608 | tf_op jit(solution)/shard_map/all_to_all | solution.py:388
  80.7 0.0 collective-permute-done.refs_0_
  80.8 31.0 %hidden.2 = (bf16[1024,2048]{1,0:T(8,128)(2,1)}, bf16[1024,2048]{1,0:T(8,128)(2,1)}, bf16[1024,1024]{1,0:T(8,128)(2,1)}, bf16[1024,1024]{1,0:T(8,128)(2,1)}, bf1...) custom-call(bf16[64,16,2048]{2,1,0:T(8,128)(2,1)} %collective-permute-done.refs_0_, ...), custom_call_target="tpu_custom_call" | custom-call | flops 2684354560 | bytes 4718592 | tf_op jit(solution)/shard_map/hidden/pallas_call | solution.py:222
  111.8 0.3 collective-permute-start.1
  112.1 14.0 %early_grads.1 = (f32[2048,1024]{1,0:T(8,128)}, f32[2048,1024]{1,0:T(8,128)}) custom-call(bf16[1024,2048]{1,0:T(8,128)(2,1)} %get-tuple-element.39.x_ref.x0_ref, bf16[1024,2048]{1,0:T(8,128)(2,1)} %get-tuple-element.40.dy_ref, bf16[1024,1024]{1,0:T(8,128)(2,1)} %get-tuple-element.41.dg_ref, bf16[1024,1024]{1,0:T(8,128)(2,1)} %get-tuple-element.42.h_ref), custom_call_target="tpu_custom_call" | custom-call | flops 1073741824 | bytes 3670016 | tf_op jit(solution)/shard_map/early_grads/pallas_call | solution.py:286
  126.1 0.0 collective-permute-done.1.b_ref
  126.1 4.0 %add.2 = bf16[64,16,1024]{2,1,0:T(8,128)(2,1)} custom-call(bf16[64,16,1024]{2,1,0:T(8,128)(2,1)S(1)} %copy-done.1, bf16[64,16,1024]{2,1,0:T(8,128)(2,1)} %collective-permute-done.1.b_ref), custom_call_target="tpu_custom_call" | custom-call | bytes 786432 | tf_op jit(solution)/shard_map/add/pallas_call | solution.py:260
  130.1 4.6 %all-to-all-done.1.refs_1_ = bf16[64,16,2048]{2,1,0:T(8,128)(2,1)} async-done(((bf16[64,16,2048]{2,1,0:T(8,128)(2,1)}), bf16[64,16,2048]{2,1,0:T(8,128)(2,1)}, u32[]{:S(2)}, u32[]{:S(2)}) %all-to-all-start.1) | async-done | bytes 4194336 | tf_op jit(solution)/shard_map/all_to_all | solution.py:388
  134.7 8.0 %all-to-all-start.2 = ((bf16[64,16,1024]{2,1,0:T(8,128)(2,1)}), bf16[64,16,1024]{2,1,0:T(8,128)(2,1)S(1)}, u32[]{:S(2)}, u32[]{:S(2)}) async-start(bf16[64,16,1024]{2,1,0:T(8,128)(2,1)} %add.2), calls=%async_computation.2 | async-start | bytes 4194304 | tf_op jit(solution)/shard_map/all_to_all | solution.py:388
  142.7 0.0 copy-start.2
  142.7 30.9 %hidden.3 = (bf16[1024,2048]{1,0:T(8,128)(2,1)}, bf16[1024,2048]{1,0:T(8,128)(2,1)}, bf16[1024,1024]{1,0:T(8,128)(2,1)}, bf16[1024,1024]{1,0:T(8,128)(2,1)}, bf1...) custom-call(bf16[64,16,2048]{2,1,0:T(8,128)(2,1)} %collective-permute-done.2.refs_0_, ...), custom_call_target="tpu_custom_call" | custom-call | flops 2684354560 | bytes 4718592 | tf_op jit(solution)/shard_map/hidden/pallas_call | solution.py:222
  173.6 0.0 copy-start
  173.7 0.3 collective-permute-start.3
  174.0 1.3 collect.2.refs_2_
  175.3 2.8 %collective-permute-done.3.b_ref = bf16[64,16,1024]{2,1,0:T(8,128)(2,1)S(1)} collective-permute-done((bf16[64,16,1024]{2,1,0:T(8,128)(2,1)}, bf16[64,16,1024]{2,1,0:T(8,128)(2,1)S(1)}, u32[]{:S(2)}, u32[]{:S(2)}) %collective-permute-start.3) | collective-permute-done | bytes 2097184 | tf_op jit(solution)/shard_map/ppermute | solution.py:392
  178.1 2.1 add.3
  180.2 10.5 %all-to-all-start.3 = ((bf16[64,16,1024]{2,1,0:T(8,128)(2,1)}), bf16[64,16,1024]{2,1,0:T(8,128)(2,1)S(1)}, u32[]{:S(2)}, u32[]{:S(2)}) async-start(bf16[64,16,1024]{2,1,0:T(8,128)(2,1)} %add.3), calls=%async_computation.3 | async-start | bytes 4194304 | tf_op jit(solution)/shard_map/all_to_all | solution.py:388
  190.6 27.3 %weight_grads.1 = (bf16[2048,1024]{1,0:T(8,128)(2,1)}, bf16[2048,1024]{1,0:T(8,128)(2,1)}, bf16[1024,2048]{1,0:T(8,128)(2,1)}) custom-call(bf16[1024,2048]{1,0:T(8,128)(2,1)} %get-tuple-element.39.x_ref.x0_ref, bf16[1024,2048]{1,0:T(8,128)(2,1)} %get-tuple-element.57.x1_ref, bf16[1024,2048]{1,0:T(8,128)(2,1)} %get-tuple-element.58.dy_ref, ...), custom_call_target="tpu_custom_call" | custom-call | flops 2147483648 | bytes 6291456 | tf_op jit(solution)/shard_map/weight_grads/pallas_call | solution.py:337
  217.9 1.9 all-to-all-done.3.refs_1_
  219.8 2.1 collect.3
  (8 shorter events, 0.0 us)
Async XLA Ops:
  6.2 65.0 %all-to-all-start = ((bf16[64,16,2048]{2,1,0:T(8,128)(2,1)}), bf16[64,16,2048]{2,1,0:T(8,128)(2,1)}, u32[]{:S(2)}, u32[]{:S(2)}) async-start(bf16[64,16,2048]{2,1,0:T(8,128)(2,1)} %pack.2), calls=%async_computation | async-start | bytes 8388608 | tf_op jit(solution)/shard_map/all_to_all | solution.py:388
  71.3 9.5 %collective-permute-start = (bf16[64,16,2048]{2,1,0:T(8,128)(2,1)}, bf16[64,16,2048]{2,1,0:T(8,128)(2,1)}, u32[]{:S(2)}, u32[]{:S(2)}) collective-permute-start(bf16[64,16,2048]{2,1,0:T(8,128)(2,1)} %all-to-all-done.refs_1_), channel_id=1, source_target_pairs={{0,32},{32,0},{1,33},{33,1},{2,34},{34,2},{3,35},{35,3},{4,36},{36... | collective-permute-start | bytes 12582920 | tf_op jit(solution)/shard_map/ppermute | solution.py:392
  71.3 63.4 %all-to-all-start.1 = ((bf16[64,16,2048]{2,1,0:T(8,128)(2,1)}), bf16[64,16,2048]{2,1,0:T(8,128)(2,1)}, u32[]{:S(2)}, u32[]{:S(2)}) async-start(bf16[64,16,2048]{2,1,0:T(8,128)(2,1)} %pack.3), calls=%async_computation.1 | async-start | bytes 8388608 | tf_op jit(solution)/shard_map/all_to_all | solution.py:388
  111.8 14.3 %collective-permute-start.1 = (bf16[64,16,1024]{2,1,0:T(8,128)(2,1)}, bf16[64,16,1024]{2,1,0:T(8,128)(2,1)}, u32[]{:S(2)}, u32[]{:S(2)}) collective-permute-start(bf16[64,16,1024]{2,1,0:T(8,128)(2,1)} %get-tuple-element.38), channel_id=1, source_target_pairs={{0,32},{32,0},{1,33},{33,1},{2,34},{34,2},{3,35},{35,3},{4,36},{36... | collective-permute-start | bytes 6291464 | tf_op jit(solution)/shard_map/ppermute | solution.py:392
  112.1 14.0 %copy-start.1 = (bf16[64,16,1024]{2,1,0:T(8,128)(2,1)S(1)}, bf16[64,16,1024]{2,1,0:T(8,128)(2,1)}, u32[]{:S(2)}) copy-start(bf16[64,16,1024]{2,1,0:T(8,128)(2,1)} %get-tuple-element.47.a_ref) | copy-start | bytes 6291460
  134.7 8.0 %collective-permute-start.2 = (bf16[64,16,2048]{2,1,0:T(8,128)(2,1)}, bf16[64,16,2048]{2,1,0:T(8,128)(2,1)}, u32[]{:S(2)}, u32[]{:S(2)}) collective-permute-start(bf16[64,16,2048]{2,1,0:T(8,128)(2,1)} %all-to-all-done.1.refs_1_), channel_id=1, source_target_pairs={{0,32},{32,0},{1,33},{33,1},{2,34},{34,2},{3,35},{35,3},{4,36},{36... | collective-permute-start | bytes 12582920 | tf_op jit(solution)/shard_map/ppermute | solution.py:392
  134.7 39.0 %all-to-all-start.2 = ((bf16[64,16,1024]{2,1,0:T(8,128)(2,1)}), bf16[64,16,1024]{2,1,0:T(8,128)(2,1)S(1)}, u32[]{:S(2)}, u32[]{:S(2)}) async-start(bf16[64,16,1024]{2,1,0:T(8,128)(2,1)} %add.2), calls=%async_computation.2 | async-start | bytes 4194304 | tf_op jit(solution)/shard_map/all_to_all | solution.py:388
  142.7 31.3 %copy-start.2 = (s32[128,2]{0,1:T(2,128)S(1)}, s32[128,2]{0,1:T(2,128)}, u32[]{:S(2)}) copy-start(s32[128,2]{0,1:T(2,128)} %param.10) | copy-start | bytes 3076
  173.6 4.5 %copy-start = (bf16[64,16,1024]{2,1,0:T(8,128)(2,1)S(1)}, bf16[64,16,1024]{2,1,0:T(8,128)(2,1)}, u32[]{:S(2)}) copy-start(bf16[64,16,1024]{2,1,0:T(8,128)(2,1)} %get-tuple-element.50.a_ref) | copy-start | bytes 6291460
  173.7 4.5 %collective-permute-start.3 = (bf16[64,16,1024]{2,1,0:T(8,128)(2,1)}, bf16[64,16,1024]{2,1,0:T(8,128)(2,1)S(1)}, u32[]{:S(2)}, u32[]{:S(2)}) collective-permute-start(bf16[64,16,1024]{2,1,0:T(8,128)(2,1)} %get-tuple-element.52), channel_id=1, source_target_pairs={{0,32},{32,0},{1,33},{33,1},{2,34},{34,2},{3,35},{35,3},{4,36},{36... | collective-permute-start | bytes 6291464 | tf_op jit(solution)/shard_map/ppermute | solution.py:392
  180.2 39.6 %all-to-all-start.3 = ((bf16[64,16,1024]{2,1,0:T(8,128)(2,1)}), bf16[64,16,1024]{2,1,0:T(8,128)(2,1)S(1)}, u32[]{:S(2)}, u32[]{:S(2)}) async-start(bf16[64,16,1024]{2,1,0:T(8,128)(2,1)} %add.3), calls=%async_computation.3 | async-start | bytes 4194304 | tf_op jit(solution)/shard_map/all_to_all | solution.py:388

commit v4 on v3

--- a/solution.py
+++ b/solution.py
@@ -49,7 +49,7 @@
     return jnp.sum(jnp.where(same, row, jnp.zeros_like(row)), axis=1, keepdims=True)
 
 
-def pack_kernel(chunk, experts, ids_ref, gates_ref, tok_ref, grad_ref, out_ref, picks):
+def pack_kernel(chunk, experts, ids_ref, gates_ref, tok_ref, grad_ref, out_ref, picks, gates):
     tok = ids_ref.shape[1]
 
     @pl.when(pl.program_id(0) == 0)
@@ -60,20 +60,19 @@
         for k in range(2):
             there = jnp.where(slots[k] >= 0, slots[k] + RANKS, -1)
             picks[1 + k] = (at == there).astype(BF16)
+            gates[k] = as_column(gates_ref[k : k + 1, :])
 
     packed = jnp.dot(picks[0], tok_ref[...], preferred_element_type=F32)
     for k in range(2):
-        gate = as_column(gates_ref[k : k + 1, :])
-        dy = (gate * grad_ref[...].astype(F32)).astype(BF16)
+        dy = (gates[k] * grad_ref[...].astype(F32)).astype(BF16)
         packed = packed + jnp.dot(picks[1 + k], dy, preferred_element_type=F32)
     packed = packed.astype(BF16).reshape(experts, ROWS, packed.shape[1])
     out_ref[:experts] = packed
     out_ref[experts:] = packed
 
 
-def pack(chunk, experts, ids, gates, tokens, grad_out):
+def pack(chunk, experts, ids, gates, tokens, grad_out, cols=1024):
     tok, width = tokens.shape
-    cols = 512
     return pl.pallas_call(
         lambda *refs: pack_kernel(chunk, experts, *refs),
         grid=(width // cols,),
@@ -85,7 +84,10 @@
         ],
         out_specs=pl.BlockSpec((2 * experts, ROWS, cols), lambda i: (0, 0, i)),
         out_shape=jax.ShapeDtypeStruct((2 * experts, ROWS, width), BF16),
-        scratch_shapes=[pltpu.VMEM((3, experts * ROWS, tok), BF16)],
+        scratch_shapes=[
+            pltpu.VMEM((3, experts * ROWS, tok), BF16),
+            pltpu.VMEM((2, tok, 1), F32),
+        ],
         compiler_params=params(60),
         cost_estimate=cost(2 * 3 * tok * experts * ROWS * width, 12, 0),
         name="pack",
@@ -103,7 +105,7 @@
 
 
 def hidden_kernel(
-    unit, out, got0, got1, wg, wu, wd, x, dy, h, dg, du, dx0, dx1,
+    got0, got1, wg, wu, wd, x, dy, h, dg, du, dx0, dx1,
     got_v0, got_v1, wg_v, wu_v, wd_v, x_v0, x_v1, dy_v0, dy_v1, h_v, dg_v, du_v, dx_v,
     got_sem, w_sem, row_sem, hid_sem, dx_sem,
 ):
@@ -112,7 +114,7 @@
     peers, _, width = got0.shape
     hid = wg.shape[1]
     rows = peers * RANKS
-    split = 512
+    split, out, unit = 512, 512, 256
     splits, units = width // split, hid // unit
 
     def got_copy(group, i):
@@ -133,22 +135,28 @@
             for n, (src, dst) in enumerate(((x_v, x), (dy_v, dy)))
         ]
 
-    hid_copies = [
-        pltpu.make_async_copy(src, dst, hid_sem.at[n])
-        for n, (src, dst) in enumerate(((h_v, h), (dg_v, dg), (du_v, du)))
-    ]
-    dx_copies = [
-        pltpu.make_async_copy(dx_v.at[block(peers, n)], (dx0, dx1)[n], dx_sem.at[n])
-        for n in range(2)
-    ]
+    def hid_copies(group):
+        at = (block(rows, group), slice(None))
+        return [
+            pltpu.make_async_copy(src.at[at], dst.at[at], hid_sem.at[n, group])
+            for n, (src, dst) in enumerate(((h_v, h), (dg_v, dg), (du_v, du)))
+        ]
+
+    def dx_copies(i):
+        cols = block(out, i)
+        return [
+            pltpu.make_async_copy(
+                dx_v.at[block(peers, n), :, cols], dx.at[:, :, cols], dx_sem.at[n, i]
+            )
+            for n, dx in enumerate((dx0, dx1))
+        ]
 
     for i in range(splits):
         got_copy(0, i).start()
-    for which in range(3):
-        w_copy(which, 0).start()
-    for i in range(splits):
-        got_copy(1, i).start()
-    for j in range(1, units):
+    for j in range(units):
+        if j == 2:
+            for i in range(splits):
+                got_copy(1, i).start()
         for which in range(3):
             w_copy(which, j).start()
 
@@ -163,19 +171,17 @@
         got_copy(0, i).wait()
         split_rows(0, i)
 
+    wide = 2 * unit
     for group in range(2):
         here = block(rows, group)
 
-        @pl.loop(0, units)
+        @pl.loop(0, hid // wide)
         def _(j):
             if group == 0:
-                for which in range(3):
-                    w_copy(which, j).wait()
-                for part in range(splits // units):
-                    got_copy(1, j * (splits // units) + part).wait()
-                for part in range(splits // units):
-                    split_rows(1, j * (splits // units) + part)
-            cols = block(unit, j)
+                for part in range(2):
+                    for which in range(3):
+                        w_copy(which, 2 * j + part).wait()
+            cols = block(wide, j)
             g = jnp.dot(x_v[group][...], wg_v[:, cols], preferred_element_type=F32)
             u = jnp.dot(x_v[group][...], wu_v[:, cols], preferred_element_type=F32)
             sig = jax.nn.sigmoid(g)
@@ -188,10 +194,14 @@
             dg_v[here, cols] = (dh * slope).astype(BF16)
             du_v[here, cols] = (dh * silu).astype(BF16)
 
-        for copy in row_copies(group):
+        for copy in row_copies(group) + hid_copies(group):
             copy.start()
-    for copy in hid_copies:
-        copy.start()
+        if group == 0:
+
+            @pl.loop(0, splits)
+            def _(i):
+                got_copy(1, i).wait()
+                split_rows(1, i)
 
     half = width // 2
 
@@ -205,22 +215,24 @@
             ) + lax.dot_general(du_v[...], wu_v[at, :], CONTRACT_LAST, preferred_element_type=F32)
             parts.append(part.reshape(2 * peers, RANKS, out))
         dx_v[:, :, block(out, i)] = jnp.concatenate(parts, axis=1).astype(BF16)
-
-    for copy in dx_copies:
-        copy.start()
-    for copy in [c for group in range(2) for c in row_copies(group)] + hid_copies + dx_copies:
+        for copy in dx_copies(i):
+            copy.start()
+
+    for copy in [c for group in range(2) for c in row_copies(group) + hid_copies(group)]:
         copy.wait()
-
-
-def hidden_pass(got0, got1, wg, wu, wd, unit=512, out=512):
+    for copy in [c for i in range(half // out) for c in dx_copies(i)]:
+        copy.wait()
+
+
+def hidden_pass(got0, got1, wg, wu, wd):
     peers, _, width = got0.shape
     hid = wg.shape[1]
     rows = 2 * peers * RANKS
-    splits, units = width // 512, hid // unit
+    splits, units = width // 512, hid // 256
     wide, narrow = (jax.ShapeDtypeStruct((rows, n), BF16) for n in (width, hid))
     dx = jax.ShapeDtypeStruct((peers, ROWS, width // 2), BF16)
     return pl.pallas_call(
-        lambda *refs: hidden_kernel(unit, out, *refs),
+        hidden_kernel,
         in_specs=[pl.BlockSpec(memory_space=pl.ANY)] * 5,
         out_specs=[pl.BlockSpec(memory_space=pl.ANY)] * 7,
         out_shape=[wide, wide, narrow, narrow, narrow, dx, dx],
@@ -241,8 +253,8 @@
             pltpu.SemaphoreType.DMA((2, splits)),
             pltpu.SemaphoreType.DMA((3, units)),
             pltpu.SemaphoreType.DMA((2, 2)),
-            pltpu.SemaphoreType.DMA((3,)),
-            pltpu.SemaphoreType.DMA((2,)),
+            pltpu.SemaphoreType.DMA((3, 2)),
+            pltpu.SemaphoreType.DMA((2, width // 1024)),
         ],
         compiler_params=params(60),
         cost_estimate=cost(2 * 5 * rows * width * hid, 36, rows * hid),
@@ -250,19 +262,26 @@
     )(got0, got1, wg, wu, wd)
 
 
-def add_kernel(a_ref, b_ref, out_ref):
-    out_ref[...] = (a_ref[...].astype(F32) + b_ref[...].astype(F32)).astype(BF16)
+def add_kernel(a_ref, b_ref, out_ref, sums, sem):
+    parts = sem.shape[0]
+    size = sums.shape[0] // parts
+    copies = []
+    for n in range(parts):
+        at = block(size, n)
+        sums[at] = (a_ref[at].astype(F32) + b_ref[at].astype(F32)).astype(BF16)
+        copies.append(pltpu.make_async_copy(sums.at[at], out_ref.at[at], sem.at[n]))
+        copies[-1].start()
+    for copy in copies:
+        copy.wait()
 
 
 def add(a, b):
-    peers, rows, width = a.shape
-    part = pl.BlockSpec((peers // 4, rows, width), lambda i: (i, 0, 0))
     return pl.pallas_call(
         add_kernel,
-        grid=(4,),
-        in_specs=[part, part],
-        out_specs=part,
+        in_specs=[pl.BlockSpec(memory_space=pltpu.VMEM)] * 2,
+        out_specs=pl.BlockSpec(memory_space=pl.ANY),
         out_shape=jax.ShapeDtypeStruct(a.shape, BF16),
+        scratch_shapes=[pltpu.VMEM(a.shape, BF16), pltpu.SemaphoreType.DMA((4,))],
         compiler_params=params(32),
         cost_estimate=cost(0, 6, 0),
         name="add",

time: 223 us -> 220 us (0.987)
  Pallas kernels: 124 us -> 119 us
  waiting for transfers between devices: 56.9 us -> 59.3 us
    pallas_call x4, Pallas kernels: 68 us -> 65.1 us  [the longest x2 60.6 us: hidden_pass(): pl.pallas_call(hidden_kernel, in_specs=[pl.BlockSpec(memory_space=pl.ANY)...]
    all_to_all x4, waiting for transfers between devices: 54.1 us -> 56.5 us  [exchange(): return lax.all_to_all(rows, PEERS, split_axis=0, concat_axis=0, tiled=True)]
where the time goes in v4:
time: 220 us
  Pallas kernels  119 us (54%)
  waiting for transfers between devices  59.3 us (27%)
  starting transfers between devices  40.3 us (18%)
    pallas_call x2, Pallas kernels, hidden_pass(): pl.pallas_call(hidden_kernel, in_specs=[pl.BlockSpec(memory_space=pl.ANY)...  60.6 us
    all_to_all x4, waiting for transfers between devices, exchange(): return lax.all_to_all(rows, PEERS, split_axis=0, concat_axis=0, tiled=True)  56.5 us
    all_to_all x4, starting transfers between devices, exchange(): return lax.all_to_all(rows, PEERS, split_axis=0, concat_axis=0, tiled=True)  39.7 us
    pallas_call x1, Pallas kernels, weight_grads(): pl.pallas_call(weight_grads_kernel, grid=(width // cols,), in_specs=[narr...  27.3 us
    pallas_call x1, Pallas kernels, early_grads(): pl.pallas_call(early_grads_kernel, grid=(width // cols,), in_specs=[narro...  14 us
    pallas_call x2, Pallas kernels, pack(): pl.pallas_call(lambda *refs: pack_kernel(chunk, experts, *refs), grid=(wi...  9.69 us
    pallas_call x2, Pallas kernels, add(): pl.pallas_call(add_kernel, in_specs=[pl.BlockSpec(memory_space=pltpu.VMEM...  4.55 us
  transfers between devices with their start and end apart: 8, of which 4 were waited for; matrix products, arithmetic and copies ran while one was open for 0% of the time, Pallas kernels for 51%

profile of v4, /device:TPU:0, one launch (start us, length us, event | category | flops | bytes accessed | tf_op | source)
XLA Modules:
  0.0 219.9 jit_solution(14729473488870046818)
XLA Ops:
  0.6 4.8 %pack.2 = bf16[64,16,2048]{2,1,0:T(8,128)(2,1)} custom-call(s32[2,128]{1,0:T(2,128)} %bitcast.8, f32[2,128]{1,0:T(2,128)} %bitcast.18, bf16[128,2048]{1,0:T(8,128)(2,1)} %refs_2_.3, bf16[128,2048]{1,0:T(8,128)(2,1)} %refs_3_.3), custom_call_target="tpu_custom_call" | custom-call | flops 100663296 | bytes 1572864 | tf_op jit(solution)/shard_map/pack/pallas_call | solution.py:76
  5.5 11.8 %all-to-all-start = ((bf16[64,16,2048]{2,1,0:T(8,128)(2,1)}), bf16[64,16,2048]{2,1,0:T(8,128)(2,1)}, u32[]{:S(2)}, u32[]{:S(2)}) async-start(bf16[64,16,2048]{2,1,0:T(8,128)(2,1)} %pack.2), calls=%async_computation | async-start | bytes 8388608 | tf_op jit(solution)/shard_map/all_to_all | solution.py:407
  17.2 4.8 %pack.3 = bf16[64,16,2048]{2,1,0:T(8,128)(2,1)} custom-call(s32[2,128]{1,0:T(2,128)} %bitcast.9, f32[2,128]{1,0:T(2,128)} %bitcast.19, bf16[128,2048]{1,0:T(8,128)(2,1)} %refs_2_.3, bf16[128,2048]{1,0:T(8,128)(2,1)} %refs_3_.3), custom_call_target="tpu_custom_call" | custom-call | flops 100663296 | bytes 1572864 | tf_op jit(solution)/shard_map/pack/pallas_call | solution.py:76
  22.1 48.4 %all-to-all-done.got1 = bf16[64,16,2048]{2,1,0:T(8,128)(2,1)} async-done(((bf16[64,16,2048]{2,1,0:T(8,128)(2,1)}), bf16[64,16,2048]{2,1,0:T(8,128)(2,1)}, u32[]{:S(2)}, u32[]{:S(2)}) %all-to-all-start) | async-done | bytes 4194336 | tf_op jit(solution)/shard_map/all_to_all | solution.py:407
  70.5 0.0 collective-permute-start
  70.5 9.5 %all-to-all-start.1 = ((bf16[64,16,2048]{2,1,0:T(8,128)(2,1)}), bf16[64,16,2048]{2,1,0:T(8,128)(2,1)}, u32[]{:S(2)}, u32[]{:S(2)}) async-start(bf16[64,16,2048]{2,1,0:T(8,128)(2,1)} %pack.3), calls=%async_computation.1 | async-start | bytes 8388608 | tf_op jit(solution)/shard_map/all_to_all | solution.py:407
  80.0 0.0 collective-permute-done.got0
  80.0 30.3 %hidden.2 = (bf16[1024,2048]{1,0:T(8,128)(2,1)}, bf16[1024,2048]{1,0:T(8,128)(2,1)}, bf16[1024,1024]{1,0:T(8,128)(2,1)}, bf16[1024,1024]{1,0:T(8,128)(2,1)}, bf1...) custom-call(bf16[64,16,2048]{2,1,0:T(8,128)(2,1)} %collective-permute-done.got0, ...), custom_call_target="tpu_custom_call" | custom-call | flops 2684354560 | bytes 4718592 | tf_op jit(solution)/shard_map/hidden/pallas_call | solution.py:234
  110.4 0.3 collective-permute-start.1
  110.7 14.0 %early_grads.1 = (f32[2048,1024]{1,0:T(8,128)}, f32[2048,1024]{1,0:T(8,128)}) custom-call(bf16[1024,2048]{1,0:T(8,128)(2,1)} %get-tuple-element.39.x_ref.x0_ref, bf16[1024,2048]{1,0:T(8,128)(2,1)} %get-tuple-element.40.dy_ref, bf16[1024,1024]{1,0:T(8,128)(2,1)} %get-tuple-element.41.dg_ref, bf16[1024,1024]{1,0:T(8,128)(2,1)} %get-tuple-element.42.h_ref), custom_call_target="tpu_custom_call" | custom-call | flops 1073741824 | bytes 3670016 | tf_op jit(solution)/shard_map/early_grads/pallas_call | solution.py:305
  124.7 3.1 %add.2 = bf16[64,16,1024]{2,1,0:T(8,128)(2,1)} custom-call(bf16[64,16,1024]{2,1,0:T(8,128)(2,1)S(1)} %copy-done.1, bf16[64,16,1024]{2,1,0:T(8,128)(2,1)} %collective-permute-done.1.b_ref), custom_call_target="tpu_custom_call" | custom-call | bytes 786432 | tf_op jit(solution)/shard_map/add/pallas_call | solution.py:279
  127.8 6.2 %all-to-all-done.1.got1 = bf16[64,16,2048]{2,1,0:T(8,128)(2,1)} async-done(((bf16[64,16,2048]{2,1,0:T(8,128)(2,1)}), bf16[64,16,2048]{2,1,0:T(8,128)(2,1)}, u32[]{:S(2)}, u32[]{:S(2)}) %all-to-all-start.1) | async-done | bytes 4194336 | tf_op jit(solution)/shard_map/all_to_all | solution.py:407
  133.9 7.8 %all-to-all-start.2 = ((bf16[64,16,1024]{2,1,0:T(8,128)(2,1)}), bf16[64,16,1024]{2,1,0:T(8,128)(2,1)S(1)}, u32[]{:S(2)}, u32[]{:S(2)}) async-start(bf16[64,16,1024]{2,1,0:T(8,128)(2,1)} %add.2), calls=%async_computation.2 | async-start | bytes 4194304 | tf_op jit(solution)/shard_map/all_to_all | solution.py:407
  141.7 0.0 copy-start.2
  141.7 30.2 %hidden.3 = (bf16[1024,2048]{1,0:T(8,128)(2,1)}, bf16[1024,2048]{1,0:T(8,128)(2,1)}, bf16[1024,1024]{1,0:T(8,128)(2,1)}, bf16[1024,1024]{1,0:T(8,128)(2,1)}, bf1...) custom-call(bf16[64,16,2048]{2,1,0:T(8,128)(2,1)} %collective-permute-done.2.got0, ...), custom_call_target="tpu_custom_call" | custom-call | flops 2684354560 | bytes 4718592 | tf_op jit(solution)/shard_map/hidden/pallas_call | solution.py:234
  172.0 0.0 copy-start
  172.0 0.3 collective-permute-start.3
  172.3 1.3 collect.2.refs_2_
  173.6 2.8 %collective-permute-done.3.b_ref = bf16[64,16,1024]{2,1,0:T(8,128)(2,1)S(1)} collective-permute-done((bf16[64,16,1024]{2,1,0:T(8,128)(2,1)}, bf16[64,16,1024]{2,1,0:T(8,128)(2,1)S(1)}, u32[]{:S(2)}, u32[]{:S(2)}) %collective-permute-start.3) | collective-permute-done | bytes 2097184 | tf_op jit(solution)/shard_map/ppermute | solution.py:411
  176.4 1.5 add.3
  177.9 10.7 %all-to-all-start.3 = ((bf16[64,16,1024]{2,1,0:T(8,128)(2,1)}), bf16[64,16,1024]{2,1,0:T(8,128)(2,1)S(1)}, u32[]{:S(2)}, u32[]{:S(2)}) async-start(bf16[64,16,1024]{2,1,0:T(8,128)(2,1)} %add.3), calls=%async_computation.3 | async-start | bytes 4194304 | tf_op jit(solution)/shard_map/all_to_all | solution.py:407
  188.6 27.3 %weight_grads.1 = (bf16[2048,1024]{1,0:T(8,128)(2,1)}, bf16[2048,1024]{1,0:T(8,128)(2,1)}, bf16[1024,2048]{1,0:T(8,128)(2,1)}) custom-call(bf16[1024,2048]{1,0:T(8,128)(2,1)} %get-tuple-element.39.x_ref.x0_ref, bf16[1024,2048]{1,0:T(8,128)(2,1)} %get-tuple-element.57.x1_ref, bf16[1024,2048]{1,0:T(8,128)(2,1)} %get-tuple-element.58.dy_ref, ...), custom_call_target="tpu_custom_call" | custom-call | flops 2147483648 | bytes 6291456 | tf_op jit(solution)/shard_map/weight_grads/pallas_call | solution.py:356
  215.9 1.9 all-to-all-done.3.refs_1_
  217.8 2.1 collect.3
  (8 shorter events, 0.0 us)
Async XLA Ops:
  5.5 65.0 %all-to-all-start = ((bf16[64,16,2048]{2,1,0:T(8,128)(2,1)}), bf16[64,16,2048]{2,1,0:T(8,128)(2,1)}, u32[]{:S(2)}, u32[]{:S(2)}) async-start(bf16[64,16,2048]{2,1,0:T(8,128)(2,1)} %pack.2), calls=%async_computation | async-start | bytes 8388608 | tf_op jit(solution)/shard_map/all_to_all | solution.py:407
  70.5 9.5 %collective-permute-start = (bf16[64,16,2048]{2,1,0:T(8,128)(2,1)}, bf16[64,16,2048]{2,1,0:T(8,128)(2,1)}, u32[]{:S(2)}, u32[]{:S(2)}) collective-permute-start(bf16[64,16,2048]{2,1,0:T(8,128)(2,1)} %all-to-all-done.got1), channel_id=1, source_target_pairs={{0,32},{32,0},{1,33},{33,1},{2,34},{34,2},{3,35},{35,3},{4,36},{36... | collective-permute-start | bytes 12582920 | tf_op jit(solution)/shard_map/ppermute | solution.py:411
  70.5 63.4 %all-to-all-start.1 = ((bf16[64,16,2048]{2,1,0:T(8,128)(2,1)}), bf16[64,16,2048]{2,1,0:T(8,128)(2,1)}, u32[]{:S(2)}, u32[]{:S(2)}) async-start(bf16[64,16,2048]{2,1,0:T(8,128)(2,1)} %pack.3), calls=%async_computation.1 | async-start | bytes 8388608 | tf_op jit(solution)/shard_map/all_to_all | solution.py:407
  110.4 14.3 %collective-permute-start.1 = (bf16[64,16,1024]{2,1,0:T(8,128)(2,1)}, bf16[64,16,1024]{2,1,0:T(8,128)(2,1)}, u32[]{:S(2)}, u32[]{:S(2)}) collective-permute-start(bf16[64,16,1024]{2,1,0:T(8,128)(2,1)} %get-tuple-element.38), channel_id=1, source_target_pairs={{0,32},{32,0},{1,33},{33,1},{2,34},{34,2},{3,35},{35,3},{4,36},{36... | collective-permute-start | bytes 6291464 | tf_op jit(solution)/shard_map/ppermute | solution.py:411
  110.7 14.0 %copy-start.1 = (bf16[64,16,1024]{2,1,0:T(8,128)(2,1)S(1)}, bf16[64,16,1024]{2,1,0:T(8,128)(2,1)}, u32[]{:S(2)}) copy-start(bf16[64,16,1024]{2,1,0:T(8,128)(2,1)} %get-tuple-element.47.a_ref) | copy-start | bytes 6291460
  133.9 7.8 %collective-permute-start.2 = (bf16[64,16,2048]{2,1,0:T(8,128)(2,1)}, bf16[64,16,2048]{2,1,0:T(8,128)(2,1)}, u32[]{:S(2)}, u32[]{:S(2)}) collective-permute-start(bf16[64,16,2048]{2,1,0:T(8,128)(2,1)} %all-to-all-done.1.got1), channel_id=1, source_target_pairs={{0,32},{32,0},{1,33},{33,1},{2,34},{34,2},{3,35},{35,3},{4,36},{36... | collective-permute-start | bytes 12582920 | tf_op jit(solution)/shard_map/ppermute | solution.py:411
  133.9 38.0 %all-to-all-start.2 = ((bf16[64,16,1024]{2,1,0:T(8,128)(2,1)}), bf16[64,16,1024]{2,1,0:T(8,128)(2,1)S(1)}, u32[]{:S(2)}, u32[]{:S(2)}) async-start(bf16[64,16,1024]{2,1,0:T(8,128)(2,1)} %add.2), calls=%async_computation.2 | async-start | bytes 4194304 | tf_op jit(solution)/shard_map/all_to_all | solution.py:407
  141.7 30.6 %copy-start.2 = (s32[128,2]{0,1:T(2,128)S(1)}, s32[128,2]{0,1:T(2,128)}, u32[]{:S(2)}) copy-start(s32[128,2]{0,1:T(2,128)} %param.10) | copy-start | bytes 3076
  172.0 4.5 %copy-start = (bf16[64,16,1024]{2,1,0:T(8,128)(2,1)S(1)}, bf16[64,16,1024]{2,1,0:T(8,128)(2,1)}, u32[]{:S(2)}) copy-start(bf16[64,16,1024]{2,1,0:T(8,128)(2,1)} %get-tuple-element.50.a_ref) | copy-start | bytes 6291460
  172.0 4.5 %collective-permute-start.3 = (bf16[64,16,1024]{2,1,0:T(8,128)(2,1)}, bf16[64,16,1024]{2,1,0:T(8,128)(2,1)S(1)}, u32[]{:S(2)}, u32[]{:S(2)}) collective-permute-start(bf16[64,16,1024]{2,1,0:T(8,128)(2,1)} %get-tuple-element.52), channel_id=1, source_target_pairs={{0,32},{32,0},{1,33},{33,1},{2,34},{34,2},{3,35},{35,3},{4,36},{36... | collective-permute-start | bytes 6291464 | tf_op jit(solution)/shard_map/ppermute | solution.py:411
  177.9 39.9 %all-to-all-start.3 = ((bf16[64,16,1024]{2,1,0:T(8,128)(2,1)}), bf16[64,16,1024]{2,1,0:T(8,128)(2,1)S(1)}, u32[]{:S(2)}, u32[]{:S(2)}) async-start(bf16[64,16,1024]{2,1,0:T(8,128)(2,1)} %add.3), calls=%async_computation.3 | async-start | bytes 4194304 | tf_op jit(solution)/shard_map/all_to_all | solution.py:407

commit v5 on v4

--- a/solution.py
+++ b/solution.py
@@ -49,44 +49,51 @@
     return jnp.sum(jnp.where(same, row, jnp.zeros_like(row)), axis=1, keepdims=True)
 
 
-def pack_kernel(chunk, experts, ids_ref, gates_ref, tok_ref, grad_ref, out_ref, picks, gates):
-    tok = ids_ref.shape[1]
-
-    @pl.when(pl.program_id(0) == 0)
-    def _():
-        slots = route_slots(ids_ref, experts, chunk)
-        at = lax.broadcasted_iota(jnp.int32, (experts * ROWS, tok), 0)
-        picks[0] = ((at == slots[0]) | (at == slots[1])).astype(BF16)
-        for k in range(2):
-            there = jnp.where(slots[k] >= 0, slots[k] + RANKS, -1)
-            picks[1 + k] = (at == there).astype(BF16)
-            gates[k] = as_column(gates_ref[k : k + 1, :])
-
-    packed = jnp.dot(picks[0], tok_ref[...], preferred_element_type=F32)
+def pack_kernel(chunk, experts, ids_ref, gates_ref, tok_ref, grad_ref, out, pick, rows, packed, sem):
+    tok, width = tok_ref.shape
+    cols = 512
+    slots = route_slots(ids_ref, experts, chunk)
+    at = lax.broadcasted_iota(jnp.int32, (experts * ROWS, tok), 0)
+    pick[:, :tok] = ((at == slots[0]) | (at == slots[1])).astype(BF16)
+    rows[:tok] = tok_ref[...]
     for k in range(2):
-        dy = (gates[k] * grad_ref[...].astype(F32)).astype(BF16)
-        packed = packed + jnp.dot(picks[1 + k], dy, preferred_element_type=F32)
-    packed = packed.astype(BF16).reshape(experts, ROWS, packed.shape[1])
-    out_ref[:experts] = packed
-    out_ref[experts:] = packed
-
-
-def pack(chunk, experts, ids, gates, tokens, grad_out, cols=1024):
+        here = slice((1 + k) * tok, (2 + k) * tok)
+        there = jnp.where(slots[k] >= 0, slots[k] + RANKS, -1)
+        pick[:, here] = (at == there).astype(BF16)
+        gate = as_column(gates_ref[k : k + 1, :])
+        rows[here] = (gate * grad_ref[...].astype(F32)).astype(BF16)
+
+    copies = []
+    for i in range(width // cols):
+        part = block(cols, i)
+        packed[:, :, part] = (
+            jnp.dot(pick[...], rows[:, part], preferred_element_type=F32)
+            .astype(BF16)
+            .reshape(experts, ROWS, cols)
+        )
+        for yhi in range(2):
+            copies.append(
+                pltpu.make_async_copy(
+                    packed.at[:, :, part], out.at[block(experts, yhi), :, part], sem.at[yhi, i]
+                )
+            )
+            copies[-1].start()
+    for copy in copies:
+        copy.wait()
+
+
+def pack(chunk, experts, ids, gates, tokens, grad_out):
     tok, width = tokens.shape
     return pl.pallas_call(
         lambda *refs: pack_kernel(chunk, experts, *refs),
-        grid=(width // cols,),
-        in_specs=[
-            pl.BlockSpec((2, tok), lambda i: (0, 0)),
-            pl.BlockSpec((2, tok), lambda i: (0, 0)),
-            pl.BlockSpec((tok, cols), lambda i: (0, i)),
-            pl.BlockSpec((tok, cols), lambda i: (0, i)),
-        ],
-        out_specs=pl.BlockSpec((2 * experts, ROWS, cols), lambda i: (0, 0, i)),
+        in_specs=[pl.BlockSpec(memory_space=pltpu.VMEM)] * 4,
+        out_specs=pl.BlockSpec(memory_space=pl.ANY),
         out_shape=jax.ShapeDtypeStruct((2 * experts, ROWS, width), BF16),
         scratch_shapes=[
-            pltpu.VMEM((3, experts * ROWS, tok), BF16),
-            pltpu.VMEM((2, tok, 1), F32),
+            pltpu.VMEM((experts * ROWS, 3 * tok), BF16),
+            pltpu.VMEM((3 * tok, width), BF16),
+            pltpu.VMEM((experts, ROWS, width), BF16),
+            pltpu.SemaphoreType.DMA((2, width // 512)),
         ],
         compiler_params=params(60),
         cost_estimate=cost(2 * 3 * tok * experts * ROWS * width, 12, 0),

time: 220 us -> 220 us (level)
  transfers between devices with their start and end apart: 8 -> 8, of which waited for: 4 -> 4; matrix products, arithmetic and copies ran while one was open for 0% -> 0% of each run, Pallas kernels for 51% -> 50%
where the time goes in v5:
time: 220 us; the launch traced here: 219 us
  Pallas kernels  118 us (54%)
  waiting for transfers between devices  60.2 us (27%)
  starting transfers between devices  40.3 us (18%)
    pallas_call x2, Pallas kernels, hidden_pass(): pl.pallas_call(hidden_kernel, in_specs=[pl.BlockSpec(memory_space=pl.ANY)...  60.6 us
    all_to_all x4, waiting for transfers between devices, exchange(): return lax.all_to_all(rows, PEERS, split_axis=0, concat_axis=0, tiled=True)  57.4 us
    all_to_all x4, starting transfers between devices, exchange(): return lax.all_to_all(rows, PEERS, split_axis=0, concat_axis=0, tiled=True)  39.7 us
    pallas_call x1, Pallas kernels, weight_grads(): pl.pallas_call(weight_grads_kernel, grid=(width // cols,), in_specs=[narr...  27.3 us
    pallas_call x1, Pallas kernels, early_grads(): pl.pallas_call(early_grads_kernel, grid=(width // cols,), in_specs=[narro...  14 us
    pallas_call x2, Pallas kernels, pack(): pl.pallas_call(lambda *refs: pack_kernel(chunk, experts, *refs), in_specs...  7.8 us
    pallas_call x2, Pallas kernels, add(): pl.pallas_call(add_kernel, in_specs=[pl.BlockSpec(memory_space=pltpu.VMEM...  4.55 us
  transfers between devices with their start and end apart: 8, of which 4 were waited for; matrix products, arithmetic and copies ran while one was open for 0% of the time, Pallas kernels for 50%

profile of v5, /device:TPU:0, one launch (start us, length us, event | category | flops | bytes accessed | tf_op | source)
XLA Modules:
  0.0 218.9 jit_solution(10051998006715528221)
XLA Ops:
  0.6 3.9 %pack.2 = bf16[64,16,2048]{2,1,0:T(8,128)(2,1)} custom-call(s32[2,128]{1,0:T(2,128)} %bitcast.8, f32[2,128]{1,0:T(2,128)} %bitcast.18, bf16[128,2048]{1,0:T(8,128)(2,1)} %refs_2_.3, bf16[128,2048]{1,0:T(8,128)(2,1)} %refs_3_.3), custom_call_target="tpu_custom_call" | custom-call | flops 100663296 | bytes 1572864 | tf_op jit(solution)/shard_map/pack/pallas_call | solution.py:87
  4.5 11.8 %all-to-all-start = ((bf16[64,16,2048]{2,1,0:T(8,128)(2,1)}), bf16[64,16,2048]{2,1,0:T(8,128)(2,1)}, u32[]{:S(2)}, u32[]{:S(2)}) async-start(bf16[64,16,2048]{2,1,0:T(8,128)(2,1)} %pack.2), calls=%async_computation | async-start | bytes 8388608 | tf_op jit(solution)/shard_map/all_to_all | solution.py:414
  16.3 3.9 %pack.3 = bf16[64,16,2048]{2,1,0:T(8,128)(2,1)} custom-call(s32[2,128]{1,0:T(2,128)} %bitcast.9, f32[2,128]{1,0:T(2,128)} %bitcast.19, bf16[128,2048]{1,0:T(8,128)(2,1)} %refs_2_.3, bf16[128,2048]{1,0:T(8,128)(2,1)} %refs_3_.3), custom_call_target="tpu_custom_call" | custom-call | flops 100663296 | bytes 1572864 | tf_op jit(solution)/shard_map/pack/pallas_call | solution.py:87
  20.2 49.4 %all-to-all-done.got1 = bf16[64,16,2048]{2,1,0:T(8,128)(2,1)} async-done(((bf16[64,16,2048]{2,1,0:T(8,128)(2,1)}), bf16[64,16,2048]{2,1,0:T(8,128)(2,1)}, u32[]{:S(2)}, u32[]{:S(2)}) %all-to-all-start) | async-done | bytes 4194336 | tf_op jit(solution)/shard_map/all_to_all | solution.py:414
  69.6 9.5 %all-to-all-start.1 = ((bf16[64,16,2048]{2,1,0:T(8,128)(2,1)}), bf16[64,16,2048]{2,1,0:T(8,128)(2,1)}, u32[]{:S(2)}, u32[]{:S(2)}) async-start(bf16[64,16,2048]{2,1,0:T(8,128)(2,1)} %pack.3), calls=%async_computation.1 | async-start | bytes 8388608 | tf_op jit(solution)/shard_map/all_to_all | solution.py:414
  79.1 30.3 %hidden.2 = (bf16[1024,2048]{1,0:T(8,128)(2,1)}, bf16[1024,2048]{1,0:T(8,128)(2,1)}, bf16[1024,1024]{1,0:T(8,128)(2,1)}, bf16[1024,1024]{1,0:T(8,128)(2,1)}, bf1...) custom-call(bf16[64,16,2048]{2,1,0:T(8,128)(2,1)} %collective-permute-done.got0, ...), custom_call_target="tpu_custom_call" | custom-call | flops 2684354560 | bytes 4718592 | tf_op jit(solution)/shard_map/hidden/pallas_call | solution.py:241
  109.4 0.3 collective-permute-start.1
  109.7 14.0 %early_grads.1 = (f32[2048,1024]{1,0:T(8,128)}, f32[2048,1024]{1,0:T(8,128)}) custom-call(bf16[1024,2048]{1,0:T(8,128)(2,1)} %get-tuple-element.39.x_ref.x0_ref, bf16[1024,2048]{1,0:T(8,128)(2,1)} %get-tuple-element.40.dy_ref, bf16[1024,1024]{1,0:T(8,128)(2,1)} %get-tuple-element.41.dg_ref, bf16[1024,1024]{1,0:T(8,128)(2,1)} %get-tuple-element.42.h_ref), custom_call_target="tpu_custom_call" | custom-call | flops 1073741824 | bytes 3670016 | tf_op jit(solution)/shard_map/early_grads/pallas_call | solution.py:312
  123.7 0.0 collective-permute-done.1.b_ref
  123.7 3.1 %add.2 = bf16[64,16,1024]{2,1,0:T(8,128)(2,1)} custom-call(bf16[64,16,1024]{2,1,0:T(8,128)(2,1)S(1)} %copy-done.1, bf16[64,16,1024]{2,1,0:T(8,128)(2,1)} %collective-permute-done.1.b_ref), custom_call_target="tpu_custom_call" | custom-call | bytes 786432 | tf_op jit(solution)/shard_map/add/pallas_call | solution.py:286
  126.8 6.2 %all-to-all-done.1.got1 = bf16[64,16,2048]{2,1,0:T(8,128)(2,1)} async-done(((bf16[64,16,2048]{2,1,0:T(8,128)(2,1)}), bf16[64,16,2048]{2,1,0:T(8,128)(2,1)}, u32[]{:S(2)}, u32[]{:S(2)}) %all-to-all-start.1) | async-done | bytes 4194336 | tf_op jit(solution)/shard_map/all_to_all | solution.py:414
  133.0 0.0 collective-permute-start.2
  133.0 7.8 %all-to-all-start.2 = ((bf16[64,16,1024]{2,1,0:T(8,128)(2,1)}), bf16[64,16,1024]{2,1,0:T(8,128)(2,1)S(1)}, u32[]{:S(2)}, u32[]{:S(2)}) async-start(bf16[64,16,1024]{2,1,0:T(8,128)(2,1)} %add.2), calls=%async_computation.2 | async-start | bytes 4194304 | tf_op jit(solution)/shard_map/all_to_all | solution.py:414
  140.7 0.0 copy-start.2
  140.8 30.2 %hidden.3 = (bf16[1024,2048]{1,0:T(8,128)(2,1)}, bf16[1024,2048]{1,0:T(8,128)(2,1)}, bf16[1024,1024]{1,0:T(8,128)(2,1)}, bf16[1024,1024]{1,0:T(8,128)(2,1)}, bf1...) custom-call(bf16[64,16,2048]{2,1,0:T(8,128)(2,1)} %collective-permute-done.2.got0, ...), custom_call_target="tpu_custom_call" | custom-call | flops 2684354560 | bytes 4718592 | tf_op jit(solution)/shard_map/hidden/pallas_call | solution.py:241
  171.0 0.0 copy-start
  171.0 0.3 collective-permute-start.3
  171.3 1.3 collect.2.refs_2_
  172.7 2.8 %collective-permute-done.3.b_ref = bf16[64,16,1024]{2,1,0:T(8,128)(2,1)S(1)} collective-permute-done((bf16[64,16,1024]{2,1,0:T(8,128)(2,1)}, bf16[64,16,1024]{2,1,0:T(8,128)(2,1)S(1)}, u32[]{:S(2)}, u32[]{:S(2)}) %collective-permute-start.3) | collective-permute-done | bytes 2097184 | tf_op jit(solution)/shard_map/ppermute | solution.py:418
  175.5 1.5 add.3
  177.0 10.7 %all-to-all-start.3 = ((bf16[64,16,1024]{2,1,0:T(8,128)(2,1)}), bf16[64,16,1024]{2,1,0:T(8,128)(2,1)S(1)}, u32[]{:S(2)}, u32[]{:S(2)}) async-start(bf16[64,16,1024]{2,1,0:T(8,128)(2,1)} %add.3), calls=%async_computation.3 | async-start | bytes 4194304 | tf_op jit(solution)/shard_map/all_to_all | solution.py:414
  187.7 27.3 %weight_grads.1 = (bf16[2048,1024]{1,0:T(8,128)(2,1)}, bf16[2048,1024]{1,0:T(8,128)(2,1)}, bf16[1024,2048]{1,0:T(8,128)(2,1)}) custom-call(bf16[1024,2048]{1,0:T(8,128)(2,1)} %get-tuple-element.39.x_ref.x0_ref, bf16[1024,2048]{1,0:T(8,128)(2,1)} %get-tuple-element.57.x1_ref, bf16[1024,2048]{1,0:T(8,128)(2,1)} %get-tuple-element.58.dy_ref, ...), custom_call_target="tpu_custom_call" | custom-call | flops 2147483648 | bytes 6291456 | tf_op jit(solution)/shard_map/weight_grads/pallas_call | solution.py:363
  215.0 1.9 all-to-all-done.3.refs_1_
  216.8 2.1 collect.3
  (8 shorter events, 0.0 us)
Async XLA Ops:
  4.5 65.0 %all-to-all-start = ((bf16[64,16,2048]{2,1,0:T(8,128)(2,1)}), bf16[64,16,2048]{2,1,0:T(8,128)(2,1)}, u32[]{:S(2)}, u32[]{:S(2)}) async-start(bf16[64,16,2048]{2,1,0:T(8,128)(2,1)} %pack.2), calls=%async_computation | async-start | bytes 8388608 | tf_op jit(solution)/shard_map/all_to_all | solution.py:414
  69.6 9.5 %collective-permute-start = (bf16[64,16,2048]{2,1,0:T(8,128)(2,1)}, bf16[64,16,2048]{2,1,0:T(8,128)(2,1)}, u32[]{:S(2)}, u32[]{:S(2)}) collective-permute-start(bf16[64,16,2048]{2,1,0:T(8,128)(2,1)} %all-to-all-done.got1), channel_id=1, source_target_pairs={{0,32},{32,0},{1,33},{33,1},{2,34},{34,2},{3,35},{35,3},{4,36},{36... | collective-permute-start | bytes 12582920 | tf_op jit(solution)/shard_map/ppermute | solution.py:418
  69.6 63.4 %all-to-all-start.1 = ((bf16[64,16,2048]{2,1,0:T(8,128)(2,1)}), bf16[64,16,2048]{2,1,0:T(8,128)(2,1)}, u32[]{:S(2)}, u32[]{:S(2)}) async-start(bf16[64,16,2048]{2,1,0:T(8,128)(2,1)} %pack.3), calls=%async_computation.1 | async-start | bytes 8388608 | tf_op jit(solution)/shard_map/all_to_all | solution.py:414
  109.4 14.3 %collective-permute-start.1 = (bf16[64,16,1024]{2,1,0:T(8,128)(2,1)}, bf16[64,16,1024]{2,1,0:T(8,128)(2,1)}, u32[]{:S(2)}, u32[]{:S(2)}) collective-permute-start(bf16[64,16,1024]{2,1,0:T(8,128)(2,1)} %get-tuple-element.38), channel_id=1, source_target_pairs={{0,32},{32,0},{1,33},{33,1},{2,34},{34,2},{3,35},{35,3},{4,36},{36... | collective-permute-start | bytes 6291464 | tf_op jit(solution)/shard_map/ppermute | solution.py:418
  109.7 14.0 %copy-start.1 = (bf16[64,16,1024]{2,1,0:T(8,128)(2,1)S(1)}, bf16[64,16,1024]{2,1,0:T(8,128)(2,1)}, u32[]{:S(2)}) copy-start(bf16[64,16,1024]{2,1,0:T(8,128)(2,1)} %get-tuple-element.47.a_ref) | copy-start | bytes 6291460
  133.0 7.8 %collective-permute-start.2 = (bf16[64,16,2048]{2,1,0:T(8,128)(2,1)}, bf16[64,16,2048]{2,1,0:T(8,128)(2,1)}, u32[]{:S(2)}, u32[]{:S(2)}) collective-permute-start(bf16[64,16,2048]{2,1,0:T(8,128)(2,1)} %all-to-all-done.1.got1), channel_id=1, source_target_pairs={{0,32},{32,0},{1,33},{33,1},{2,34},{34,2},{3,35},{35,3},{4,36},{36... | collective-permute-start | bytes 12582920 | tf_op jit(solution)/shard_map/ppermute | solution.py:418
  133.0 38.0 %all-to-all-start.2 = ((bf16[64,16,1024]{2,1,0:T(8,128)(2,1)}), bf16[64,16,1024]{2,1,0:T(8,128)(2,1)S(1)}, u32[]{:S(2)}, u32[]{:S(2)}) async-start(bf16[64,16,1024]{2,1,0:T(8,128)(2,1)} %add.2), calls=%async_computation.2 | async-start | bytes 4194304 | tf_op jit(solution)/shard_map/all_to_all | solution.py:414
  140.7 30.6 %copy-start.2 = (s32[128,2]{0,1:T(2,128)S(1)}, s32[128,2]{0,1:T(2,128)}, u32[]{:S(2)}) copy-start(s32[128,2]{0,1:T(2,128)} %param.10) | copy-start | bytes 3076
  171.0 4.5 %copy-start = (bf16[64,16,1024]{2,1,0:T(8,128)(2,1)S(1)}, bf16[64,16,1024]{2,1,0:T(8,128)(2,1)}, u32[]{:S(2)}) copy-start(bf16[64,16,1024]{2,1,0:T(8,128)(2,1)} %get-tuple-element.50.a_ref) | copy-start | bytes 6291460
  171.0 4.5 %collective-permute-start.3 = (bf16[64,16,1024]{2,1,0:T(8,128)(2,1)}, bf16[64,16,1024]{2,1,0:T(8,128)(2,1)S(1)}, u32[]{:S(2)}, u32[]{:S(2)}) collective-permute-start(bf16[64,16,1024]{2,1,0:T(8,128)(2,1)} %get-tuple-element.52), channel_id=1, source_target_pairs={{0,32},{32,0},{1,33},{33,1},{2,34},{34,2},{3,35},{35,3},{4,36},{36... | collective-permute-start | bytes 6291464 | tf_op jit(solution)/shard_map/ppermute | solution.py:418
  177.0 39.8 %all-to-all-start.3 = ((bf16[64,16,1024]{2,1,0:T(8,128)(2,1)}), bf16[64,16,1024]{2,1,0:T(8,128)(2,1)S(1)}, u32[]{:S(2)}, u32[]{:S(2)}) async-start(bf16[64,16,1024]{2,1,0:T(8,128)(2,1)} %add.3), calls=%async_computation.3 | async-start | bytes 4194304 | tf_op jit(solution)/shard_map/all_to_all | solution.py:414

commit v6 on v5

--- a/solution.py
+++ b/solution.py
@@ -374,35 +374,31 @@
 
 
 def collect_kernel(chunk, experts, ids_ref, back_ref, *refs):
-    half = pl.program_id(0)
     tok = ids_ref.shape[1]
+    half = back_ref.shape[2]
     lane = lax.broadcasted_iota(jnp.int32, (tok, experts * ROWS), 1)
-    pick = jnp.zeros((tok, experts * ROWS), jnp.bool_)
-    for slot in route_slots(ids_ref, experts, chunk):
-        there = jnp.where(slot >= 0, slot + half * RANKS, -1)
-        pick = pick | (lane == as_column(there))
+    slots = [as_column(slot) for slot in route_slots(ids_ref, experts, chunk)]
     dx = (back_ref[:experts].astype(F32) + back_ref[experts:].astype(F32)).astype(BF16)
-    dx = dx.reshape(experts * ROWS, dx.shape[2])
-    total = jnp.dot(pick.astype(BF16), dx, preferred_element_type=F32)
-    if len(refs) > 1:
-        total = refs[0][...] + total
-    refs[-1][...] = total.astype(refs[-1].dtype)
+    dx = dx.reshape(experts * ROWS, half)
+    for side in range(2):
+        cols = slice(side * half, (side + 1) * half)
+        pick = jnp.zeros((tok, experts * ROWS), jnp.bool_)
+        for slot in slots:
+            pick = pick | (lane == jnp.where(slot >= 0, slot + side * RANKS, -1))
+        total = jnp.dot(pick.astype(BF16), dx, preferred_element_type=F32)
+        if len(refs) > 1:
+            total = refs[0][:, cols] + total
+        refs[-1][:, cols] = total.astype(refs[-1].dtype)
 
 
 def collect(chunk, experts, ids, back, before=None):
     tok = ids.shape[1]
-    peers, _, half = back.shape
-    out = pl.BlockSpec((tok, half), lambda i: (0, i))
+    half = back.shape[2]
     more = () if before is None else (before,)
     return pl.pallas_call(
         lambda *refs: collect_kernel(chunk, experts, *refs),
-        grid=(2,),
-        in_specs=[
-            pl.BlockSpec((2, tok), lambda i: (0, 0)),
-            pl.BlockSpec((peers, ROWS, half), lambda i: (0, 0, 0)),
-        ]
-        + [out] * len(more),
-        out_specs=out,
+        in_specs=[pl.BlockSpec(memory_space=pltpu.VMEM)] * (2 + len(more)),
+        out_specs=pl.BlockSpec(memory_space=pltpu.VMEM),
         out_shape=jax.ShapeDtypeStruct((tok, 2 * half), BF16 if more else F32),
         compiler_params=params(24),
         cost_estimate=cost(2 * 2 * tok * experts * ROWS * half, 4, 0),

time: 220 us -> 219 us (level)
  no operation moved by 1% of the time
where the time goes in v6:
time: 219 us; the launch traced here: 218 us
  Pallas kernels  117 us (53%)
  waiting for transfers between devices  60.8 us (28%)
  starting transfers between devices  40.3 us (18%)
    pallas_call x2, Pallas kernels, hidden_pass(): pl.pallas_call(hidden_kernel, in_specs=[pl.BlockSpec(memory_space=pl.ANY)...  60.6 us
    all_to_all x4, waiting for transfers between devices, exchange(): return lax.all_to_all(rows, PEERS, split_axis=0, concat_axis=0, tiled=True)  57.4 us
    all_to_all x4, starting transfers between devices, exchange(): return lax.all_to_all(rows, PEERS, split_axis=0, concat_axis=0, tiled=True)  39.7 us
    pallas_call x1, Pallas kernels, weight_grads(): pl.pallas_call(weight_grads_kernel, grid=(width // cols,), in_specs=[narr...  27.3 us
    pallas_call x1, Pallas kernels, early_grads(): pl.pallas_call(early_grads_kernel, grid=(width // cols,), in_specs=[narro...  14 us
    pallas_call x2, Pallas kernels, pack(): pl.pallas_call(lambda *refs: pack_kernel(chunk, experts, *refs), in_specs...  7.8 us
    pallas_call x2, Pallas kernels, add(): pl.pallas_call(add_kernel, in_specs=[pl.BlockSpec(memory_space=pltpu.VMEM...  4.55 us
  transfers between devices with their start and end apart: 8, of which 4 were waited for; matrix products, arithmetic and copies ran while one was open for 0% of the time, Pallas kernels for 50%

profile of v6, /device:TPU:0, one launch (start us, length us, event | category | flops | bytes accessed | tf_op | source)
XLA Modules:
  0.0 218.4 jit_solution(7144251126017826759)
XLA Ops:
  0.6 3.9 %pack.2 = bf16[64,16,2048]{2,1,0:T(8,128)(2,1)} custom-call(s32[2,128]{1,0:T(2,128)} %bitcast.8, f32[2,128]{1,0:T(2,128)} %bitcast.18, bf16[128,2048]{1,0:T(8,128)(2,1)} %refs_2_.3, bf16[128,2048]{1,0:T(8,128)(2,1)} %refs_3_.3), custom_call_target="tpu_custom_call" | custom-call | flops 100663296 | bytes 1572864 | tf_op jit(solution)/shard_map/pack/pallas_call | solution.py:87
  4.5 11.8 %all-to-all-start = ((bf16[64,16,2048]{2,1,0:T(8,128)(2,1)}), bf16[64,16,2048]{2,1,0:T(8,128)(2,1)}, u32[]{:S(2)}, u32[]{:S(2)}) async-start(bf16[64,16,2048]{2,1,0:T(8,128)(2,1)} %pack.2), calls=%async_computation | async-start | bytes 8388608 | tf_op jit(solution)/shard_map/all_to_all | solution.py:410
  16.3 3.9 %pack.3 = bf16[64,16,2048]{2,1,0:T(8,128)(2,1)} custom-call(s32[2,128]{1,0:T(2,128)} %bitcast.9, f32[2,128]{1,0:T(2,128)} %bitcast.19, bf16[128,2048]{1,0:T(8,128)(2,1)} %refs_2_.3, bf16[128,2048]{1,0:T(8,128)(2,1)} %refs_3_.3), custom_call_target="tpu_custom_call" | custom-call | flops 100663296 | bytes 1572864 | tf_op jit(solution)/shard_map/pack/pallas_call | solution.py:87
  20.2 49.4 %all-to-all-done.got1 = bf16[64,16,2048]{2,1,0:T(8,128)(2,1)} async-done(((bf16[64,16,2048]{2,1,0:T(8,128)(2,1)}), bf16[64,16,2048]{2,1,0:T(8,128)(2,1)}, u32[]{:S(2)}, u32[]{:S(2)}) %all-to-all-start) | async-done | bytes 4194336 | tf_op jit(solution)/shard_map/all_to_all | solution.py:410
  69.6 9.5 %all-to-all-start.1 = ((bf16[64,16,2048]{2,1,0:T(8,128)(2,1)}), bf16[64,16,2048]{2,1,0:T(8,128)(2,1)}, u32[]{:S(2)}, u32[]{:S(2)}) async-start(bf16[64,16,2048]{2,1,0:T(8,128)(2,1)} %pack.3), calls=%async_computation.1 | async-start | bytes 8388608 | tf_op jit(solution)/shard_map/all_to_all | solution.py:410
  79.0 0.0 collective-permute-done.got0
  79.1 30.3 %hidden.2 = (bf16[1024,2048]{1,0:T(8,128)(2,1)}, bf16[1024,2048]{1,0:T(8,128)(2,1)}, bf16[1024,1024]{1,0:T(8,128)(2,1)}, bf16[1024,1024]{1,0:T(8,128)(2,1)}, bf1...) custom-call(bf16[64,16,2048]{2,1,0:T(8,128)(2,1)} %collective-permute-done.got0, ...), custom_call_target="tpu_custom_call" | custom-call | flops 2684354560 | bytes 4718592 | tf_op jit(solution)/shard_map/hidden/pallas_call | solution.py:241
  109.4 0.3 collective-permute-start.1
  109.7 14.0 %early_grads.1 = (f32[2048,1024]{1,0:T(8,128)}, f32[2048,1024]{1,0:T(8,128)}) custom-call(bf16[1024,2048]{1,0:T(8,128)(2,1)} %get-tuple-element.39.x_ref.x0_ref, bf16[1024,2048]{1,0:T(8,128)(2,1)} %get-tuple-element.40.dy_ref, bf16[1024,1024]{1,0:T(8,128)(2,1)} %get-tuple-element.41.dg_ref, bf16[1024,1024]{1,0:T(8,128)(2,1)} %get-tuple-element.42.h_ref), custom_call_target="tpu_custom_call" | custom-call | flops 1073741824 | bytes 3670016 | tf_op jit(solution)/shard_map/early_grads/pallas_call | solution.py:312
  123.7 0.0 collective-permute-done.1.b_ref
  123.7 3.1 %add.2 = bf16[64,16,1024]{2,1,0:T(8,128)(2,1)} custom-call(bf16[64,16,1024]{2,1,0:T(8,128)(2,1)S(1)} %copy-done.1, bf16[64,16,1024]{2,1,0:T(8,128)(2,1)} %collective-permute-done.1.b_ref), custom_call_target="tpu_custom_call" | custom-call | bytes 786432 | tf_op jit(solution)/shard_map/add/pallas_call | solution.py:286
  126.8 6.2 %all-to-all-done.1.got1 = bf16[64,16,2048]{2,1,0:T(8,128)(2,1)} async-done(((bf16[64,16,2048]{2,1,0:T(8,128)(2,1)}), bf16[64,16,2048]{2,1,0:T(8,128)(2,1)}, u32[]{:S(2)}, u32[]{:S(2)}) %all-to-all-start.1) | async-done | bytes 4194336 | tf_op jit(solution)/shard_map/all_to_all | solution.py:410
  133.0 7.8 %all-to-all-start.2 = ((bf16[64,16,1024]{2,1,0:T(8,128)(2,1)}), bf16[64,16,1024]{2,1,0:T(8,128)(2,1)S(1)}, u32[]{:S(2)}, u32[]{:S(2)}) async-start(bf16[64,16,1024]{2,1,0:T(8,128)(2,1)} %add.2), calls=%async_computation.2 | async-start | bytes 4194304 | tf_op jit(solution)/shard_map/all_to_all | solution.py:410
  140.7 0.0 copy-start.2
  140.8 30.2 %hidden.3 = (bf16[1024,2048]{1,0:T(8,128)(2,1)}, bf16[1024,2048]{1,0:T(8,128)(2,1)}, bf16[1024,1024]{1,0:T(8,128)(2,1)}, bf16[1024,1024]{1,0:T(8,128)(2,1)}, bf1...) custom-call(bf16[64,16,2048]{2,1,0:T(8,128)(2,1)} %collective-permute-done.2.got0, ...), custom_call_target="tpu_custom_call" | custom-call | flops 2684354560 | bytes 4718592 | tf_op jit(solution)/shard_map/hidden/pallas_call | solution.py:241
  171.0 0.0 copy-start
  171.0 0.3 collective-permute-start.3
  171.3 0.8 collect.2.refs_2_
  172.1 3.3 %collective-permute-done.3.b_ref = bf16[64,16,1024]{2,1,0:T(8,128)(2,1)S(1)} collective-permute-done((bf16[64,16,1024]{2,1,0:T(8,128)(2,1)}, bf16[64,16,1024]{2,1,0:T(8,128)(2,1)S(1)}, u32[]{:S(2)}, u32[]{:S(2)}) %collective-permute-start.3) | collective-permute-done | bytes 2097184 | tf_op jit(solution)/shard_map/ppermute | solution.py:414
  175.5 1.5 add.3
  177.0 10.7 %all-to-all-start.3 = ((bf16[64,16,1024]{2,1,0:T(8,128)(2,1)}), bf16[64,16,1024]{2,1,0:T(8,128)(2,1)S(1)}, u32[]{:S(2)}, u32[]{:S(2)}) async-start(bf16[64,16,1024]{2,1,0:T(8,128)(2,1)} %add.3), calls=%async_computation.3 | async-start | bytes 4194304 | tf_op jit(solution)/shard_map/all_to_all | solution.py:410
  187.7 27.3 %weight_grads.1 = (bf16[2048,1024]{1,0:T(8,128)(2,1)}, bf16[2048,1024]{1,0:T(8,128)(2,1)}, bf16[1024,2048]{1,0:T(8,128)(2,1)}) custom-call(bf16[1024,2048]{1,0:T(8,128)(2,1)} %get-tuple-element.39.x_ref.x0_ref, bf16[1024,2048]{1,0:T(8,128)(2,1)} %get-tuple-element.57.x1_ref, bf16[1024,2048]{1,0:T(8,128)(2,1)} %get-tuple-element.58.dy_ref, ...), custom_call_target="tpu_custom_call" | custom-call | flops 2147483648 | bytes 6291456 | tf_op jit(solution)/shard_map/weight_grads/pallas_call | solution.py:363
  215.0 1.9 all-to-all-done.3.refs_1_
  216.8 1.6 collect.3
  (8 shorter events, 0.0 us)
Async XLA Ops:
  4.5 65.0 %all-to-all-start = ((bf16[64,16,2048]{2,1,0:T(8,128)(2,1)}), bf16[64,16,2048]{2,1,0:T(8,128)(2,1)}, u32[]{:S(2)}, u32[]{:S(2)}) async-start(bf16[64,16,2048]{2,1,0:T(8,128)(2,1)} %pack.2), calls=%async_computation | async-start | bytes 8388608 | tf_op jit(solution)/shard_map/all_to_all | solution.py:410
  69.6 9.5 %collective-permute-start = (bf16[64,16,2048]{2,1,0:T(8,128)(2,1)}, bf16[64,16,2048]{2,1,0:T(8,128)(2,1)}, u32[]{:S(2)}, u32[]{:S(2)}) collective-permute-start(bf16[64,16,2048]{2,1,0:T(8,128)(2,1)} %all-to-all-done.got1), channel_id=1, source_target_pairs={{0,32},{32,0},{1,33},{33,1},{2,34},{34,2},{3,35},{35,3},{4,36},{36... | collective-permute-start | bytes 12582920 | tf_op jit(solution)/shard_map/ppermute | solution.py:414
  69.6 63.4 %all-to-all-start.1 = ((bf16[64,16,2048]{2,1,0:T(8,128)(2,1)}), bf16[64,16,2048]{2,1,0:T(8,128)(2,1)}, u32[]{:S(2)}, u32[]{:S(2)}) async-start(bf16[64,16,2048]{2,1,0:T(8,128)(2,1)} %pack.3), calls=%async_computation.1 | async-start | bytes 8388608 | tf_op jit(solution)/shard_map/all_to_all | solution.py:410
  109.4 14.3 %collective-permute-start.1 = (bf16[64,16,1024]{2,1,0:T(8,128)(2,1)}, bf16[64,16,1024]{2,1,0:T(8,128)(2,1)}, u32[]{:S(2)}, u32[]{:S(2)}) collective-permute-start(bf16[64,16,1024]{2,1,0:T(8,128)(2,1)} %get-tuple-element.38), channel_id=1, source_target_pairs={{0,32},{32,0},{1,33},{33,1},{2,34},{34,2},{3,35},{35,3},{4,36},{36... | collective-permute-start | bytes 6291464 | tf_op jit(solution)/shard_map/ppermute | solution.py:414
  109.7 14.0 %copy-start.1 = (bf16[64,16,1024]{2,1,0:T(8,128)(2,1)S(1)}, bf16[64,16,1024]{2,1,0:T(8,128)(2,1)}, u32[]{:S(2)}) copy-start(bf16[64,16,1024]{2,1,0:T(8,128)(2,1)} %get-tuple-element.47.a_ref) | copy-start | bytes 6291460
  133.0 7.8 %collective-permute-start.2 = (bf16[64,16,2048]{2,1,0:T(8,128)(2,1)}, bf16[64,16,2048]{2,1,0:T(8,128)(2,1)}, u32[]{:S(2)}, u32[]{:S(2)}) collective-permute-start(bf16[64,16,2048]{2,1,0:T(8,128)(2,1)} %all-to-all-done.1.got1), channel_id=1, source_target_pairs={{0,32},{32,0},{1,33},{33,1},{2,34},{34,2},{3,35},{35,3},{4,36},{36... | collective-permute-start | bytes 12582920 | tf_op jit(solution)/shard_map/ppermute | solution.py:414
  133.0 38.0 %all-to-all-start.2 = ((bf16[64,16,1024]{2,1,0:T(8,128)(2,1)}), bf16[64,16,1024]{2,1,0:T(8,128)(2,1)S(1)}, u32[]{:S(2)}, u32[]{:S(2)}) async-start(bf16[64,16,1024]{2,1,0:T(8,128)(2,1)} %add.2), calls=%async_computation.2 | async-start | bytes 4194304 | tf_op jit(solution)/shard_map/all_to_all | solution.py:410
  140.7 30.6 %copy-start.2 = (s32[128,2]{0,1:T(2,128)S(1)}, s32[128,2]{0,1:T(2,128)}, u32[]{:S(2)}) copy-start(s32[128,2]{0,1:T(2,128)} %param.10) | copy-start | bytes 3076
  171.0 4.5 %copy-start = (bf16[64,16,1024]{2,1,0:T(8,128)(2,1)S(1)}, bf16[64,16,1024]{2,1,0:T(8,128)(2,1)}, u32[]{:S(2)}) copy-start(bf16[64,16,1024]{2,1,0:T(8,128)(2,1)} %get-tuple-element.50.a_ref) | copy-start | bytes 6291460
  171.0 4.5 %collective-permute-start.3 = (bf16[64,16,1024]{2,1,0:T(8,128)(2,1)}, bf16[64,16,1024]{2,1,0:T(8,128)(2,1)S(1)}, u32[]{:S(2)}, u32[]{:S(2)}) collective-permute-start(bf16[64,16,1024]{2,1,0:T(8,128)(2,1)} %get-tuple-element.52), channel_id=1, source_target_pairs={{0,32},{32,0},{1,33},{33,1},{2,34},{34,2},{3,35},{35,3},{4,36},{36... | collective-permute-start | bytes 6291464 | tf_op jit(solution)/shard_map/ppermute | solution.py:414
  177.0 39.8 %all-to-all-start.3 = ((bf16[64,16,1024]{2,1,0:T(8,128)(2,1)}), bf16[64,16,1024]{2,1,0:T(8,128)(2,1)S(1)}, u32[]{:S(2)}, u32[]{:S(2)}) async-start(bf16[64,16,1024]{2,1,0:T(8,128)(2,1)} %add.3), calls=%async_computation.3 | async-start | bytes 4194304 | tf_op jit(solution)/shard_map/all_to_all | solution.py:410

commit v7 on v6

--- a/solution.py
+++ b/solution.py
@@ -356,7 +356,7 @@
 def weight_grads(x, du, dg1, dy1, h1, early):
     rows, width = dy1.shape
     hid = h1.shape[1]
-    cols = 512
+    cols = 256
     narrow = pl.BlockSpec((rows, cols), lambda i: (0, i))
     tall = pl.BlockSpec((cols, hid), lambda i: (i, 0))
     flat = jax.ShapeDtypeStruct((width, hid), BF16)

time: 219 us -> 219 us (level)
  transfers between devices with their start and end apart: 8 -> 8, of which waited for: 4 -> 4; matrix products, arithmetic and copies ran while one was open for 0% -> 0% of each run, Pallas kernels for 50% -> 51%
where the time goes in v7:
time: 219 us; the launch traced here: 218 us
  Pallas kernels  118 us (54%)
  waiting for transfers between devices  59.7 us (27%)
  starting transfers between devices  40.3 us (18%)
    pallas_call x2, Pallas kernels, hidden_pass(): pl.pallas_call(hidden_kernel, in_specs=[pl.BlockSpec(memory_space=pl.ANY)...  60.6 us
    all_to_all x4, waiting for transfers between devices, exchange(): return lax.all_to_all(rows, PEERS, split_axis=0, concat_axis=0, tiled=True)  56.4 us
    all_to_all x4, starting transfers between devices, exchange(): return lax.all_to_all(rows, PEERS, split_axis=0, concat_axis=0, tiled=True)  39.7 us
    pallas_call x1, Pallas kernels, weight_grads(): pl.pallas_call(weight_grads_kernel, grid=(width // cols,), in_specs=[narr...  28.3 us
    pallas_call x1, Pallas kernels, early_grads(): pl.pallas_call(early_grads_kernel, grid=(width // cols,), in_specs=[narro...  14 us
    pallas_call x2, Pallas kernels, pack(): pl.pallas_call(lambda *refs: pack_kernel(chunk, experts, *refs), in_specs...  7.8 us
    pallas_call x2, Pallas kernels, add(): pl.pallas_call(add_kernel, in_specs=[pl.BlockSpec(memory_space=pltpu.VMEM...  4.55 us
  transfers between devices with their start and end apart: 8, of which 4 were waited for; matrix products, arithmetic and copies ran while one was open for 0% of the time, Pallas kernels for 51%

profile of v7, /device:TPU:0, one launch (start us, length us, event | category | flops | bytes accessed | tf_op | source)
XLA Modules:
  0.0 218.4 jit_solution(10196013276250279044)
XLA Ops:
  0.6 3.9 %pack.2 = bf16[64,16,2048]{2,1,0:T(8,128)(2,1)} custom-call(s32[2,128]{1,0:T(2,128)} %bitcast.8, f32[2,128]{1,0:T(2,128)} %bitcast.18, bf16[128,2048]{1,0:T(8,128)(2,1)} %refs_2_.3, bf16[128,2048]{1,0:T(8,128)(2,1)} %refs_3_.3), custom_call_target="tpu_custom_call" | custom-call | flops 100663296 | bytes 1572864 | tf_op jit(solution)/shard_map/pack/pallas_call | solution.py:87
  4.5 11.8 %all-to-all-start = ((bf16[64,16,2048]{2,1,0:T(8,128)(2,1)}), bf16[64,16,2048]{2,1,0:T(8,128)(2,1)}, u32[]{:S(2)}, u32[]{:S(2)}) async-start(bf16[64,16,2048]{2,1,0:T(8,128)(2,1)} %pack.2), calls=%async_computation | async-start | bytes 8388608 | tf_op jit(solution)/shard_map/all_to_all | solution.py:410
  16.3 3.9 %pack.3 = bf16[64,16,2048]{2,1,0:T(8,128)(2,1)} custom-call(s32[2,128]{1,0:T(2,128)} %bitcast.9, f32[2,128]{1,0:T(2,128)} %bitcast.19, bf16[128,2048]{1,0:T(8,128)(2,1)} %refs_2_.3, bf16[128,2048]{1,0:T(8,128)(2,1)} %refs_3_.3), custom_call_target="tpu_custom_call" | custom-call | flops 100663296 | bytes 1572864 | tf_op jit(solution)/shard_map/pack/pallas_call | solution.py:87
  20.2 49.4 %all-to-all-done.got1 = bf16[64,16,2048]{2,1,0:T(8,128)(2,1)} async-done(((bf16[64,16,2048]{2,1,0:T(8,128)(2,1)}), bf16[64,16,2048]{2,1,0:T(8,128)(2,1)}, u32[]{:S(2)}, u32[]{:S(2)}) %all-to-all-start) | async-done | bytes 4194336 | tf_op jit(solution)/shard_map/all_to_all | solution.py:410
  69.6 0.0 collective-permute-start
  69.6 9.5 %all-to-all-start.1 = ((bf16[64,16,2048]{2,1,0:T(8,128)(2,1)}), bf16[64,16,2048]{2,1,0:T(8,128)(2,1)}, u32[]{:S(2)}, u32[]{:S(2)}) async-start(bf16[64,16,2048]{2,1,0:T(8,128)(2,1)} %pack.3), calls=%async_computation.1 | async-start | bytes 8388608 | tf_op jit(solution)/shard_map/all_to_all | solution.py:410
  79.0 0.0 collective-permute-done.got0
  79.1 30.3 %hidden.2 = (bf16[1024,2048]{1,0:T(8,128)(2,1)}, bf16[1024,2048]{1,0:T(8,128)(2,1)}, bf16[1024,1024]{1,0:T(8,128)(2,1)}, bf16[1024,1024]{1,0:T(8,128)(2,1)}, bf1...) custom-call(bf16[64,16,2048]{2,1,0:T(8,128)(2,1)} %collective-permute-done.got0, ...), custom_call_target="tpu_custom_call" | custom-call | flops 2684354560 | bytes 4718592 | tf_op jit(solution)/shard_map/hidden/pallas_call | solution.py:241
  109.4 0.3 collective-permute-start.1
  109.7 14.0 %early_grads.1 = (f32[2048,1024]{1,0:T(8,128)}, f32[2048,1024]{1,0:T(8,128)}) custom-call(bf16[1024,2048]{1,0:T(8,128)(2,1)} %get-tuple-element.39.x_ref.x0_ref, bf16[1024,2048]{1,0:T(8,128)(2,1)} %get-tuple-element.40.dy_ref, bf16[1024,1024]{1,0:T(8,128)(2,1)} %get-tuple-element.41.dg_ref, bf16[1024,1024]{1,0:T(8,128)(2,1)} %get-tuple-element.42.h_ref), custom_call_target="tpu_custom_call" | custom-call | flops 1073741824 | bytes 3670016 | tf_op jit(solution)/shard_map/early_grads/pallas_call | solution.py:312
  123.7 3.1 %add.2 = bf16[64,16,1024]{2,1,0:T(8,128)(2,1)} custom-call(bf16[64,16,1024]{2,1,0:T(8,128)(2,1)S(1)} %copy-done.1, bf16[64,16,1024]{2,1,0:T(8,128)(2,1)} %collective-permute-done.1.b_ref), custom_call_target="tpu_custom_call" | custom-call | bytes 786432 | tf_op jit(solution)/shard_map/add/pallas_call | solution.py:286
  126.8 6.2 %all-to-all-done.1.got1 = bf16[64,16,2048]{2,1,0:T(8,128)(2,1)} async-done(((bf16[64,16,2048]{2,1,0:T(8,128)(2,1)}), bf16[64,16,2048]{2,1,0:T(8,128)(2,1)}, u32[]{:S(2)}, u32[]{:S(2)}) %all-to-all-start.1) | async-done | bytes 4194336 | tf_op jit(solution)/shard_map/all_to_all | solution.py:410
  133.0 7.8 %all-to-all-start.2 = ((bf16[64,16,1024]{2,1,0:T(8,128)(2,1)}), bf16[64,16,1024]{2,1,0:T(8,128)(2,1)S(1)}, u32[]{:S(2)}, u32[]{:S(2)}) async-start(bf16[64,16,1024]{2,1,0:T(8,128)(2,1)} %add.2), calls=%async_computation.2 | async-start | bytes 4194304 | tf_op jit(solution)/shard_map/all_to_all | solution.py:410
  140.7 0.0 copy-start.2
  140.8 30.2 %hidden.3 = (bf16[1024,2048]{1,0:T(8,128)(2,1)}, bf16[1024,2048]{1,0:T(8,128)(2,1)}, bf16[1024,1024]{1,0:T(8,128)(2,1)}, bf16[1024,1024]{1,0:T(8,128)(2,1)}, bf1...) custom-call(bf16[64,16,2048]{2,1,0:T(8,128)(2,1)} %collective-permute-done.2.got0, ...), custom_call_target="tpu_custom_call" | custom-call | flops 2684354560 | bytes 4718592 | tf_op jit(solution)/shard_map/hidden/pallas_call | solution.py:241
  171.0 0.0 copy-start
  171.0 0.3 collective-permute-start.3
  171.3 0.8 collect.2.refs_2_
  172.1 3.3 %collective-permute-done.3.b_ref = bf16[64,16,1024]{2,1,0:T(8,128)(2,1)S(1)} collective-permute-done((bf16[64,16,1024]{2,1,0:T(8,128)(2,1)}, bf16[64,16,1024]{2,1,0:T(8,128)(2,1)S(1)}, u32[]{:S(2)}, u32[]{:S(2)}) %collective-permute-start.3) | collective-permute-done | bytes 2097184 | tf_op jit(solution)/shard_map/ppermute | solution.py:414
  175.5 1.5 add.3
  177.0 10.7 %all-to-all-start.3 = ((bf16[64,16,1024]{2,1,0:T(8,128)(2,1)}), bf16[64,16,1024]{2,1,0:T(8,128)(2,1)S(1)}, u32[]{:S(2)}, u32[]{:S(2)}) async-start(bf16[64,16,1024]{2,1,0:T(8,128)(2,1)} %add.3), calls=%async_computation.3 | async-start | bytes 4194304 | tf_op jit(solution)/shard_map/all_to_all | solution.py:410
  187.7 28.3 %weight_grads.1 = (bf16[2048,1024]{1,0:T(8,128)(2,1)}, bf16[2048,1024]{1,0:T(8,128)(2,1)}, bf16[1024,2048]{1,0:T(8,128)(2,1)}) custom-call(bf16[1024,2048]{1,0:T(8,128)(2,1)} %get-tuple-element.39.x_ref.x0_ref, bf16[1024,2048]{1,0:T(8,128)(2,1)} %get-tuple-element.57.x1_ref, bf16[1024,2048]{1,0:T(8,128)(2,1)} %get-tuple-element.58.dy_ref, ...), custom_call_target="tpu_custom_call" | custom-call | flops 2147483648 | bytes 6291456 | tf_op jit(solution)/shard_map/weight_grads/pallas_call | solution.py:363
  216.0 0.9 all-to-all-done.3.refs_1_
  216.8 1.6 collect.3
  (8 shorter events, 0.0 us)
Async XLA Ops:
  4.5 65.0 %all-to-all-start = ((bf16[64,16,2048]{2,1,0:T(8,128)(2,1)}), bf16[64,16,2048]{2,1,0:T(8,128)(2,1)}, u32[]{:S(2)}, u32[]{:S(2)}) async-start(bf16[64,16,2048]{2,1,0:T(8,128)(2,1)} %pack.2), calls=%async_computation | async-start | bytes 8388608 | tf_op jit(solution)/shard_map/all_to_all | solution.py:410
  69.6 9.5 %collective-permute-start = (bf16[64,16,2048]{2,1,0:T(8,128)(2,1)}, bf16[64,16,2048]{2,1,0:T(8,128)(2,1)}, u32[]{:S(2)}, u32[]{:S(2)}) collective-permute-start(bf16[64,16,2048]{2,1,0:T(8,128)(2,1)} %all-to-all-done.got1), channel_id=1, source_target_pairs={{0,32},{32,0},{1,33},{33,1},{2,34},{34,2},{3,35},{35,3},{4,36},{36... | collective-permute-start | bytes 12582920 | tf_op jit(solution)/shard_map/ppermute | solution.py:414
  69.6 63.4 %all-to-all-start.1 = ((bf16[64,16,2048]{2,1,0:T(8,128)(2,1)}), bf16[64,16,2048]{2,1,0:T(8,128)(2,1)}, u32[]{:S(2)}, u32[]{:S(2)}) async-start(bf16[64,16,2048]{2,1,0:T(8,128)(2,1)} %pack.3), calls=%async_computation.1 | async-start | bytes 8388608 | tf_op jit(solution)/shard_map/all_to_all | solution.py:410
  109.4 14.3 %collective-permute-start.1 = (bf16[64,16,1024]{2,1,0:T(8,128)(2,1)}, bf16[64,16,1024]{2,1,0:T(8,128)(2,1)}, u32[]{:S(2)}, u32[]{:S(2)}) collective-permute-start(bf16[64,16,1024]{2,1,0:T(8,128)(2,1)} %get-tuple-element.38), channel_id=1, source_target_pairs={{0,32},{32,0},{1,33},{33,1},{2,34},{34,2},{3,35},{35,3},{4,36},{36... | collective-permute-start | bytes 6291464 | tf_op jit(solution)/shard_map/ppermute | solution.py:414
  109.7 14.0 %copy-start.1 = (bf16[64,16,1024]{2,1,0:T(8,128)(2,1)S(1)}, bf16[64,16,1024]{2,1,0:T(8,128)(2,1)}, u32[]{:S(2)}) copy-start(bf16[64,16,1024]{2,1,0:T(8,128)(2,1)} %get-tuple-element.47.a_ref) | copy-start | bytes 6291460
  133.0 7.8 %collective-permute-start.2 = (bf16[64,16,2048]{2,1,0:T(8,128)(2,1)}, bf16[64,16,2048]{2,1,0:T(8,128)(2,1)}, u32[]{:S(2)}, u32[]{:S(2)}) collective-permute-start(bf16[64,16,2048]{2,1,0:T(8,128)(2,1)} %all-to-all-done.1.got1), channel_id=1, source_target_pairs={{0,32},{32,0},{1,33},{33,1},{2,34},{34,2},{3,35},{35,3},{4,36},{36... | collective-permute-start | bytes 12582920 | tf_op jit(solution)/shard_map/ppermute | solution.py:414
  133.0 38.0 %all-to-all-start.2 = ((bf16[64,16,1024]{2,1,0:T(8,128)(2,1)}), bf16[64,16,1024]{2,1,0:T(8,128)(2,1)S(1)}, u32[]{:S(2)}, u32[]{:S(2)}) async-start(bf16[64,16,1024]{2,1,0:T(8,128)(2,1)} %add.2), calls=%async_computation.2 | async-start | bytes 4194304 | tf_op jit(solution)/shard_map/all_to_all | solution.py:410
  140.7 30.6 %copy-start.2 = (s32[128,2]{0,1:T(2,128)S(1)}, s32[128,2]{0,1:T(2,128)}, u32[]{:S(2)}) copy-start(s32[128,2]{0,1:T(2,128)} %param.10) | copy-start | bytes 3076
  171.0 4.5 %copy-start = (bf16[64,16,1024]{2,1,0:T(8,128)(2,1)S(1)}, bf16[64,16,1024]{2,1,0:T(8,128)(2,1)}, u32[]{:S(2)}) copy-start(bf16[64,16,1024]{2,1,0:T(8,128)(2,1)} %get-tuple-element.50.a_ref) | copy-start | bytes 6291460
  171.0 4.5 %collective-permute-start.3 = (bf16[64,16,1024]{2,1,0:T(8,128)(2,1)}, bf16[64,16,1024]{2,1,0:T(8,128)(2,1)S(1)}, u32[]{:S(2)}, u32[]{:S(2)}) collective-permute-start(bf16[64,16,1024]{2,1,0:T(8,128)(2,1)} %get-tuple-element.52), channel_id=1, source_target_pairs={{0,32},{32,0},{1,33},{33,1},{2,34},{34,2},{3,35},{35,3},{4,36},{36... | collective-permute-start | bytes 6291464 | tf_op jit(solution)/shard_map/ppermute | solution.py:414
  177.0 39.8 %all-to-all-start.3 = ((bf16[64,16,1024]{2,1,0:T(8,128)(2,1)}), bf16[64,16,1024]{2,1,0:T(8,128)(2,1)S(1)}, u32[]{:S(2)}, u32[]{:S(2)}) async-start(bf16[64,16,1024]{2,1,0:T(8,128)(2,1)} %add.3), calls=%async_computation.3 | async-start | bytes 4194304 | tf_op jit(solution)/shard_map/all_to_all | solution.py:410
